TPU v7x, 128 devices: a whole 4x4x4 slice. The times are simulated.
128 devices in a mesh: lat: 16 (over x, z), lon: 8 (over y, core).
Axes of the slice: x: 4, y: 4, z: 4, core: 2. Of those that a mesh axis runs over, the one named last changes fastest.
Arguments:
- control: float32 [16, 1024, 7200], P(None, 'lat', 'lon'), may hold values from -6 to 6
- inverse: float32 [32, 16, 32, 32], P('lat'), may hold values from -1 to 2
- coupling: float32 [16], replicated, may hold values from 0.2 to 1
- jacobian: float32 [16, 128], replicated, may hold values from -1.5 to 1.5
- error_weight: float32 [128], replicated, may hold values from 0.2 to 2
- response: float32 [512], replicated, may hold values from 1 to 10
- obs_values: float32 [262144, 128], P(('lat', 'lon')), may hold values from -6 to 6
- obs_tile: int32 [262144, 1], P(('lat', 'lon')), may hold values from 0 to 127; in each aligned block of 2048 rows (0 to 2047, 2048 to 4095, ...) at most 32 rows name the same one
- obs_points: int32 [262144, 4], P(('lat', 'lon')), may hold values from 0 to 57599
- obs_weights: float32 [262144, 4], P(('lat', 'lon')), may hold values from 0.1 to 1
- live_rows: int32 [128], P(('lat', 'lon')), may hold values from 1536 to 2048, as said below
Outputs:
- state: float32 [16, 1024, 7200], P(None, 'lat', 'lon')
- gradient: float32 [16, 1024, 7200], P(None, 'lat', 'lon')
- direction: float32 [16, 1024, 7200], P(None, 'lat', 'lon')
Inputs may be any that keep to these rules, and one draw needn't show every extreme that they name: `obs_tile`: no tile is named by more than 32 rows of one device's list; in every draw some device's list names some tile exactly 32 times. `obs_points`: cell index within the named tile, row-major over 64 latitudes and 900 longitudes. `live_rows`: some device has all 2048 rows live in every draw.
All inputs are finite; a program needn't handle non-finite values.
Results may differ from a plain program's by a relative error of at most 0.0001.
Values sent between devices are 32-bit elements; how exact they have to be, the bound alone decides.
No kernel may reach another device: no remote copies, remote signals or barrier semaphores. Data moves between devices by JAX's collectives and lax.ppermute only.
A program may use at most 192 MiB of HBM per device.

v0:
```python
import math

import jax
import jax.numpy as jnp
from jax import lax
from jax.sharding import PartitionSpec as P

CH = 16
KEEP = 512
BLOCK_LATITUDES = 32
STEPS = 2


MATMUL_ACCURACY = lax.Precision.HIGHEST


def extended(cells, sides, width):
    for axis, dim in sides:
        count = lax.axis_size(axis)
        ends = count - 1
        head = lax.slice_in_dim(cells, 0, width, axis=dim)
        tail = lax.slice_in_dim(cells, cells.shape[dim] - width, cells.shape[dim], axis=dim)
        cells = jnp.concatenate(
            [
                lax.ppermute(tail, axis, [(i, (i + 1) % count) for i in range(ends)]),
                cells,
                lax.ppermute(head, axis, [((i + 1) % count, i) for i in range(ends)]),
            ],
            axis=dim,
        )
    return cells


def band_edges(blocks):
    edge_rows = jnp.concatenate(
        [blocks[:, 0, 0:1], blocks[:, -1, BLOCK_LATITUDES - 1 : BLOCK_LATITUDES]], axis=1
    )
    padded = extended(edge_rows, (("lat", 1),), 1)
    firsts = blocks[:, :, 0]
    lasts = blocks[:, :, BLOCK_LATITUDES - 1]
    northern_row = jnp.concatenate([padded[:, 0:1], lasts[:, :-1]], axis=1)
    southern_row = jnp.concatenate([firsts[:, 1:], padded[:, 3:4]], axis=1)
    return (northern_row, southern_row)


def smooth_forward(field, inverse, coupling):
    channels, row_count, cols = field.shape
    blocks = field.reshape(channels, row_count // BLOCK_LATITUDES, BLOCK_LATITUDES, cols)
    northern_row, southern_row = band_edges(blocks)
    coupled_rows = coupling[:, None, None]
    mixed = jnp.einsum("bcij,cbjn->cbin", inverse, blocks, precision=MATMUL_ACCURACY)
    upper = jnp.einsum(
        "osj,som->sojm", inverse[:, :, :, 0], coupled_rows * northern_row, precision=MATMUL_ACCURACY
    )
    lower = jnp.einsum(
        "osj,som->sojm",
        inverse[:, :, :, BLOCK_LATITUDES - 1],
        coupled_rows * southern_row,
        precision=MATMUL_ACCURACY,
    )
    return (mixed + upper + lower).reshape(field.shape)


def smooth_adjoint(field, inverse, coupling):
    channels, row_count, cols = field.shape
    blocks = field.reshape(channels, row_count // BLOCK_LATITUDES, BLOCK_LATITUDES, cols)
    mixed = jnp.einsum("bcji,cbjn->cbin", inverse, blocks, precision=MATMUL_ACCURACY)
    northern_row, southern_row = band_edges(mixed)
    coupled_rows = coupling[:, None, None]
    row_index = jnp.arange(BLOCK_LATITUDES, dtype=jnp.int32)[None, None, :, None]
    first_mask = (row_index == 0).astype(jnp.float32)
    last_mask = (row_index == BLOCK_LATITUDES - 1).astype(jnp.float32)
    result = (
        mixed
        + first_mask * (coupled_rows * northern_row)[:, :, None, :]
        + last_mask * (coupled_rows * southern_row)[:, :, None, :]
    )
    return result.reshape(field.shape)


def circle_filter(circles, response):
    item_count, row_count, circle_length = circles.shape
    flat_rows = circles.reshape(item_count * row_count, circle_length)
    span_len = circle_length // 8
    wavenumber = jnp.arange(KEEP, dtype=jnp.int32)
    damping_factor = (
        jnp.where(wavenumber == 0, 1.0, 2.0).astype(jnp.float32) * response / circle_length
    )
    doubled = jnp.concatenate([damping_factor, damping_factor])

    def make_table(block_index):
        longitude = block_index * span_len + jnp.arange(span_len, dtype=jnp.int32)
        product = longitude[:, None] * wavenumber[None, :] % circle_length
        phase_arg = product.astype(jnp.float32) * (2.0 * math.pi / circle_length)
        return jnp.concatenate([jnp.cos(phase_arg), jnp.sin(phase_arg)], axis=1)

    def accumulate(running, block_index):
        segment = lax.dynamic_slice_in_dim(flat_rows, block_index * span_len, span_len, 1)
        return (
            running + jnp.dot(segment, make_table(block_index), precision=MATMUL_ACCURACY),
            None,
        )

    start_sum = jnp.zeros((flat_rows.shape[0], 2 * KEEP), jnp.float32)
    coeffs, unused_out = lax.scan(accumulate, start_sum, jnp.arange(8, dtype=jnp.int32))
    coeffs = coeffs * doubled

    def synthesize(output_rows, block_index):
        piece = jnp.dot(coeffs, make_table(block_index).T, precision=MATMUL_ACCURACY)
        zero_index = jnp.zeros((), jnp.int32)
        return (
            lax.dynamic_update_slice(output_rows, piece, (zero_index, block_index * span_len)),
            None,
        )

    output_rows, unused_pieces = lax.scan(
        synthesize, jnp.zeros_like(flat_rows), jnp.arange(8, dtype=jnp.int32)
    )
    return output_rows.reshape(circles.shape)


def body(
    control,
    inverse,
    coupling,
    jacobian,
    error_weight,
    response,
    obs_values,
    obs_tile,
    obs_points,
    obs_weights,
    live_rows,
):
    lat_count = lax.axis_size("lat")
    lon_count = lax.axis_size("lon")
    tile_count = lat_count * lon_count
    rows_dev = obs_values.shape[0]
    slot_count = 2 * rows_dev // tile_count
    total_slots = tile_count * slot_count
    live_mask = (jnp.arange(rows_dev, dtype=jnp.int32) < live_rows[0]).astype(jnp.float32)
    weights_live = obs_weights * live_mask[:, None]
    target = obs_tile[:, 0]
    sort_order = jnp.argsort(target, stable=True)
    sorted_target = target[sort_order]
    starts = jnp.sum(
        (target[None, :] < jnp.arange(tile_count, dtype=jnp.int32)[:, None]).astype(jnp.int32),
        axis=1,
    )
    rank_sorted = jnp.arange(rows_dev, dtype=jnp.int32) - starts[sorted_target]
    slot_rank = jnp.zeros((rows_dev,), jnp.int32).at[sort_order].set(rank_sorted)
    position = target * slot_count + slot_rank
    stencil = jnp.concatenate([obs_points.astype(jnp.float32), weights_live], axis=1)
    send_payload = (
        jnp.zeros((total_slots, obs_values.shape[1]), jnp.float32).at[position].set(obs_values)
    )
    send_stencil = jnp.zeros((total_slots, 8), jnp.float32).at[position].set(stencil)
    received = (
        lax.all_to_all(
            send_payload.reshape(tile_count, slot_count, -1),
            ("lat", "lon"),
            split_axis=0,
            concat_axis=0,
            tiled=True,
        ),
        lax.all_to_all(
            send_stencil.reshape(tile_count, slot_count, 8),
            ("lat", "lon"),
            split_axis=0,
            concat_axis=0,
            tiled=True,
        ),
    )
    recv_payload = received[0].reshape(total_slots, -1)
    recv_stencil = received[1].reshape(total_slots, 8).T
    recv_points = recv_stencil[:4].astype(jnp.int32)
    recv_weights = recv_stencil[4:]
    state = control
    for step_index in range(STEPS):
        state = smooth_forward(state, inverse, coupling)
    state_flat = state.reshape(CH, -1)
    gathered = state_flat[:, recv_points]
    interp = jnp.sum(recv_weights[None, :, :] * gathered, axis=1)
    model_obs = jnp.einsum("cs,cj->sj", interp, jacobian, precision=MATMUL_ACCURACY)
    weighted = (model_obs - recv_payload) * error_weight
    adjoint_cols = jnp.einsum("sj,cj->cs", weighted, jacobian, precision=MATMUL_ACCURACY)
    spread = recv_weights[None, :, :] * adjoint_cols[:, None, :]
    adjoint_flat = jnp.zeros_like(state_flat).at[:, recv_points].add(spread)
    adjoint = adjoint_flat.reshape(state.shape)
    for step_index in range(STEPS):
        adjoint = smooth_adjoint(adjoint, inverse, coupling)
    gradient = control + adjoint
    filtered = circle_filter(
        lax.all_to_all(gradient, "lon", split_axis=1, concat_axis=2, tiled=True), response
    )
    direction = lax.all_to_all(filtered, "lon", split_axis=2, concat_axis=1, tiled=True)
    return (state, gradient, direction)


def solution(mesh):
    return jax.shard_map(
        body,
        mesh=mesh,
        in_specs=(
            P(None, "lat", "lon"),
            P("lat", None, None, None),
            P(),
            P(),
            P(),
            P(),
            P(("lat", "lon"), None),
            P(("lat", "lon"), None),
            P(("lat", "lon"), None),
            P(("lat", "lon"), None),
            P(("lat", "lon")),
        ),
        out_specs=(P(None, "lat", "lon"), P(None, "lat", "lon"), P(None, "lat", "lon")),
        check_vma=False,
    )
```

profile of v0, /device:TPU:5, one launch (start us, length us, event | category | flops | bytes accessed | tf_op | source)
XLA Modules:
  0.0 879.5 jit_solution(2545102897848865806)
XLA Ops:
  10.4 5.7 sort.17
  16.2 11.8 %gather_fusion = s32[2048]{0:T(1024)S(1)} fusion(s32[2048]{0:T(1024)S(1)} %bitcast.131, s32[2048]{0:T(1024)S(1)} %get-tuple-element.202), kind=kCustom, calls=%fused_computation | custom fusion | bytes 24576 | tf_op jit(solution)/shard_map/gather | solution.py:145
  28.0 12.6 %gather_fusion.1 = s32[2048]{0:T(1024)S(1)} fusion(s32[128]{0:T(128)S(1)} %convert_reduce_fusion, s32[2048]{0:T(1024)S(1)} %broadcast_clamp_fusion.1), kind=kCustom, calls=%fused_computation.1 | custom fusion | bytes 24576 | tf_op jit(solution)/shard_map/gather | solution.py:150
  40.7 8.0 scatter_custom_fusion
  50.8 6.5 scatter_custom_fusion.1
  58.8 9.1 %all-to-all-start = ((f32[128,1,256]{2,1,0:T(1,128)}), f32[128,1,256]{2,1,0:T(1,128)S(1)}, u32[]{:S(2)}, u32[]{:S(2)}) async-start(f32[128,1,256]{2,1,0:T(1,128)} %reshape.227), calls=%async_computation | async-start | bytes 262144 | tf_op jit(solution)/shard_map/all_to_all | solution.py:166
  70.7 7.5 scatter_custom_fusion.2
  78.6 8.4 bitcast_add_fusion.1
  87.0 10.2 %all-to-all-start.1 = ((f32[128,32,128]{2,1,0:T(8,128)}), f32[128,32,128]{2,1,0:T(8,128)}, u32[]{:S(2)}, u32[]{:S(2)}) async-start(f32[128,32,128]{2,1,0:T(8,128)} %bitcast.24), calls=%async_computation.1 | async-start | bytes 4194304 | tf_op jit(solution)/shard_map/all_to_all | solution.py:159
  101.8 4.1 collective-permute-start.3
  108.0 17.2 %collective-permute-done.2 = f32[16,1,900]{2,1,0:T(1,128)S(1)} collective-permute-done((f32[16,1,900]{2,1,0:T(1,128)S(1)}, f32[16,1,900]{2,1,0:T(1,128)S(1)}, u32[]{:S(2)}, u32[]{:S(2)}) %collective-permute-start.2) | collective-permute-done | bytes 57632 | tf_op jit(solution)/shard_map/ppermute | solution.py:25
  125.4 8.4 multiply_add_fusion.2
  133.9 5.3 reshape_reshape.6
  139.2 15.0 %copy.203 = f32[16,57600]{0,1:T(8,128)} copy(f32[16,57600]{1,0:T(8,128)} %reshape_reshape.6) | data formatting | bytes 7372800 | tf_op jit(solution)/shard_map/reshape;reshape | solution.py:181
  156.3 63.7 %gather_fusion.2 = f32[16384,16]{1,0:T(8,128)} fusion(f32[16,57600]{0,1:T(8,128)} %copy.203, s32[16384]{0:T(1024)S(1)} %broadcast_clamp_fusion), kind=kCustom, calls=%fused_computation.2 | custom fusion | bytes 2162688 | tf_op jit(solution)/shard_map/gather | solution.py:182
  220.1 5.3 multiply_reduce_fusion
  231.4 5.3 broadcast_multiply_fusion
  236.8 101.0 %scatter_custom_fusion.3 = f32[16,57600]{0,1:T(8,128)} fusion(s32[16384]{0:T(1024)S(1)} %bitcast.158, f32[16384,16]{1,0:T(8,128)} %bitcast.143, f32[]{:T(128)} %constant.104.clone.1), kind=kCustom, calls=%fused_computation.45 | custom fusion | flops 262144 | bytes 3686912 | tf_op jit(solution)/shard_map/scatter-add | solution.py:188
  337.8 16.8 %copy.205 = f32[16,57600]{1,0:T(8,128)} copy(f32[16,57600]{0,1:T(8,128)} %scatter_custom_fusion.3) | data formatting | bytes 7372800 | tf_op jit(solution)/shard_map/scatter-add | solution.py:188
  354.7 6.4 reshape_reshape.7
  361.1 5.5 fusion.48
  373.2 4.4 collective-permute-start.4
  382.9 4.2 multiply_add_fusion.1
  387.1 5.2 fusion.41
  398.9 4.6 collective-permute-start.7
  405.1 4.2 multiply_add_fusion
  414.9 4.4 copy.213
  419.4 8.5 all-to-all-start.2
  427.9 48.8 %all-to-all-done.2 = f32[16,64,900]{2,0,1:T(8,128)} async-done(((f32[16,64,900]{2,0,1:T(8,128)}), f32[16,64,900]{2,0,1:T(8,128)}, u32[]{:S(2)}, u32[]{:S(2)}) %all-to-all-start.2) | async-done | bytes 3686432 | tf_op jit(solution)/shard_map/all_to_all | solution.py:194
  476.7 6.6 copy.265
  483.4 5.8 reshape.153
  489.2 113.6 %while.27 = (s32[]{:T(128)}, f32[128,1024]{1,0:T(8,128)S(1)}, s32[8]{0:T(128)S(1)}, f32[128,7200]{1,0:T(8,128)}, s32[]{:T(128)}, /*index=5*/s32[1]{0:T(128)}, s32[]{:T(128)}, s32[]{:T(128)}) while((s32[]{:T(128)}, f32[128,1024]{1,0:T(8,128)S(1)}, s32[8]{0:T(128)S(1)}, f32[128,7200]{1,0:T(8,128)}, s32[]{:T(128)}, ...), condition=%wide.region_8.9_spmd.clone, body=%wide.region_7.8_spmd.clone.sunk | while | flops 1420909440 | bytes 8961217 | solution.py:105
  490.4 8.8 %fusion.87 = (f32[900,512]{1,0:T(8,128)S(1)}, f32[900,512]{1,0:T(8,128)}) fusion(s32[900]{0:T(1024)S(1)} %iota_add_fusion.5), kind=kLoop, calls=%fused_computation.38.clone.1 | loop fusion | flops 4147200 | bytes 3690000 | tf_op jit(solution)/shard_map/while/body/eval_jaxpr/cos | solution.py:95
  499.2 4.1 fusion.88
  504.6 8.8 %fusion.87 = (f32[900,512]{1,0:T(8,128)S(1)}, f32[900,512]{1,0:T(8,128)}) fusion(s32[900]{0:T(1024)S(1)} %iota_add_fusion.5), kind=kLoop, calls=%fused_computation.38.clone.1 | loop fusion | flops 4147200 | bytes 3690000 | tf_op jit(solution)/shard_map/while/body/eval_jaxpr/cos | solution.py:95
  513.4 4.1 fusion.88
  518.8 8.8 %fusion.87 = (f32[900,512]{1,0:T(8,128)S(1)}, f32[900,512]{1,0:T(8,128)}) fusion(s32[900]{0:T(1024)S(1)} %iota_add_fusion.5), kind=kLoop, calls=%fused_computation.38.clone.1 | loop fusion | flops 4147200 | bytes 3690000 | tf_op jit(solution)/shard_map/while/body/eval_jaxpr/cos | solution.py:95
  527.6 4.1 fusion.88
  533.0 8.8 %fusion.87 = (f32[900,512]{1,0:T(8,128)S(1)}, f32[900,512]{1,0:T(8,128)}) fusion(s32[900]{0:T(1024)S(1)} %iota_add_fusion.5), kind=kLoop, calls=%fused_computation.38.clone.1 | loop fusion | flops 4147200 | bytes 3690000 | tf_op jit(solution)/shard_map/while/body/eval_jaxpr/cos | solution.py:95
  541.8 4.1 fusion.88
  547.2 8.8 %fusion.87 = (f32[900,512]{1,0:T(8,128)S(1)}, f32[900,512]{1,0:T(8,128)}) fusion(s32[900]{0:T(1024)S(1)} %iota_add_fusion.5), kind=kLoop, calls=%fused_computation.38.clone.1 | loop fusion | flops 4147200 | bytes 3690000 | tf_op jit(solution)/shard_map/while/body/eval_jaxpr/cos | solution.py:95
  556.0 4.1 fusion.88
  561.4 8.8 %fusion.87 = (f32[900,512]{1,0:T(8,128)S(1)}, f32[900,512]{1,0:T(8,128)}) fusion(s32[900]{0:T(1024)S(1)} %iota_add_fusion.5), kind=kLoop, calls=%fused_computation.38.clone.1 | loop fusion | flops 4147200 | bytes 3690000 | tf_op jit(solution)/shard_map/while/body/eval_jaxpr/cos | solution.py:95
  570.3 4.1 fusion.88
  575.6 8.8 %fusion.87 = (f32[900,512]{1,0:T(8,128)S(1)}, f32[900,512]{1,0:T(8,128)}) fusion(s32[900]{0:T(1024)S(1)} %iota_add_fusion.5), kind=kLoop, calls=%fused_computation.38.clone.1 | loop fusion | flops 4147200 | bytes 3690000 | tf_op jit(solution)/shard_map/while/body/eval_jaxpr/cos | solution.py:95
  584.5 4.1 fusion.88
  589.9 8.8 %fusion.87 = (f32[900,512]{1,0:T(8,128)S(1)}, f32[900,512]{1,0:T(8,128)}) fusion(s32[900]{0:T(1024)S(1)} %iota_add_fusion.5), kind=kLoop, calls=%fused_computation.38.clone.1 | loop fusion | flops 4147200 | bytes 3690000 | tf_op jit(solution)/shard_map/while/body/eval_jaxpr/cos | solution.py:95
  598.7 4.1 fusion.88
  604.9 109.7 %while.26 = (s32[]{:T(128)}, f32[128,7200]{0,1:T(8,128)}, s32[8]{0:T(128)S(1)}, f32[128,1024]{1,0:T(8,128)S(1)}, s32[]{:T(128)}, /*index=5*/s32[1]{0:T(128)}, s32[]{:T(128)}, s32[]{:T(128)}) while((s32[]{:T(128)}, f32[128,7200]{0,1:T(8,128)}, s32[8]{0:T(128)S(1)}, f32[128,1024]{1,0:T(8,128)S(1)}, s32[]{:T(128)}, ...), condition=%wide.region_10.11_spmd.clone, body=%wide.region_9.10_spmd.clone.sunk | while | flops 1420647296 | bytes 9286839 | solution.py:116
  606.3 7.5 fusion.83
  620.0 7.5 fusion.83
  633.7 7.5 fusion.83
  647.4 7.5 fusion.83
  661.1 7.5 fusion.83
  674.8 7.5 fusion.83
  688.5 7.5 fusion.83
  702.1 7.5 fusion.83
  714.5 5.3 copy.215
  719.8 15.5 %copy.216 = f32[16,8,7200]{0,1,2:T(8,128)} copy(f32[16,8,7200]{2,1,0:T(8,128)} %bitcast.141) | data formatting | bytes 7372800 | tf_op jit(solution)/shard_map/reshape | solution.py:119
  735.4 16.7 %reshape.229 = f32[8,1,115200]{2,1,0:T(1,128)} reshape(f32[7200,8,16]{2,1,0:T(8,128)} %bitcast.133) | data formatting | bytes 7372800
  752.1 49.7 %all_to_all.43 = f32[8,1,115200]{2,1,0:T(1,128)} all-to-all(f32[8,1,115200]{2,1,0:T(1,128)} %reshape.229), channel_id=1, replica_groups=mesh['lat'=16,'lon'=8] {'lon'}, dimensions={0} | all-to-all | bytes 7372800 | tf_op jit(solution)/shard_map/all_to_all | solution.py:196
  801.8 35.0 %reduce.3 = f32[8,115200]{1,0:T(8,128)} reduce(f32[8,1,115200]{2,1,0:T(1,128)} %all_to_all.43, f32[]{:T(128)} %broadcast.167), dimensions={1}, to_apply=%all_to_all.35.reduce_sub_computation | reduce | bytes 7372804 | tf_op jit(solution)/shard_map/all_to_all | solution.py:196
  836.9 21.5 %reshape.230 = f32[7200,8,16]{2,1,0:T(8,128)} reshape(f32[8,115200]{1,0:T(8,128)} %reduce.3) | data formatting | bytes 7372800
  858.4 20.7 %copy.218 = f32[16,8,8,900]{3,2,1,0:T(8,128)} copy(f32[16,8,8,900]{0,2,3,1:T(8,128)} %bitcast.134) | data formatting | bytes 7372800 | tf_op jit(solution)/shard_map/all_to_all | solution.py:196
  (152 shorter events, 106.7 us)
Async XLA Ops:
  0.6 224.8 %copy-start = (f32[16,128]{1,0:T(8,128)S(1)}, f32[16,128]{1,0:T(8,128)}, u32[]{:S(2)}) copy-start(f32[16,128]{1,0:T(8,128)} %param.18) | copy-start | bytes 24580
  0.6 15.5 %copy-start.2 = (s32[2048,1]{0,1:T(1,128)S(1)}, s32[2048,1]{0,1:T(1,128)}, u32[]{:S(2)}) copy-start(s32[2048,1]{0,1:T(1,128)} %param.22) | copy-start | bytes 24580
  2.0 76.3 %collective-permute-start = (f32[16,1,900]{2,1,0:T(1,128)S(1)}, f32[16,1,900]{2,1,0:T(1,128)S(1)}, u32[]{:S(2)}, u32[]{:S(2)}) collective-permute-start(f32[16,1,900]{2,1,0:T(1,128)S(1)} %get-tuple-element.196), channel_id=1, source_target_pairs={{0,8},{8,16},{16,24},{24,32},{32,40},{40,48},{48,56},{56,64},{64,7... | collective-permute-start | bytes 172808 | tf_op jit(solution)/shard_map/ppermute | solution.py:25
  5.5 72.8 %collective-permute-start.1 = (f32[16,1,900]{2,1,0:T(1,128)S(1)}, f32[16,1,900]{2,1,0:T(1,128)S(1)}, u32[]{:S(2)}, u32[]{:S(2)}) collective-permute-start(f32[16,1,900]{2,1,0:T(1,128)S(1)} %get-tuple-element.197), channel_id=1, source_target_pairs={{8,0},{16,8},{24,16},{32,24},{40,32},{48,40},{56,48},{64,56},{72,6... | collective-permute-start | bytes 172808 | tf_op jit(solution)/shard_map/ppermute | solution.py:27
  28.0 21.4 %copy-start.6 = (s32[2048,4]{0,1:T(4,128)S(1)}, s32[2048,4]{0,1:T(4,128)}, u32[]{:S(2)}) copy-start(s32[2048,4]{0,1:T(4,128)} %param.23) | copy-start | bytes 98308
  28.0 21.4 %copy-start.7 = (f32[2048,4]{0,1:T(4,128)S(1)}, f32[2048,4]{0,1:T(4,128)}, u32[]{:S(2)}) copy-start(f32[2048,4]{0,1:T(4,128)} %param.24) | copy-start | bytes 98308
  40.7 29.3 %copy-start.3 = (f32[2,16,32,32]{3,2,1,0:T(8,128)S(1)}, f32[2,16,32,32]{3,2,1,0:T(8,128)}, u32[]{:S(2)}) copy-start(f32[2,16,32,32]{3,2,1,0:T(8,128)} %param.16) | copy-start | bytes 393220
  57.9 20.4 %copy-start.8 = (f32[16]{0:T(128)S(1)}, f32[16]{0:T(128)}, u32[]{:S(2)}) copy-start(f32[16]{0:T(128)} %param.17) | copy-start | bytes 196
  58.8 28.2 %all-to-all-start = ((f32[128,1,256]{2,1,0:T(1,128)}), f32[128,1,256]{2,1,0:T(1,128)S(1)}, u32[]{:S(2)}, u32[]{:S(2)}) async-start(f32[128,1,256]{2,1,0:T(1,128)} %reshape.227), calls=%async_computation | async-start | bytes 262144 | tf_op jit(solution)/shard_map/all_to_all | solution.py:166
  87.0 138.4 %all-to-all-start.1 = ((f32[128,32,128]{2,1,0:T(8,128)}), f32[128,32,128]{2,1,0:T(8,128)}, u32[]{:S(2)}, u32[]{:S(2)}) async-start(f32[128,32,128]{2,1,0:T(8,128)} %bitcast.24), calls=%async_computation.1 | async-start | bytes 4194304 | tf_op jit(solution)/shard_map/all_to_all | solution.py:159
  98.6 26.6 %collective-permute-start.2 = (f32[16,1,900]{2,1,0:T(1,128)S(1)}, f32[16,1,900]{2,1,0:T(1,128)S(1)}, u32[]{:S(2)}, u32[]{:S(2)}) collective-permute-start(f32[16,1,900]{2,1,0:T(1,128)S(1)} %get-tuple-element.192), channel_id=1, source_target_pairs={{0,8},{8,16},{16,24},{24,32},{32,40},{40,48},{48,56},{56,64},{64,7... | collective-permute-start | bytes 172808 | tf_op jit(solution)/shard_map/ppermute | solution.py:25
  101.8 23.4 %collective-permute-start.3 = (f32[16,1,900]{2,1,0:T(1,128)S(1)}, f32[16,1,900]{2,1,0:T(1,128)S(1)}, u32[]{:S(2)}, u32[]{:S(2)}) collective-permute-start(f32[16,1,900]{2,1,0:T(1,128)S(1)} %get-tuple-element.193), channel_id=1, source_target_pairs={{8,0},{16,8},{24,16},{32,24},{40,32},{48,40},{56,48},{64,56},{72,6... | collective-permute-start | bytes 172808 | tf_op jit(solution)/shard_map/ppermute | solution.py:27
  220.1 5.4 copy-start.10
  373.2 7.8 collective-permute-start.4
  377.6 5.0 collective-permute-start.5
  396.1 7.6 collective-permute-start.6
  398.9 5.9 collective-permute-start.7
  409.3 2.2 copy-start.4
  412.9 2.0 copy-start.5
  419.3 8.6 copy-start.9
  419.4 57.4 %all-to-all-start.2 = ((f32[16,64,900]{2,0,1:T(8,128)}), f32[16,64,900]{2,0,1:T(8,128)}, u32[]{:S(2)}, u32[]{:S(2)}) async-start(f32[16,64,900]{2,0,1:T(8,128)} %copy.213), calls=%async_computation.2 | async-start | bytes 8388608 | tf_op jit(solution)/shard_map/all_to_all | solution.py:194
  858.4 20.7 %copy-start.1 = (f32[16,128]{1,0:T(8,128)S(1)}, f32[16,128]{1,0:T(8,128)}, u32[]{:S(2)}) copy-start(f32[16,128]{1,0:T(8,128)} %param.18) | copy-start | bytes 24580
where the time goes:
time: 892 us; the launch traced here: 879 us
  local copies, waits for them, and re-layouts  303 us (34%)
  other arithmetic  296 us (33%)
  matrix products  90.1 us (10%)
  waiting for transfers between devices  68.7 us (8%)
  starting transfers between devices  57.8 us (6%)
  blocking collectives  49.7 us (6%)
  loops' own time  11.1 us (1%)
    cos x16, other arithmetic, make_table(): return jnp.concatenate([jnp.cos(phase_arg), jnp.sin(phase_arg)], axis=1)  131 us
    scatter-add x1, other arithmetic, body(): adjoint_flat = jnp.zeros_like(state_flat).at[:, recv_points].add(spread)  101 us
    gather x1, local copies, waits for them, and re-layouts, body(): gathered = state_flat[:, recv_points]  63.7 us
    all_to_all x1, blocking collectives, body(): lax.all_to_all(filtered, 'lon', split_axis=2, concat_axis=1, tiled=True)  49.7 us
    all_to_all x1, waiting for transfers between devices, body(): lax.all_to_all(gradient, 'lon', split_axis=1, concat_axis=2, tiled=True)  48.8 us
    unnamed x31, local copies, waits for them, and re-layouts  42.9 us
    all_to_all x1, other arithmetic, body(): lax.all_to_all(filtered, 'lon', split_axis=2, concat_axis=1, tiled=True)  35 us
    dot_general x8, matrix products, accumulate(): jnp.dot(segment, make_table(block_index), precision=MATMUL_ACCURACY)  32.9 us
  transfers between devices with their start and end apart: 11, of which 4 were waited for; matrix products, arithmetic and copies ran while one was open for 19% of the time, Pallas kernels for 0%

commit v1 on v0

v1 whole, which is shorter than its diff:
```python
import functools

import jax
import jax.numpy as jnp
import numpy as np
from jax import lax
from jax.experimental import pallas as pl
from jax.experimental.pallas import tpu as pltpu
from jax.sharding import PartitionSpec as P

CH = 16
KEEP = 512
NLON = 7200
CLON = 900
RLAT = 64
HALF = 32
SLOTS = 32
TILES = 128
ROWS = 2048
LANES = 128
WORDS = LANES + SLOTS * 32
CELL_ROWS = 8 * 1024
ACCS = 4
F32 = jnp.float32
BF16 = jnp.bfloat16
EXACT = lax.Precision.HIGHEST
VMEM_BYTES = 60 * 1024 * 1024
VM = pl.BlockSpec(memory_space=pltpu.VMEM)
SM = pl.BlockSpec(memory_space=pltpu.SMEM)


def params():
    return pltpu.CompilerParams(vmem_limit_bytes=VMEM_BYTES)


def split(x):
    head = x.astype(BF16)
    return head, (x - head.astype(F32)).astype(BF16)


def mm(a, b):
    return jnp.dot(a, b, preferred_element_type=F32)


def mm_tn(a, b):
    return lax.dot_general(a, b, (((0,), (0,)), ((), ())), preferred_element_type=F32)


def dot3(a, b):
    a_head, a_tail = split(a)
    b_head, b_tail = split(b)
    rows = a.shape[0]
    both = mm(jnp.concatenate([a_head, a_tail], axis=0), b_head)
    return both[:rows] + both[rows:] + mm(a_head, b_tail)


def base_tables():
    longitude = np.arange(CLON)[:, None]
    wavenumber = np.arange(KEEP)[None, :]
    phase = 2.0 * np.pi * ((longitude * wavenumber) % NLON) / NLON
    table = np.concatenate([np.cos(phase), np.sin(phase)], axis=1).astype(np.float32)
    return table, np.ascontiguousarray(table.T)


def turn_tables():
    tile = np.arange(8)[:, None]
    wavenumber = np.arange(KEEP)[None, :]
    phase = 2.0 * np.pi * ((tile * wavenumber) % 8) / 8
    return np.stack([np.cos(phase), np.sin(phase)], axis=1).astype(np.float32)


def table_kernel(base_ref, across_ref, row_ref, col_ref, head_ref, tail_ref, head_t_ref, tail_t_ref):
    turn_cos = row_ref[0:1, :]
    turn_sin = row_ref[1:2, :]
    cos = base_ref[:, :KEEP]
    sin = base_ref[:, KEEP:]
    for part, value in ((0, cos * turn_cos - sin * turn_sin), (1, sin * turn_cos + cos * turn_sin)):
        head, tail = split(value)
        head_ref[:, part * KEEP : (part + 1) * KEEP] = head
        tail_ref[:, part * KEEP : (part + 1) * KEEP] = tail
    turn_cos = col_ref[:, 0:1]
    turn_sin = col_ref[:, 1:2]
    cos = across_ref[:KEEP, :]
    sin = across_ref[KEEP:, :]
    for part, value in ((0, cos * turn_cos - sin * turn_sin), (1, sin * turn_cos + cos * turn_sin)):
        head, tail = split(value)
        head_t_ref[part * KEEP : (part + 1) * KEEP, :] = head
        tail_t_ref[part * KEEP : (part + 1) * KEEP, :] = tail


def make_tables(lon):
    base, across = base_tables()
    turns = lax.dynamic_index_in_dim(jnp.asarray(turn_tables()), lon, 0, keepdims=False)
    return pl.pallas_call(
        table_kernel,
        out_shape=(
            jax.ShapeDtypeStruct((CLON, 2 * KEEP), BF16),
            jax.ShapeDtypeStruct((CLON, 2 * KEEP), BF16),
            jax.ShapeDtypeStruct((2 * KEEP, CLON), BF16),
            jax.ShapeDtypeStruct((2 * KEEP, CLON), BF16),
        ),
        in_specs=[VM] * 4,
        out_specs=[VM] * 4,
        compiler_params=params(),
        name="tables",
    )(jnp.asarray(base), jnp.asarray(across), turns, turns.T)


def band_matrices(inverse, coupling):
    zero = jnp.zeros((CH, HALF, HALF), F32)
    blocks = jnp.concatenate(
        [jnp.concatenate([inverse[0], zero], axis=2), jnp.concatenate([zero, inverse[1]], axis=2)], axis=1
    )
    c = coupling[:, None, None]
    column = jnp.arange(RLAT)[None, None, :]
    step = blocks + c * (
        jnp.where(column == HALF, blocks[:, :, HALF - 1 : HALF], 0.0)
        + jnp.where(column == HALF - 1, blocks[:, :, HALF : HALF + 1], 0.0)
    )
    first, last = blocks[:, :, 0:1], blocks[:, :, RLAT - 1 : RLAT]
    products = jnp.einsum(
        "cij,cjk->cik", step, jnp.concatenate([step, first, last], axis=2), precision=EXACT
    )
    twice, step_first, step_last = products[:, :, :RLAT], products[:, :, RLAT : RLAT + 1], products[:, :, RLAT + 1 :]
    pad = jnp.zeros((CH, RLAT, 6), F32)
    forward = jnp.concatenate([twice, c * step_first, c * first, pad, c * step_last, c * last, pad], axis=2)
    backward = jnp.concatenate([twice, first, step_first, pad, last, step_last, pad], axis=2)
    row = jnp.arange(RLAT)[None, :, None]
    first_unit = jnp.broadcast_to((row == 0).astype(F32), (CH, RLAT, 1))
    last_unit = jnp.broadcast_to((row == RLAT - 1).astype(F32), (CH, RLAT, 1))
    top_row = jnp.swapaxes(step[:, 0:1, :], 1, 2)
    bottom_row = jnp.swapaxes(step[:, RLAT - 1 :, :], 1, 2)
    edges = jnp.concatenate([first_unit, top_row, pad, last_unit, bottom_row, pad], axis=2)
    mend = jnp.concatenate([c * top_row, c * first_unit, pad, c * bottom_row, c * last_unit, pad], axis=2)
    alpha = jnp.concatenate([c * blocks[:, 0:1, 0:1], c * blocks[:, RLAT - 1 :, RLAT - 1 :]], axis=2)
    place = jnp.arange(16)[None, :, None]
    alpha_rows = jnp.where(place == 2, alpha[:, :, 0:1], 0.0) + jnp.where(place == 10, alpha[:, :, 1:2], 0.0)
    return forward, backward, jnp.swapaxes(edges, 1, 2), mend, alpha_rows


def edges_kernel(field_ref, edges_ref, alpha_ref, north_ref, south_ref):
    for channel in range(CH):
        rows = dot3(edges_ref[channel], field_ref[channel]) + alpha_ref[channel]
        north_ref[channel] = rows[:8]
        south_ref[channel] = rows[8:]


def send_edges(north, south):
    count = lax.axis_size("lat")
    from_south = lax.ppermute(north, "lat", [(i + 1, i) for i in range(count - 1)])
    from_north = lax.ppermute(south, "lat", [(i, i + 1) for i in range(count - 1)])
    return from_north, from_south


def forward_kernel(field_ref, north_ref, south_ref, matrix_ref, state_ref, cells_ref):
    column = lax.broadcasted_iota(jnp.int32, (RLAT, 80), 1)
    for channel in range(CH):
        matrix = matrix_ref[channel]
        alpha_north = north_ref[channel, 2:3, 0:1]
        alpha_south = south_ref[channel, 2:3, 0:1]
        matrix = (
            matrix
            + jnp.where(column == 0, matrix[:, 65:66] * alpha_north, 0.0)
            + jnp.where(column == RLAT - 1, matrix[:, 73:74] * alpha_south, 0.0)
        )
        field = jnp.concatenate([field_ref[channel], north_ref[channel], south_ref[channel]], axis=0)
        state_ref[channel] = dot3(matrix, field)
    for group in range(8):
        for lane_tile in range(2):
            lanes = slice(lane_tile * LANES, (lane_tile + 1) * LANES)
            piece = state_ref[:, group * 8 : (group + 1) * 8, lanes].reshape(LANES, LANES)
            cells_ref[group, lanes, :] = piece.T


def forward_diffusion(control, from_north, from_south, forward):
    width = 256
    return pl.pallas_call(
        forward_kernel,
        grid=(4,),
        out_shape=(
            jax.ShapeDtypeStruct((CH, RLAT, CLON), F32),
            jax.ShapeDtypeStruct((8, 1024, LANES), F32),
        ),
        in_specs=[
            pl.BlockSpec((CH, RLAT, width), lambda i: (0, 0, i)),
            pl.BlockSpec((CH, 8, width), lambda i: (0, 0, i)),
            pl.BlockSpec((CH, 8, width), lambda i: (0, 0, i)),
            pl.BlockSpec((CH, RLAT, 80), lambda i: (0, 0, 0)),
        ],
        out_specs=(
            pl.BlockSpec((CH, RLAT, width), lambda i: (0, 0, i)),
            pl.BlockSpec((8, width, LANES), lambda i: (0, i, 0)),
        ),
        compiler_params=params(),
        name="forward",
    )(control, from_north, from_south, forward)


def route_kernel(live_ref, values_ref, tile_ref, tile_row_ref, points_ref, weights_ref, project_ref, out_ref, rank_ref):
    live = live_ref[0]
    lane = lax.broadcasted_iota(jnp.int32, (1, LANES), 1)
    block = 256
    below = (
        lax.broadcasted_iota(jnp.int32, (block, block), 1) < lax.broadcasted_iota(jnp.int32, (block, block), 0)
    ).astype(F32).astype(BF16)
    base = jnp.zeros((1, LANES), F32)
    for part in range(ROWS // block):
        rows = slice(part * block, (part + 1) * block)
        index = part * block + lax.broadcasted_iota(jnp.int32, (block, 1), 0)
        named = ((tile_ref[rows, :] == lane) & (index < live)).astype(F32)
        before = mm(below, named.astype(BF16)) + base
        rank_ref[rows, :] = jnp.sum(named * before, axis=1, keepdims=True).astype(jnp.int32)
        base = base + jnp.sum(named, axis=0, keepdims=True)
    target = lax.broadcasted_iota(jnp.int32, (TILES, 1), 0)
    order = lax.broadcasted_iota(jnp.int32, (1, ROWS), 1)
    chosen = ((tile_row_ref[...] == target) & (order < live)).astype(F32).astype(BF16)
    group = lane // 32
    inner = lane % 32
    points = points_ref[...]
    latitude = points // CLON
    longitude = points - latitude * CLON
    cell_row = ((latitude // 8) * 1024 + longitude).astype(F32)
    level = (latitude % 8).astype(F32)
    weights = weights_ref[...]
    features = dot3(values_ref[...], project_ref[...])
    cell_rows = jnp.zeros((ROWS, LANES), F32)
    for point in range(4):
        features = jnp.where(inner == point, weights[:, point : point + 1], features)
        features = jnp.where(inner == 4 + point, level[:, point : point + 1], features)
        cell_rows = jnp.where(group == point, cell_row[:, point : point + 1], cell_rows)
    rank = jnp.broadcast_to(rank_ref[...], (ROWS, LANES))

    def deliver(masked):
        head, tail = split(masked)
        return mm(chosen, head) + mm(chosen, tail)

    out_ref[:, :LANES] = deliver(jnp.where(rank == inner, cell_rows, 0.0))
    for tile in range(8):
        lanes = slice((tile + 1) * LANES, (tile + 2) * LANES)
        out_ref[:, lanes] = deliver(jnp.where(rank == tile * 4 + group, features, 0.0))


def route(live_rows, obs_values, obs_tile, obs_points, obs_weights, jacobian, error_weight):
    project = jnp.pad((jacobian * error_weight).T, ((0, 0), (8, 8)))
    project = jnp.concatenate([project] * 4, axis=1)
    return pl.pallas_call(
        route_kernel,
        out_shape=jax.ShapeDtypeStruct((TILES, WORDS), F32),
        in_specs=[SM] + [VM] * 6,
        out_specs=VM,
        scratch_shapes=[pltpu.VMEM((ROWS, 1), jnp.int32)],
        compiler_params=params(),
        name="route",
    )(live_rows, obs_values, obs_tile, obs_tile.reshape(1, ROWS), obs_points, obs_weights, project)


def pick_table():
    pick = np.zeros((LANES, 4 * LANES), np.float32)
    for slot in range(4):
        for channel in range(CH):
            first = slot * LANES + channel * 8
            pick[slot * 32 + 8 + channel, first : first + 8] = -1.0
    return np.concatenate([pick, pick], axis=0)


def observe_kernel(
    rows_ref,
    cells_ref,
    gram_ref,
    pick_ref,
    control_ref,
    north_ref,
    south_ref,
    matrix_ref,
    coupling_ref,
    local_ref,
    to_north_ref,
    to_south_ref,
    index_ref,
    where_ref,
    mask_ref,
    columns_ref,
    values_ref,
    field_ref,
    index_semaphore,
    control_semaphore,
    *sums,
):
    index_ref[...] = rows_ref[:, :LANES].astype(jnp.int32)
    copy = pltpu.make_async_copy(index_ref, where_ref, index_semaphore)
    copy.start()
    control_copy = pltpu.make_async_copy(control_ref, local_ref, control_semaphore)
    control_copy.start()
    zero_rows = 256

    def clear(step, carry):
        for total in sums:
            total[pl.ds(pl.multiple_of(step * zero_rows, zero_rows), zero_rows), :] = jnp.zeros((zero_rows, LANES), F32)
        return carry

    lax.fori_loop(0, CELL_ROWS // zero_rows, clear, 0)
    lane_level = (lax.broadcasted_iota(jnp.int32, (1, LANES), 1) % 8).astype(F32)
    gram_head, gram_tail = split(gram_ref[...])
    gram_both = jnp.concatenate([gram_head, gram_tail], axis=0)

    def prepare(tile, carry):
        data = rows_ref[:, pl.ds(pl.multiple_of((tile + 1) * LANES, LANES), LANES)]
        values = mm(jnp.concatenate(split(data), axis=1), pick_ref[...])
        for slot in range(4):
            values_ref[tile * 4 + slot] = values[:, slot * LANES : (slot + 1) * LANES]
            for point in range(4):
                weight = data[:, slot * 32 + point : slot * 32 + point + 1]
                level = data[:, slot * 32 + 4 + point : slot * 32 + 5 + point]
                mask_ref[point, tile * 4 + slot] = jnp.where(level == lane_level, weight, 0.0)
        return carry

    lax.fori_loop(0, 8, prepare, 0)
    copy.wait()
    chunk = 16

    def move(fetch, store):
        def source(step, carry):
            for slot in range(SLOTS):
                if fetch is not None:
                    taken = fetch * chunk + step
                    interp = None
                    for point in range(4):
                        cell = where_ref[taken, point * 32 + slot]
                        term = cells_ref[pl.ds(cell, 1), :] * mask_ref[point, slot, pl.ds(taken, 1), :]
                        interp = term if interp is None else interp + term
                if store is not None:
                    given = store * chunk + step
                    column = columns_ref[slot, pl.ds(given, 1), :]
                    cells = [where_ref[given, point * 32 + slot] for point in range(4)]
                    fresh = [
                        sums[point][pl.ds(cells[point], 1), :] + mask_ref[point, slot, pl.ds(given, 1), :] * column
                        for point in range(4)
                    ]
                    for point in range(4):
                        sums[point][pl.ds(cells[point], 1), :] = fresh[point]
                if fetch is not None:
                    columns_ref[slot, pl.ds(taken, 1), :] = interp
            return carry

        lax.fori_loop(0, chunk, source, 0)

    def weigh(index):
        rows = pl.ds(pl.multiple_of(index * chunk, chunk), chunk)
        interp = columns_ref[:, rows, :].reshape(SLOTS * chunk, LANES)
        head, tail = split(interp)
        columns = mm(head, gram_head) + mm(jnp.concatenate([tail, head], axis=1), gram_both)
        columns_ref[:, rows, :] = columns.reshape(SLOTS, chunk, LANES) + values_ref[:, rows, :]

    move(0, None)
    weigh(0)

    def rounds(index, carry):
        move(index, index - 1)
        weigh(index)
        return carry

    last = TILES // chunk - 1
    lax.fori_loop(1, last + 1, rounds, 0)
    move(None, last)

    def turn(tile, carry):
        first = pl.multiple_of(tile * LANES, LANES)
        for group in range(8):
            piece = sums[0][pl.ds(group * 1024 + first, LANES), :]
            for total in sums[1:]:
                piece = piece + total[pl.ds(group * 1024 + first, LANES), :]
            field_ref[:, group * 8 : (group + 1) * 8, pl.ds(first, LANES)] = piece.T.reshape(CH, 8, LANES)
        return carry

    lax.fori_loop(0, 8, turn, 0)
    control_copy.wait()

    column = lax.broadcasted_iota(jnp.int32, (RLAT, 80), 1)
    for channel in range(CH):
        matrix = matrix_ref[channel]
        coupling = coupling_ref[channel]
        alpha_north = north_ref[channel, 2:3, 0:1] * coupling
        alpha_south = south_ref[channel, 2:3, 0:1] * coupling
        matrix = (
            matrix
            + jnp.where(column == 0, matrix[:, 64:65] * alpha_north, 0.0)
            + jnp.where(column == RLAT - 1, matrix[:, 72:73] * alpha_south, 0.0)
        )
        matrix_head, matrix_tail = split(matrix.T)
        head, tail = split(field_ref[channel])
        both = mm(jnp.concatenate([matrix_head, matrix_tail], axis=0), head)
        result = both[:80] + both[80:] + mm(matrix_head, tail)
        local_ref[channel] = local_ref[channel] + result[:RLAT, :CLON]
        to_north_ref[channel] = result[RLAT : RLAT + 8, :CLON]
        to_south_ref[channel] = result[RLAT + 8 :, :CLON]


def observe(rows, cells, gram, control, from_north, from_south, backward, coupling):
    edge = jax.ShapeDtypeStruct((CH, 8, CLON), F32)
    return pl.pallas_call(
        observe_kernel,
        out_shape=(jax.ShapeDtypeStruct((CH, RLAT, CLON), F32), edge, edge),
        in_specs=[VM] * 4 + [pl.BlockSpec(memory_space=pl.ANY)] + [VM] * 3 + [SM],
        out_specs=(VM, VM, VM),
        scratch_shapes=[
            pltpu.VMEM((TILES, LANES), jnp.int32),
            pltpu.SMEM((TILES, LANES), jnp.int32),
            pltpu.VMEM((4, SLOTS, TILES, LANES), F32),
            pltpu.VMEM((SLOTS, TILES, LANES), F32),
            pltpu.VMEM((SLOTS, TILES, LANES), F32),
            pltpu.VMEM((CH, RLAT, 1024), F32),
            pltpu.SemaphoreType.DMA,
            pltpu.SemaphoreType.DMA,
        ]
        + [pltpu.VMEM((CELL_ROWS, LANES), F32)] * ACCS,
        compiler_params=params(),
        name="observe",
    )(rows, cells, gram, jnp.asarray(pick_table(), BF16), control, from_north, from_south, backward, coupling)


def spectra_kernel(order_ref, local_ref, north_ref, south_ref, mend_ref, head_ref, tail_ref, gradient_ref, other_ref, mine_ref):
    for part, out_ref in ((0, other_ref), (1, mine_ref)):
        for half in range(2):
            pieces = []
            for place in (2 * half, 2 * half + 1):
                pair = order_ref[part * 4 + place]
                for inner in range(2):
                    channel = pair * 2 + inner
                    edges = jnp.concatenate([north_ref[channel], south_ref[channel]], axis=0)
                    piece = local_ref[channel] + dot3(mend_ref[channel], edges)
                    gradient_ref[channel] = piece
                    pieces.append(piece)
            head, tail = split(jnp.concatenate(pieces, axis=0))
            rows = 256
            both = mm(jnp.concatenate([head, tail], axis=0), head_ref[...])
            result = both[:rows] + both[rows:] + mm(head, tail_ref[...])
            out_ref[2 * half] = result[:128]
            out_ref[2 * half + 1] = result[128:]


def spectra(order, local, from_north, from_south, mend, head, tail):
    block = jax.ShapeDtypeStruct((4, 128, 2 * KEEP), F32)
    return pl.pallas_call(
        spectra_kernel,
        out_shape=(jax.ShapeDtypeStruct((CH, RLAT, CLON), F32), block, block),
        in_specs=[SM] + [VM] * 6,
        out_specs=(VM, VM, VM),
        compiler_params=params(),
        name="spectra",
    )(order, local, from_north, from_south, mend, head, tail)


def synthesis_kernel(order_ref, head_ref, tail_ref, *refs):
    pieces, out_ref = refs[:-1], refs[-1]
    for half in range(len(pieces) // 2):
        head, tail = split(jnp.concatenate([pieces[2 * half][...], pieces[2 * half + 1][...]], axis=0))
        both = mm(jnp.concatenate([head, tail], axis=0), head_ref[...])
        result = both[:256] + both[256:] + mm(head, tail_ref[...])
        for place in range(2):
            pair = order_ref[2 * half + place]
            for inner in range(2):
                first = place * 128 + inner * RLAT
                out_ref[pair * 2 + inner] = result[first : first + RLAT]


def synthesis(order, head, tail, pieces):
    return pl.pallas_call(
        synthesis_kernel,
        out_shape=jax.ShapeDtypeStruct((CH, RLAT, CLON), F32),
        in_specs=[SM] + [VM] * (2 + len(pieces)),
        out_specs=VM,
        compiler_params=params(),
        name="synthesis",
    )(order, head, tail, *pieces)


def body(
    control,
    inverse,
    coupling,
    jacobian,
    error_weight,
    response,
    obs_values,
    obs_tile,
    obs_points,
    obs_weights,
    live_rows,
):
    lon = lax.axis_index("lon")
    ring, core = lon // 2, lon % 2
    partner = [(i, i ^ 1) for i in range(8)]
    onward = [(i, (i + 2) % 8) for i in range(8)]
    back = [(i, (i - 2) % 8) for i in range(8)]

    forward, backward, edges, mend, alpha = band_matrices(inverse, coupling)
    edge = jax.ShapeDtypeStruct((CH, 8, CLON), F32)
    north, south = pl.pallas_call(
        edges_kernel,
        out_shape=(edge, edge),
        in_specs=[VM] * 3,
        out_specs=(VM, VM),
        compiler_params=params(),
        name="edges",
    )(control, edges, alpha)
    from_north, from_south = send_edges(north, south)

    routed = route(live_rows, obs_values, obs_tile, obs_points, obs_weights, jacobian, error_weight)
    rows = lax.all_to_all(routed, ("lat", "lon"), split_axis=0, concat_axis=0, tiled=True)

    state, cells = forward_diffusion(control, from_north, from_south, forward)
    gram = jnp.dot(jacobian * error_weight, jacobian.T, precision=EXACT)
    gram = jnp.repeat(jnp.repeat(gram, 8, axis=0), 8, axis=1)
    local, north, south = observe(
        rows, cells.reshape(CELL_ROWS, LANES), gram, control, from_north, from_south, backward, coupling
    )
    edge_north, edge_south = send_edges(north, south)
    lon_after, north = lax.optimization_barrier((lon, north))
    head, tail, head_t, tail_t = make_tables(lon_after)

    offsets = jnp.array([2, 1, 3, 0], jnp.int32)
    chips = (ring + offsets) % 4
    order = jnp.concatenate([chips * 2 + (1 - core), chips * 2 + core]).astype(jnp.int32)
    gradient, other, mine = spectra(order, local, edge_north, edge_south, mend, head, tail)
    pairs = mine + lax.ppermute(other, "lon", partner)
    far, near, prior, own = pairs[0], pairs[1], pairs[2], pairs[3]
    far_next = lax.ppermute(far[:64], "lon", onward)
    far_prior = lax.ppermute(far[64:], "lon", back)
    from_prior = lax.ppermute(jnp.concatenate([near[:64] + far_next, near[64:]]), "lon", onward)
    from_next = lax.ppermute(jnp.concatenate([prior[:64], prior[64:] + far_prior]), "lon", back)
    wavenumber = jnp.arange(KEEP, dtype=jnp.int32)
    factor = jnp.where(wavenumber == 0, 1.0, 2.0).astype(F32) * response / NLON
    spectrum = (own + from_prior + from_next) * jnp.concatenate([factor, factor])

    from_prior = lax.ppermute(spectrum, "lon", onward)
    from_next = lax.ppermute(spectrum, "lon", back)
    far_a = lax.ppermute(from_prior[:64], "lon", onward)
    far_b = lax.ppermute(from_next[64:], "lon", back)
    across = jnp.concatenate([far_a, far_b])
    pieces = [across, from_next, from_prior, spectrum]
    swapped = [lax.ppermute(piece, "lon", partner) for piece in pieces]
    direction = synthesis(order, head_t, tail_t, swapped + pieces)
    return (state, gradient, direction)


def solution(mesh):
    return jax.shard_map(
        body,
        mesh=mesh,
        in_specs=(
            P(None, "lat", "lon"),
            P("lat", None, None, None),
            P(),
            P(),
            P(),
            P(),
            P(("lat", "lon"), None),
            P(("lat", "lon"), None),
            P(("lat", "lon"), None),
            P(("lat", "lon"), None),
            P(("lat", "lon")),
        ),
        out_specs=(P(None, "lat", "lon"), P(None, "lat", "lon"), P(None, "lat", "lon")),
        check_vma=False,
    )
```

time: 892 us -> 240 us (0.27)
  other arithmetic: 296 us -> 10.3 us
  local copies, waits for them, and re-layouts: 303 us -> 24.8 us
  Pallas kernels: 0 us -> 118 us
  matrix products: 90.1 us -> 1.15 us
  blocking collectives: 49.7 us -> 0 us
  waiting for transfers between devices: 68.7 us -> 33.6 us
  starting transfers between devices: 57.8 us -> 46.5 us
  loops' own time: 11.1 us -> 0 us
    cos x16 -> x0, other arithmetic: 131 us -> none  [make_table(): return jnp.concatenate([jnp.cos(phase_arg), jnp.sin(phase_arg)], axis=1)]
    pallas_call x0 -> x7, Pallas kernels: none -> 118 us  [the longest x1 56.1 us: observe(): pl.pallas_call(observe_kernel, out_shape=(jax.ShapeDtypeStruct((CH, RLAT,...]
    scatter-add x1 -> x0, other arithmetic: 101 us -> none  [body(): adjoint_flat = jnp.zeros_like(state_flat).at[:, recv_points].add(spread)]
    dot_general x22 -> x2, matrix products: 90.1 us -> 1.15 us  [the longest x1 0.88 us: band_matrices(): jnp.einsum('cij,cjk->cik', step, jnp.concatenate([step, first, last], axi...]
    gather x3 -> x0, local copies, waits for them, and re-layouts: 88.1 us -> none  [the longest x1 63.7 us: body(): gathered = state_flat[:, recv_points]]
    all_to_all x1 -> x0, blocking collectives: 49.7 us -> none  [body(): lax.all_to_all(filtered, 'lon', split_axis=2, concat_axis=1, tiled=True)]
    all_to_all x3 -> x1, waiting for transfers between devices: 48.8 us -> 0.01 us  [body(): lax.all_to_all(routed, ('lat', 'lon'), split_axis=0, concat_axis=0, tiled...]
    unnamed x31 -> x48, local copies, waits for them, and re-layouts: 42.9 us -> 6.85 us
  transfers between devices with their start and end apart: 11 -> 18, of which waited for: 4 -> 6; matrix products, arithmetic and copies ran while one was open for 19% -> 11% of each run, Pallas kernels for 0% -> 14%
where the time goes in v1:
time: 240 us; the launch traced here: 236 us
  Pallas kernels  118 us (49%)
  starting transfers between devices  46.5 us (19%)
  waiting for transfers between devices  33.6 us (14%)
  local copies, waits for them, and re-layouts  24.8 us (10%)
  other arithmetic  10.3 us (4%)
    pallas_call x1, Pallas kernels, observe(): pl.pallas_call(observe_kernel, out_shape=(jax.ShapeDtypeStruct((CH, RLAT,...  56.1 us
    pallas_call x1, Pallas kernels, spectra(): pl.pallas_call(spectra_kernel, out_shape=(jax.ShapeDtypeStruct((CH, RLAT,...  13.6 us
    pallas_call x1, Pallas kernels, route(): pl.pallas_call(route_kernel, out_shape=jax.ShapeDtypeStruct((TILES, WORDS...  13.2 us
    pallas_call x1, Pallas kernels, synthesis(): pl.pallas_call(synthesis_kernel, out_shape=jax.ShapeDtypeStruct((CH, RLAT...  12.1 us
    pallas_call x1, Pallas kernels, forward_diffusion(): pl.pallas_call(forward_kernel, grid=(4,), out_shape=(jax.ShapeDtypeStruct...  10.5 us
    all_to_all x1, starting transfers between devices, body(): lax.all_to_all(routed, ('lat', 'lon'), split_axis=0, concat_axis=0, tiled...  9.94 us
    ppermute x1, waiting for transfers between devices, body(): lax.ppermute(jnp.concatenate([prior[:64], prior[64:] + far_prior]), 'lon'...  9.71 us
    ppermute x1, waiting for transfers between devices, body(): from_prior = lax.ppermute(spectrum, 'lon', onward)  9.22 us
  transfers between devices with their start and end apart: 18, of which 6 were waited for; matrix products, arithmetic and copies ran while one was open for 11% of the time, Pallas kernels for 14%

profile of v1, /device:TPU:5, one launch (start us, length us, event | category | flops | bytes accessed | tf_op | source)
XLA Modules:
  0.0 236.4 jit_solution(14820140957194948073)
XLA Ops:
  0.7 1.1 slice_bitcast_fusion.8
  1.7 0.1 select_maximum_fusion
  1.9 1.5 broadcast_multiply_fusion.4
  3.4 0.4 multiply_add_fusion
  3.8 0.1 copy.114
  3.9 0.3 fusion.14
  4.2 0.8 select_add_fusion.alpha_ref
  5.0 1.3 concatenate.45
  6.3 4.1 %edges.1 = (f32[16,8,900]{2,1,0:T(8,128)}, f32[16,8,900]{2,1,0:T(8,128)}) custom-call(f32[16,64,900]{2,1,0:T(8,128)} %control_ref.1, f32[16,16,64]{2,1,0:T(8,128)} %bitcast.65, f32[16,16,1]{2,1,0:T(8,128)} %select_add_fusion.alpha_ref), custom_call_target="tpu_custom_call" | custom-call | tf_op jit(solution)/shard_map/edges/pallas_call | solution.py:498
  10.4 3.7 %collective-permute-start = (f32[16,8,900]{2,1,0:T(8,128)}, f32[16,8,900]{2,1,0:T(8,128)}, u32[]{:S(2)}, u32[]{:S(2)}) collective-permute-start(f32[16,8,900]{2,1,0:T(8,128)} %get-tuple-element.18), channel_id=1, source_target_pairs={{0,8},{8,16},{16,24},{24,32},{32,40},{40,48},{48,56},{56,64},{64,7... | collective-permute-start | bytes 1382408 | tf_op jit(solution)/shard_map/ppermute | solution.py:151
  14.1 4.5 %collective-permute-start.1 = (f32[16,8,900]{2,1,0:T(8,128)}, f32[16,8,900]{2,1,0:T(8,128)}, u32[]{:S(2)}, u32[]{:S(2)}) collective-permute-start(f32[16,8,900]{2,1,0:T(8,128)} %get-tuple-element.19), channel_id=1, source_target_pairs={{8,0},{16,8},{24,16},{32,24},{40,32},{48,40},{56,48},{64,56},{72,6... | collective-permute-start | bytes 1382408 | tf_op jit(solution)/shard_map/ppermute | solution.py:150
  19.3 1.3 copy.117.tile_ref
  20.6 1.3 copy.118.points_ref
  22.0 1.3 copy.119.weights_ref
  23.3 0.1 copy.116
  23.4 0.1 multiply_bitcast_fusion
  23.5 0.1 pad.6
  23.6 0.8 pad_maximum_fusion.2.project_ref
  24.4 13.2 %route.1 = f32[128,1152]{1,0:T(8,128)} custom-call(s32[1]{0:T(128)S(6)} %copy.135.live_ref, f32[2048,128]{1,0:T(8,128)} %values_ref.1, s32[2048,1]{1,0:T(8,128)} %copy.117.tile_ref, s32[1,2048]{1,0:T(1,128)} %bitcast.66, s32[2048,4]{1,0:T(8,128)} %copy.118.points_ref, f32[2048,4]{1,0:T(8,128)} %copy.119.weights_ref, f32[128,128]{1,0:T(8,128)} %pad_maximum_fusion.2.project_ref), custom_call_target="tpu_custom_call" | custom-call | tf_op jit(solution)/shard_map/route/pallas_call | solution.py:246
  37.6 2.5 %copy.120 = f32[128,1,1152]{2,1,0:T(1,128)} copy(f32[128,1,1152]{2,0,1:T(8,128)} %bitcast.63) | data formatting | bytes 1179648 | tf_op jit(solution)/shard_map/all_to_all | solution.py:509
  40.1 9.9 %all-to-all-start = ((f32[128,1,1152]{2,1,0:T(1,128)}), f32[128,1,1152]{2,1,0:T(1,128)S(1)}, u32[]{:S(2)}, u32[]{:S(2)}) async-start(f32[128,1,1152]{2,1,0:T(1,128)} %copy.120), calls=%async_computation | async-start | bytes 1179648 | tf_op jit(solution)/shard_map/all_to_all | solution.py:509
  50.0 0.3 fusion.11
  50.3 0.3 copy.125
  50.6 1.0 copy.123
  51.7 0.7 copy.122.gram_ref
  52.5 0.9 fusion.3
  53.4 3.5 %broadcast_multiply_fusion.5 = (f32[16,64,1]{2,1,0:T(8,128)}, f32[16,64,1]{2,1,0:T(8,128)}, f32[16,64,1]{2,1,0:T(8,128)}, f32[16,64,1]{2,1,0:T(8,128)}, f32[16,6...) fusion(f32[16]{0:T(128)S(1)} %copy-done.17, f32[16,64,66]{2,1,0:T(8,128)S(1)} %fusion.3, ...), kind=kLoop, calls=%fused_computation.34 | loop fusion | flops 6144 | bytes 49728 | tf_op jit(solution)/shard_map/mul | solution.py:126
  56.9 2.8 %concatenate.50.matrix_ref = f32[16,64,80]{2,1,0:T(8,128)} concatenate(f32[16,64,64]{2,1,0:T(8,128)S(1)} %bitcast.60, f32[16,64,1]{2,1,0:T(8,128)S(1)} %get-tuple-element.58, f32[16,64,1]{2,1,0:T(8,128)} %get-tuple-element.56, f32[16,64,6]{2,1,0:T(8,128)S(1)} %broadcast_in_dim.119, f32[16,64,1]{2,1,0:T(8,128)S(1)} %get-tuple-element.57, f32[16,64,1]{2,1,0:T(8,128)} %get-tuple-element.55, ...), dimensions={2} | concatenate | bytes 655360 | tf_op jit(solution)/shard_map/concatenate | solution.py:127
  59.7 2.9 %concatenate.47.matrix_ref = f32[16,64,80]{2,1,0:T(8,128)} concatenate(f32[16,64,64]{2,1,0:T(8,128)S(1)} %bitcast.61, f32[16,64,1]{2,1,0:T(8,128)} %get-tuple-element.50, f32[16,64,1]{2,1,0:T(8,128)} %get-tuple-element.48, f32[16,64,6]{2,1,0:T(8,128)S(1)} %broadcast_in_dim.119, f32[16,64,1]{2,1,0:T(8,128)} %get-tuple-element.49, f32[16,64,1]{2,1,0:T(8,128)S(1)} %copy-done.1, ...), dimensions={2} | concatenate | bytes 655360 | tf_op jit(solution)/shard_map/concatenate | solution.py:126
  62.6 2.6 %concatenate.51.mend_ref = f32[16,64,16]{2,1,0:T(8,128)} concatenate(f32[16,64,1]{2,1,0:T(8,128)} %get-tuple-element.66, f32[16,64,1]{2,1,0:T(8,128)} %get-tuple-element.65, f32[16,64,6]{2,1,0:T(8,128)S(1)} %broadcast_in_dim.119, f32[16,64,1]{2,1,0:T(8,128)S(1)} %copy-done.3, f32[16,64,1]{2,1,0:T(8,128)S(1)} %copy-done.2, f32[16,64,6]{2,1,0:T(8,128)S(1)} %broadcast_in_dim.119), dimensions={2} | concatenate | bytes 131072 | tf_op jit(solution)/shard_map/concatenate | solution.py:134
  65.2 10.5 %forward.1 = (f32[16,64,900]{2,1,0:T(8,128)}, f32[8,1024,128]{2,1,0:T(8,128)}) custom-call(f32[16,64,900]{2,1,0:T(8,128)} %control_ref.1, f32[16,8,900]{2,1,0:T(8,128)} %collective-permute-done.north_ref, f32[16,8,900]{2,1,0:T(8,128)} %collective-permute-done.1.south_ref, f32[16,64,80]{2,1,0:T(8,128)} %concatenate.47.matrix_ref), custom_call_target="tpu_custom_call" | custom-call | tf_op jit(solution)/shard_map/forward/pallas_call | solution.py:177
  75.6 0.9 copy.133
  76.5 56.1 %observe.1 = (f32[16,64,900]{2,1,0:T(8,128)}, f32[16,8,900]{2,1,0:T(8,128)}, f32[16,8,900]{2,1,0:T(8,128)}) custom-call(f32[128,1152]{1,0:T(8,128)} %bitcast.64, f32[8192,128]{1,0:T(8,128)} %bitcast.62, f32[128,128]{1,0:T(8,128)} %copy.122.gram_ref, bf16[256,512]{1,0:T(8,128)(2,1)} %constant.83.clone.pick_ref, f32[16,64,900]{2,1,0:T(8,128)} %control_ref.1, ...), custom_call_target="tpu_custom_call" | custom-call | tf_op jit(solution)/shard_map/observe/pallas_call | solution.py:400
  132.6 3.5 %collective-permute-start.2 = (f32[16,8,900]{2,1,0:T(8,128)}, f32[16,8,900]{2,1,0:T(8,128)S(1)}, u32[]{:S(2)}, u32[]{:S(2)}) collective-permute-start(f32[16,8,900]{2,1,0:T(8,128)} %get-tuple-element.23), channel_id=1, source_target_pairs={{0,8},{8,16},{16,24},{24,32},{32,40},{40,48},{48,56},{56,64},{64,7... | collective-permute-start | bytes 1382408 | tf_op jit(solution)/shard_map/ppermute | solution.py:151
  136.1 4.1 %collective-permute-start.3 = (f32[16,8,900]{2,1,0:T(8,128)}, f32[16,8,900]{2,1,0:T(8,128)S(1)}, u32[]{:S(2)}, u32[]{:S(2)}) collective-permute-start(f32[16,8,900]{2,1,0:T(8,128)} %get-tuple-element.24), channel_id=1, source_target_pairs={{8,0},{16,8},{24,16},{32,24},{40,32},{48,40},{56,48},{64,56},{72,6... | collective-permute-start | bytes 1382408 | tf_op jit(solution)/shard_map/ppermute | solution.py:150
  140.3 0.6 pad_add_fusion.order_ref
  140.8 1.7 dynamic-slice_bitcast_fusion
  142.5 0.7 copy.127.row_ref
  143.2 8.4 %tables.1 = (bf16[900,1024]{1,0:T(8,128)(2,1)}, bf16[900,1024]{1,0:T(8,128)(2,1)}, bf16[1024,900]{1,0:T(8,128)(2,1)}, bf16[1024,900]{1,0:T(8,128)(2,1)}) custom-call(f32[900,1024]{1,0:T(8,128)} %constant.85.clone.base_ref, f32[1024,900]{1,0:T(8,128)} %constant.86.clone.across_ref, f32[2,512]{1,0:T(2,128)} %copy.127.row_ref, f32[512,2]{1,0:T(8,128)} %get-tuple-element.45.col_ref), custom_call_target="tpu_custom_call" | custom-call | tf_op jit(solution)/shard_map/tables/pallas_call | solution.py:94
  151.7 0.8 copy-done.7
  152.5 0.2 copy-done.8
  152.6 13.6 %spectra.1 = (f32[16,64,900]{2,1,0:T(8,128)}, f32[4,128,1024]{2,1,0:T(8,128)}, f32[4,128,1024]{2,1,0:T(8,128)}) custom-call(s32[8]{0:T(128)} %pad_add_fusion.order_ref, f32[16,64,900]{2,1,0:T(8,128)} %get-tuple-element.22.local_ref, f32[16,8,900]{2,1,0:T(8,128)} %copy-done.7, f32[16,8,900]{2,1,0:T(8,128)} %copy-done.8, f32[16,64,16]{2,1,0:T(8,128)} %concatenate.51.mend_ref, ...), custom_call_target="tpu_custom_call" | custom-call | tf_op jit(solution)/shard_map/spectra/pallas_call | solution.py:443
  166.2 1.2 collective-permute-start.4
  167.4 4.0 %collective-permute-done.4 = f32[4,128,1024]{2,1,0:T(8,128)S(1)} collective-permute-done((f32[4,128,1024]{2,1,0:T(8,128)}, f32[4,128,1024]{2,1,0:T(8,128)S(1)}, u32[]{:S(2)}, u32[]{:S(2)}) %collective-permute-start.4) | collective-permute-done | bytes 2097184 | tf_op jit(solution)/shard_map/ppermute | solution.py:525
  171.4 2.0 add.75
  173.5 0.9 collective-permute-start.5
  174.4 1.8 collective-permute-start.7
  176.2 6.1 %collective-permute-done.5 = f32[64,1024]{1,0:T(8,128)S(1)} collective-permute-done((f32[64,1024]{1,0:T(8,128)S(1)}, f32[64,1024]{1,0:T(8,128)S(1)}, u32[]{:S(2)}, u32[]{:S(2)}) %collective-permute-start.5) | collective-permute-done | bytes 262176 | tf_op jit(solution)/shard_map/ppermute | solution.py:527
  182.4 2.4 %collective-permute-start.8 = (f32[128,1024]{1,0:T(8,128)S(1)}, f32[128,1024]{1,0:T(8,128)S(1)}, u32[]{:S(2)}, u32[]{:S(2)}) collective-permute-start(f32[128,1024]{1,0:T(8,128)S(1)} %pad_maximum_fusion.1), channel_id=1, source_target_pairs={{0,6},{1,7},{2,0},{3,1},{4,2},{5,3},{6,4},{7,5},{8,14},{9,15},{10,... | collective-permute-start | bytes 1572872 | tf_op jit(solution)/shard_map/ppermute | solution.py:530
  184.9 0.1 collective-permute-start.6
  185.0 9.7 %collective-permute-done.8 = f32[128,1024]{1,0:T(8,128)S(1)} collective-permute-done((f32[128,1024]{1,0:T(8,128)S(1)}, f32[128,1024]{1,0:T(8,128)S(1)}, u32[]{:S(2)}, u32[]{:S(2)}) %collective-permute-start.8) | collective-permute-done | bytes 524320 | tf_op jit(solution)/shard_map/ppermute | solution.py:530
  194.7 3.1 %collective-permute-done.6 = f32[128,1024]{1,0:T(8,128)S(1)} collective-permute-done((f32[128,1024]{1,0:T(8,128)S(1)}, f32[128,1024]{1,0:T(8,128)S(1)}, u32[]{:S(2)}, u32[]{:S(2)}) %collective-permute-start.6) | collective-permute-done | bytes 524320 | tf_op jit(solution)/shard_map/ppermute | solution.py:529
  197.8 0.1 fusion.2.refs_7_
  197.9 0.1 collective-permute-start.9
  198.0 2.7 %collective-permute-start.11 = (f32[128,1024]{1,0:T(8,128)S(1)}, f32[128,1024]{1,0:T(8,128)S(1)}, u32[]{:S(2)}, u32[]{:S(2)}) collective-permute-start(f32[128,1024]{1,0:T(8,128)S(1)} %fusion.2.refs_7_), channel_id=1, source_target_pairs={{0,6},{1,7},{2,0},{3,1},{4,2},{5,3},{6,4},{7,5},{8,14},{9,15},{10,... | collective-permute-start | bytes 1572872 | tf_op jit(solution)/shard_map/ppermute | solution.py:536
  200.7 9.2 %collective-permute-done.9.refs_6_ = f32[128,1024]{1,0:T(8,128)S(1)} collective-permute-done((f32[128,1024]{1,0:T(8,128)S(1)}, f32[128,1024]{1,0:T(8,128)S(1)}, u32[]{:S(2)}, u32[]{:S(2)}) %collective-permute-start.9) | collective-permute-done | bytes 524320 | tf_op jit(solution)/shard_map/ppermute | solution.py:535
  209.9 0.3 collective-permute-start.10
  210.3 2.7 %collective-permute-start.12 = (f32[64,1024]{1,0:T(8,128)S(1)}, f32[64,1024]{1,0:T(8,128)S(1)}, u32[]{:S(2)}, u32[]{:S(2)}) collective-permute-start(f32[64,1024]{1,0:T(8,128)S(1)} %slice.140), channel_id=1, source_target_pairs={{0,6},{1,7},{2,0},{3,1},{4,2},{5,3},{6,4},{7,5},{8,14},{9,15},{10,... | collective-permute-start | bytes 786440 | tf_op jit(solution)/shard_map/ppermute | solution.py:538
  213.0 4.2 %collective-permute-start.16 = (f32[128,1024]{1,0:T(8,128)S(1)}, f32[128,1024]{1,0:T(8,128)S(1)}, u32[]{:S(2)}, u32[]{:S(2)}) collective-permute-start(f32[128,1024]{1,0:T(8,128)S(1)} %fusion.2.refs_7_), channel_id=1, source_target_pairs={{0,1},{1,0},{2,3},{3,2},{4,5},{5,4},{6,7},{7,6},{8,9},{9,8},{10,11... | collective-permute-start | bytes 1572872 | tf_op jit(solution)/shard_map/ppermute | solution.py:541
  217.2 0.5 collective-permute-start.15
  217.8 3.8 %collective-permute-start.13 = (f32[128,1024]{1,0:T(8,128)S(1)}, f32[128,1024]{1,0:T(8,128)S(1)}, u32[]{:S(2)}, u32[]{:S(2)}) collective-permute-start(f32[128,1024]{1,0:T(8,128)S(1)} %constant_dynamic-update-slice_fusion.refs_4_), channel_id=1, source_target_pairs={{0,1},{1,0},{2,3},{3,2},{4,5},{5,4},{6,7},{7,6},{8,9},{9,8},{10,11... | collective-permute-start | bytes 1572872 | tf_op jit(solution)/shard_map/ppermute | solution.py:541
  221.6 1.5 collective-permute-done.13.refs_0_
  223.1 0.8 copy-done.12
  224.0 12.1 %synthesis.1 = f32[16,64,900]{2,1,0:T(8,128)} custom-call(s32[8]{0:T(128)} %pad_add_fusion.order_ref, bf16[1024,900]{1,0:T(8,128)(2,1)} %get-tuple-element.29.head_ref, bf16[1024,900]{1,0:T(8,128)(2,1)} %get-tuple-element.30.tail_ref, f32[128,1024]{1,0:T(8,128)} %copy-done.12, f32[128,1024]{1,0:T(8,128)} %copy-done.10, f32[128,1024]{1,0:T(8,128)} %copy-done.11, ...), custom_call_target="tpu_custom_call" | custom-call | tf_op jit(solution)/shard_map/synthesis/pallas_call | solution.py:467
  (75 shorter events, 0.6 us)
Async XLA Ops:
  0.6 1.3 copy-start.17
  6.3 13.0 %copy-start.13 = (s32[2048,1]{0,1:T(1,128)S(1)}, s32[2048,1]{0,1:T(1,128)}, u32[]{:S(2)}) copy-start(s32[2048,1]{0,1:T(1,128)} %param.23) | copy-start | bytes 24580
  6.3 14.3 %copy-start.14 = (s32[2048,4]{0,1:T(4,128)S(1)}, s32[2048,4]{0,1:T(4,128)}, u32[]{:S(2)}) copy-start(s32[2048,4]{0,1:T(4,128)} %param.24) | copy-start | bytes 98308
  10.4 11.6 %copy-start.15 = (f32[2048,4]{0,1:T(4,128)S(1)}, f32[2048,4]{0,1:T(4,128)}, u32[]{:S(2)}) copy-start(f32[2048,4]{0,1:T(4,128)} %param.25) | copy-start | bytes 98308
  10.4 12.9 %copy-start.16 = (f32[16,128]{1,0:T(8,128)S(1)}, f32[16,128]{1,0:T(8,128)}, u32[]{:S(2)}) copy-start(f32[16,128]{1,0:T(8,128)} %param.19) | copy-start | bytes 24580
  10.4 13.0 %copy-start.18 = (f32[128]{0:T(128)S(1)}, f32[128]{0:T(128)}, u32[]{:S(2)}) copy-start(f32[128]{0:T(128)} %param.20) | copy-start | bytes 1540
  10.4 54.7 %collective-permute-start = (f32[16,8,900]{2,1,0:T(8,128)}, f32[16,8,900]{2,1,0:T(8,128)}, u32[]{:S(2)}, u32[]{:S(2)}) collective-permute-start(f32[16,8,900]{2,1,0:T(8,128)} %get-tuple-element.18), channel_id=1, source_target_pairs={{0,8},{8,16},{16,24},{24,32},{32,40},{40,48},{48,56},{56,64},{64,7... | collective-permute-start | bytes 1382408 | tf_op jit(solution)/shard_map/ppermute | solution.py:151
  14.1 51.1 %collective-permute-start.1 = (f32[16,8,900]{2,1,0:T(8,128)}, f32[16,8,900]{2,1,0:T(8,128)}, u32[]{:S(2)}, u32[]{:S(2)}) collective-permute-start(f32[16,8,900]{2,1,0:T(8,128)} %get-tuple-element.19), channel_id=1, source_target_pairs={{8,0},{16,8},{24,16},{32,24},{40,32},{48,40},{56,48},{64,56},{72,6... | collective-permute-start | bytes 1382408 | tf_op jit(solution)/shard_map/ppermute | solution.py:150
  40.1 35.6 %all-to-all-start = ((f32[128,1,1152]{2,1,0:T(1,128)}), f32[128,1,1152]{2,1,0:T(1,128)S(1)}, u32[]{:S(2)}, u32[]{:S(2)}) async-start(f32[128,1,1152]{2,1,0:T(1,128)} %copy.120), calls=%async_computation | async-start | bytes 1179648 | tf_op jit(solution)/shard_map/all_to_all | solution.py:509
  56.9 2.8 %copy-start.1 = (f32[16,64,1]{2,1,0:T(8,128)S(1)}, f32[16,64,1]{2,1,0:T(8,128)}, u32[]{:S(2)}) copy-start(f32[16,64,1]{2,1,0:T(8,128)} %get-tuple-element.47) | copy-start | bytes 12292
  59.7 2.9 %copy-start.2 = (f32[16,64,1]{2,1,0:T(8,128)S(1)}, f32[16,64,1]{2,1,0:T(8,128)}, u32[]{:S(2)}) copy-start(f32[16,64,1]{2,1,0:T(8,128)} %get-tuple-element.63) | copy-start | bytes 12292
  59.7 2.9 %copy-start.3 = (f32[16,64,1]{2,1,0:T(8,128)S(1)}, f32[16,64,1]{2,1,0:T(8,128)}, u32[]{:S(2)}) copy-start(f32[16,64,1]{2,1,0:T(8,128)} %get-tuple-element.64) | copy-start | bytes 12292
  62.5 2.6 %copy-start.20 = (s32[4]{0:T(128)S(1)}, s32[4]{0:T(128)}, u32[]{:S(2)}) copy-start(s32[4]{0:T(128)} %constant.87.clone) | copy-start | bytes 52
  132.6 19.0 %collective-permute-start.2 = (f32[16,8,900]{2,1,0:T(8,128)}, f32[16,8,900]{2,1,0:T(8,128)S(1)}, u32[]{:S(2)}, u32[]{:S(2)}) collective-permute-start(f32[16,8,900]{2,1,0:T(8,128)} %get-tuple-element.23), channel_id=1, source_target_pairs={{0,8},{8,16},{16,24},{24,32},{32,40},{40,48},{48,56},{56,64},{64,7... | collective-permute-start | bytes 1382408 | tf_op jit(solution)/shard_map/ppermute | solution.py:151
  136.1 15.5 %collective-permute-start.3 = (f32[16,8,900]{2,1,0:T(8,128)}, f32[16,8,900]{2,1,0:T(8,128)S(1)}, u32[]{:S(2)}, u32[]{:S(2)}) collective-permute-start(f32[16,8,900]{2,1,0:T(8,128)} %get-tuple-element.24), channel_id=1, source_target_pairs={{8,0},{16,8},{24,16},{32,24},{40,32},{48,40},{56,48},{64,56},{72,6... | collective-permute-start | bytes 1382408 | tf_op jit(solution)/shard_map/ppermute | solution.py:150
  151.6 0.8 copy-start.7
  151.7 1.0 copy-start.8
  166.2 5.2 %collective-permute-start.4 = (f32[4,128,1024]{2,1,0:T(8,128)}, f32[4,128,1024]{2,1,0:T(8,128)S(1)}, u32[]{:S(2)}, u32[]{:S(2)}) collective-permute-start(f32[4,128,1024]{2,1,0:T(8,128)} %get-tuple-element.32), channel_id=1, source_target_pairs={{0,1},{1,0},{2,3},{3,2},{4,5},{5,4},{6,7},{7,6},{8,9},{9,8},{10,11... | collective-permute-start | bytes 6291464 | tf_op jit(solution)/shard_map/ppermute | solution.py:525
  173.5 11.5 %copy-start.19 = (f32[512]{0:T(512)S(1)}, f32[512]{0:T(512)}, u32[]{:S(2)}) copy-start(f32[512]{0:T(512)} %param.21) | copy-start | bytes 6148
  173.5 8.8 %collective-permute-start.5 = (f32[64,1024]{1,0:T(8,128)S(1)}, f32[64,1024]{1,0:T(8,128)S(1)}, u32[]{:S(2)}, u32[]{:S(2)}) collective-permute-start(f32[64,1024]{1,0:T(8,128)S(1)} %get-tuple-element.41), channel_id=1, source_target_pairs={{0,2},{1,3},{2,4},{3,5},{4,6},{5,7},{6,0},{7,1},{8,10},{9,11},{10,... | collective-permute-start | bytes 786440 | tf_op jit(solution)/shard_map/ppermute | solution.py:527
  174.4 7.9 %collective-permute-start.7 = (f32[64,1024]{1,0:T(8,128)S(1)}, f32[64,1024]{1,0:T(8,128)S(1)}, u32[]{:S(2)}, u32[]{:S(2)}) collective-permute-start(f32[64,1024]{1,0:T(8,128)S(1)} %get-tuple-element.42), channel_id=1, source_target_pairs={{0,6},{1,7},{2,0},{3,1},{4,2},{5,3},{6,4},{7,5},{8,14},{9,15},{10,... | collective-permute-start | bytes 786440 | tf_op jit(solution)/shard_map/ppermute | solution.py:528
  182.4 12.3 %collective-permute-start.8 = (f32[128,1024]{1,0:T(8,128)S(1)}, f32[128,1024]{1,0:T(8,128)S(1)}, u32[]{:S(2)}, u32[]{:S(2)}) collective-permute-start(f32[128,1024]{1,0:T(8,128)S(1)} %pad_maximum_fusion.1), channel_id=1, source_target_pairs={{0,6},{1,7},{2,0},{3,1},{4,2},{5,3},{6,4},{7,5},{8,14},{9,15},{10,... | collective-permute-start | bytes 1572872 | tf_op jit(solution)/shard_map/ppermute | solution.py:530
  184.9 12.9 %collective-permute-start.6 = (f32[128,1024]{1,0:T(8,128)S(1)}, f32[128,1024]{1,0:T(8,128)S(1)}, u32[]{:S(2)}, u32[]{:S(2)}) collective-permute-start(f32[128,1024]{1,0:T(8,128)S(1)} %pad_maximum_fusion), channel_id=1, source_target_pairs={{0,2},{1,3},{2,4},{3,5},{4,6},{5,7},{6,0},{7,1},{8,10},{9,11},{10,... | collective-permute-start | bytes 1572872 | tf_op jit(solution)/shard_map/ppermute | solution.py:529
  197.9 26.0 %copy-start = (f32[128,1024]{1,0:T(8,128)}, f32[128,1024]{1,0:T(8,128)S(1)}, u32[]{:S(2)}) copy-start(f32[128,1024]{1,0:T(8,128)S(1)} %fusion.2.refs_7_) | copy-start | bytes 1572868
  197.9 12.0 %collective-permute-start.9 = (f32[128,1024]{1,0:T(8,128)S(1)}, f32[128,1024]{1,0:T(8,128)S(1)}, u32[]{:S(2)}, u32[]{:S(2)}) collective-permute-start(f32[128,1024]{1,0:T(8,128)S(1)} %fusion.2.refs_7_), channel_id=1, source_target_pairs={{0,2},{1,3},{2,4},{3,5},{4,6},{5,7},{6,0},{7,1},{8,10},{9,11},{10,... | collective-permute-start | bytes 1572872 | tf_op jit(solution)/shard_map/ppermute | solution.py:535
  198.0 12.2 %collective-permute-start.11 = (f32[128,1024]{1,0:T(8,128)S(1)}, f32[128,1024]{1,0:T(8,128)S(1)}, u32[]{:S(2)}, u32[]{:S(2)}) collective-permute-start(f32[128,1024]{1,0:T(8,128)S(1)} %fusion.2.refs_7_), channel_id=1, source_target_pairs={{0,6},{1,7},{2,0},{3,1},{4,2},{5,3},{6,4},{7,5},{8,14},{9,15},{10,... | collective-permute-start | bytes 1572872 | tf_op jit(solution)/shard_map/ppermute | solution.py:536
  209.9 14.1 %copy-start.4 = (f32[128,1024]{1,0:T(8,128)}, f32[128,1024]{1,0:T(8,128)S(1)}, u32[]{:S(2)}) copy-start(f32[128,1024]{1,0:T(8,128)S(1)} %collective-permute-done.9.refs_6_) | copy-start | bytes 1572868
  209.9 7.8 %collective-permute-start.10 = (f32[64,1024]{1,0:T(8,128)S(1)}, f32[64,1024]{1,0:T(8,128)S(1)}, u32[]{:S(2)}, u32[]{:S(2)}) collective-permute-start(f32[64,1024]{1,0:T(8,128)S(1)} %slice.139), channel_id=1, source_target_pairs={{0,2},{1,3},{2,4},{3,5},{4,6},{5,7},{6,0},{7,1},{8,10},{9,11},{10,... | collective-permute-start | bytes 786440 | tf_op jit(solution)/shard_map/ppermute | solution.py:537
  210.2 13.7 %copy-start.5 = (f32[128,1024]{1,0:T(8,128)}, f32[128,1024]{1,0:T(8,128)S(1)}, u32[]{:S(2)}) copy-start(f32[128,1024]{1,0:T(8,128)S(1)} %collective-permute-done.11.refs_5_) | copy-start | bytes 1572868
  210.3 7.5 %collective-permute-start.12 = (f32[64,1024]{1,0:T(8,128)S(1)}, f32[64,1024]{1,0:T(8,128)S(1)}, u32[]{:S(2)}, u32[]{:S(2)}) collective-permute-start(f32[64,1024]{1,0:T(8,128)S(1)} %slice.140), channel_id=1, source_target_pairs={{0,6},{1,7},{2,0},{3,1},{4,2},{5,3},{6,4},{7,5},{8,14},{9,15},{10,... | collective-permute-start | bytes 786440 | tf_op jit(solution)/shard_map/ppermute | solution.py:538
  213.0 8.6 %collective-permute-start.16 = (f32[128,1024]{1,0:T(8,128)S(1)}, f32[128,1024]{1,0:T(8,128)S(1)}, u32[]{:S(2)}, u32[]{:S(2)}) collective-permute-start(f32[128,1024]{1,0:T(8,128)S(1)} %fusion.2.refs_7_), channel_id=1, source_target_pairs={{0,1},{1,0},{2,3},{3,2},{4,5},{5,4},{6,7},{7,6},{8,9},{9,8},{10,11... | collective-permute-start | bytes 1572872 | tf_op jit(solution)/shard_map/ppermute | solution.py:541
  217.2 4.4 %collective-permute-start.14 = (f32[128,1024]{1,0:T(8,128)S(1)}, f32[128,1024]{1,0:T(8,128)S(1)}, u32[]{:S(2)}, u32[]{:S(2)}) collective-permute-start(f32[128,1024]{1,0:T(8,128)S(1)} %collective-permute-done.11.refs_5_), channel_id=1, source_target_pairs={{0,1},{1,0},{2,3},{3,2},{4,5},{5,4},{6,7},{7,6},{8,9},{9,8},{10,11... | collective-permute-start | bytes 1572872 | tf_op jit(solution)/shard_map/ppermute | solution.py:541
  217.2 4.4 %collective-permute-start.15 = (f32[128,1024]{1,0:T(8,128)S(1)}, f32[128,1024]{1,0:T(8,128)S(1)}, u32[]{:S(2)}, u32[]{:S(2)}) collective-permute-start(f32[128,1024]{1,0:T(8,128)S(1)} %collective-permute-done.9.refs_6_), channel_id=1, source_target_pairs={{0,1},{1,0},{2,3},{3,2},{4,5},{5,4},{6,7},{7,6},{8,9},{9,8},{10,11... | collective-permute-start | bytes 1572872 | tf_op jit(solution)/shard_map/ppermute | solution.py:541
  217.8 6.2 %copy-start.6 = (f32[128,1024]{1,0:T(8,128)}, f32[128,1024]{1,0:T(8,128)S(1)}, u32[]{:S(2)}) copy-start(f32[128,1024]{1,0:T(8,128)S(1)} %constant_dynamic-update-slice_fusion.refs_4_) | copy-start | bytes 1572868
  217.8 5.4 %collective-permute-start.13 = (f32[128,1024]{1,0:T(8,128)S(1)}, f32[128,1024]{1,0:T(8,128)S(1)}, u32[]{:S(2)}, u32[]{:S(2)}) collective-permute-start(f32[128,1024]{1,0:T(8,128)S(1)} %constant_dynamic-update-slice_fusion.refs_4_), channel_id=1, source_target_pairs={{0,1},{1,0},{2,3},{3,2},{4,5},{5,4},{6,7},{7,6},{8,9},{9,8},{10,11... | collective-permute-start | bytes 1572872 | tf_op jit(solution)/shard_map/ppermute | solution.py:541
  221.6 2.3 copy-start.9
  221.6 2.3 copy-start.10
  221.6 2.3 copy-start.11
  223.1 0.8 copy-start.12

commit v2 on v1

v2 whole, which is shorter than its diff:
```python
import functools

import jax
import jax.numpy as jnp
import ml_dtypes
import numpy as np
from jax import lax
from jax.experimental import pallas as pl
from jax.experimental.pallas import tpu as pltpu
from jax.sharding import PartitionSpec as P

CH = 16
KEEP = 512
NLON = 7200
CLON = 900
RLAT = 64
HALF = 32
SLOTS = 32
TILES = 128
ROWS = 2048
LANES = 128
WORDS = LANES + SLOTS * 32
CELL_ROWS = 8 * 1024
ACCS = 4
F32 = jnp.float32
BF16 = jnp.bfloat16
EXACT = lax.Precision.HIGHEST
VM = pl.BlockSpec(memory_space=pltpu.VMEM)
SM = pl.BlockSpec(memory_space=pltpu.SMEM)


def params(mebibytes):
    return pltpu.CompilerParams(vmem_limit_bytes=mebibytes * 1024 * 1024)


def split(x):
    head = x.astype(BF16)
    return head, (x - head.astype(F32)).astype(BF16)


def mm(a, b):
    return jnp.dot(a, b, preferred_element_type=F32)


def dot3(a, b):
    a_head, a_tail = split(a)
    b_head, b_tail = split(b)
    rows = a.shape[0]
    both = mm(jnp.concatenate([a_head, a_tail], axis=0), b_head)
    return both[:rows] + both[rows:] + mm(a_head, b_tail)


def base_tables():
    longitude = np.arange(CLON)[:, None]
    wavenumber = np.arange(KEEP)[None, :]
    phase = 2.0 * np.pi * ((longitude * wavenumber) % NLON) / NLON
    table = np.concatenate([np.cos(phase), np.sin(phase)], axis=1).astype(np.float32)
    head = table.astype(ml_dtypes.bfloat16)
    tail = (table - head.astype(np.float32)).astype(ml_dtypes.bfloat16)
    return head, tail


def turn_tables():
    tile = np.arange(8)[:, None]
    wavenumber = np.arange(KEEP)[None, :]
    phase = 2.0 * np.pi * ((tile * wavenumber) % 8) / 8
    turns = np.stack([np.cos(phase), np.sin(phase)], axis=1).astype(np.float32)
    return np.concatenate([turns, np.zeros((8, 6, KEEP), np.float32)], axis=1)


def bands_kernel(
    field_ref, inverse_ref, coupling_ref, forward_ref, backward_ref, mend_ref, north_ref, south_ref
):
    def at(shape, axis):
        return lax.broadcasted_iota(jnp.int32, shape, axis)

    half = (HALF, LANES)
    upper_place = (at(half, 1) == at(half, 0)).astype(F32)
    lower_place = (at(half, 1) == at(half, 0) + HALF).astype(F32)
    full = (RLAT, LANES)
    column, row = at(full, 1), at(full, 0)
    few = (16, RLAT)
    few_column, few_row = at(few, 1), at(few, 0)
    few_place = at((16, 1), 0)
    last_row = RLAT - 1
    for channel in range(CH):
        c = coupling_ref[channel]
        blocks = jnp.concatenate(
            [
                jnp.dot(inverse_ref[0, channel], upper_place, precision=EXACT, preferred_element_type=F32),
                jnp.dot(inverse_ref[1, channel], lower_place, precision=EXACT, preferred_element_type=F32),
            ],
            axis=0,
        )
        step = blocks + c * (
            jnp.where(column == HALF, blocks[:, HALF - 1 : HALF], 0.0)
            + jnp.where(column == HALF - 1, blocks[:, HALF : HALF + 1], 0.0)
        )
        first, last = blocks[:, 0:1], blocks[:, last_row : last_row + 1]
        right = jnp.concatenate(
            [
                step + jnp.where(column == 64, c * first, 0.0) + jnp.where(column == 72, c * last, 0.0),
                step + jnp.where(column == 65, first, 0.0) + jnp.where(column == 73, last, 0.0),
            ],
            axis=1,
        )
        product = jnp.dot(step[:, :RLAT], right, precision=EXACT, preferred_element_type=F32)
        forward_ref[channel] = (
            product[:, :LANES]
            + jnp.where(column == 65, c * first, 0.0)
            + jnp.where(column == 73, c * last, 0.0)
        )
        backward_ref[channel] = (
            product[:, LANES:] + jnp.where(column == 64, first, 0.0) + jnp.where(column == 72, last, 0.0)
        )
        turned = step.T[:RLAT]
        mend_ref[channel] = c * (
            jnp.where(column == 0, turned[:, 0:1], 0.0)
            + jnp.where((column == 1) & (row == 0), 1.0, 0.0)
            + jnp.where(column == 2, turned[:, last_row : last_row + 1], 0.0)
            + jnp.where((column == 3) & (row == last_row), 1.0, 0.0)
        )
        edges = (
            jnp.where((few_row == 0) & (few_column == 0), 1.0, 0.0)
            + jnp.where(few_row == 1, step[0:1, :RLAT], 0.0)
            + jnp.where((few_row == 8) & (few_column == last_row), 1.0, 0.0)
            + jnp.where(few_row == 9, step[last_row : last_row + 1, :RLAT], 0.0)
        )
        rows = (
            dot3(edges, field_ref[channel])
            + jnp.where(few_place == 2, c * blocks[0:1, 0:1], 0.0)
            + jnp.where(few_place == 10, c * blocks[last_row : last_row + 1, last_row : last_row + 1], 0.0)
        )
        north_ref[channel] = rows[:8]
        south_ref[channel] = rows[8:]


def bands(control, inverse, coupling):
    matrix = jax.ShapeDtypeStruct((CH, RLAT, LANES), F32)
    edge = jax.ShapeDtypeStruct((CH, 8, CLON), F32)
    return pl.pallas_call(
        bands_kernel,
        out_shape=(matrix, matrix, matrix, edge, edge),
        in_specs=[VM, VM, SM],
        out_specs=(VM,) * 5,
        compiler_params=params(24),
        name="bands",
    )(control, inverse, coupling)


def send_edges(north, south):
    count = lax.axis_size("lat")
    from_south = lax.ppermute(north, "lat", [(i + 1, i) for i in range(count - 1)])
    from_north = lax.ppermute(south, "lat", [(i, i + 1) for i in range(count - 1)])
    return from_north, from_south


def forward_kernel(field_ref, north_ref, south_ref, matrix_ref, state_ref, cells_ref):
    column = lax.broadcasted_iota(jnp.int32, (RLAT, LANES), 1)
    for channel in range(CH):
        matrix = matrix_ref[channel]
        alpha_north = north_ref[channel, 2:3, 0:1]
        alpha_south = south_ref[channel, 2:3, 0:1]
        matrix = (
            matrix
            + jnp.where(column == 0, matrix[:, 65:66] * alpha_north, 0.0)
            + jnp.where(column == RLAT - 1, matrix[:, 73:74] * alpha_south, 0.0)
        )
        field = jnp.concatenate([field_ref[channel], north_ref[channel], south_ref[channel]], axis=0)
        state_ref[channel] = dot3(matrix[:, :80], field)
    for group in range(8):
        for lane_tile in range(2):
            lanes = slice(lane_tile * LANES, (lane_tile + 1) * LANES)
            piece = state_ref[:, group * 8 : (group + 1) * 8, lanes].reshape(LANES, LANES)
            cells_ref[group, lanes, :] = piece.T


def forward_diffusion(control, from_north, from_south, forward):
    width = 256
    return pl.pallas_call(
        forward_kernel,
        grid=(4,),
        out_shape=(
            jax.ShapeDtypeStruct((CH, RLAT, CLON), F32),
            jax.ShapeDtypeStruct((8, 1024, LANES), F32),
        ),
        in_specs=[
            pl.BlockSpec((CH, RLAT, width), lambda i: (0, 0, i)),
            pl.BlockSpec((CH, 8, width), lambda i: (0, 0, i)),
            pl.BlockSpec((CH, 8, width), lambda i: (0, 0, i)),
            pl.BlockSpec((CH, RLAT, LANES), lambda i: (0, 0, 0)),
        ],
        out_specs=(
            pl.BlockSpec((CH, RLAT, width), lambda i: (0, 0, i)),
            pl.BlockSpec((8, width, LANES), lambda i: (0, i, 0)),
        ),
        compiler_params=params(28),
        name="forward",
    )(control, from_north, from_south, forward)


def route_kernel(live_ref, values_ref, tile_ref, points_ref, weights_ref, project_ref, out_ref, turned_ref, column_ref, rank_ref):
    live = live_ref[0]
    lane = lax.broadcasted_iota(jnp.int32, (1, LANES), 1)
    order = lax.broadcasted_iota(jnp.int32, (1, ROWS), 1)
    points = points_ref[...]
    latitude = points // CLON
    turned_ref[0:4, :] = ((latitude // 8) * 1024 + (points - latitude * CLON)).astype(F32)
    turned_ref[4:8, :] = weights_ref[...]
    turned_ref[8:12, :] = (latitude % 8).astype(F32)
    alive = jnp.where(order < live, tile_ref[...], -1)
    turned_ref[12:13, :] = alive.astype(F32)
    for part in range(ROWS // LANES):
        some = slice(part * LANES, (part + 1) * LANES)
        column_ref[some, :] = turned_ref[:, some].T
    block = 256
    below = (
        lax.broadcasted_iota(jnp.int32, (block, block), 1) < lax.broadcasted_iota(jnp.int32, (block, block), 0)
    ).astype(F32).astype(BF16)
    lane_number = lane.astype(F32)
    base = jnp.zeros((1, LANES), F32)
    for part in range(ROWS // block):
        rows = slice(part * block, (part + 1) * block)
        named = (column_ref[rows, 12:13] == lane_number).astype(F32)
        before = mm(below, named.astype(BF16)) + base
        rank_ref[rows, :] = jnp.broadcast_to(jnp.sum(named * before, axis=1, keepdims=True), (block, LANES))
        base = base + jnp.sum(named, axis=0, keepdims=True)
    chosen = (alive == lax.broadcasted_iota(jnp.int32, (TILES, 1), 0)).astype(F32).astype(BF16)
    group = lane // 32
    inner = lane % 32
    features = dot3(values_ref[...], project_ref[...])
    cell_rows = jnp.zeros((ROWS, LANES), F32)
    for point in range(4):
        features = jnp.where(inner == point, column_ref[:, 4 + point : 5 + point], features)
        features = jnp.where(inner == 4 + point, column_ref[:, 8 + point : 9 + point], features)
        cell_rows = jnp.where(group == point, column_ref[:, point : point + 1], cell_rows)
    rank = rank_ref[...]

    def deliver(masked):
        both = mm(chosen, jnp.concatenate(split(masked), axis=1))
        return both[:, :LANES] + both[:, LANES:]

    out_ref[:, 0, :LANES] = deliver(jnp.where(rank == inner.astype(F32), cell_rows, 0.0))
    for tile in range(8):
        lanes = slice((tile + 1) * LANES, (tile + 2) * LANES)
        out_ref[:, 0, lanes] = deliver(jnp.where(rank == (tile * 4 + group).astype(F32), features, 0.0))


def route(live_rows, obs_values, obs_tile, obs_points, obs_weights, jacobian, error_weight):
    project = jnp.pad((jacobian * error_weight).T, ((0, 0), (8, 8)))
    project = jnp.concatenate([project] * 4, axis=1)
    return pl.pallas_call(
        route_kernel,
        out_shape=jax.ShapeDtypeStruct((TILES, 1, WORDS), F32),
        in_specs=[SM] + [VM] * 5,
        out_specs=VM,
        scratch_shapes=[
            pltpu.VMEM((LANES, ROWS), F32),
            pltpu.VMEM((ROWS, LANES), F32),
            pltpu.VMEM((ROWS, LANES), F32),
        ],
        compiler_params=params(32),
        name="route",
    )(live_rows, obs_values, obs_tile.T, obs_points.T, obs_weights.T, project)


def pick_table():
    pick = np.zeros((LANES, 4 * LANES), np.float32)
    for slot in range(4):
        for channel in range(CH):
            first = slot * LANES + channel * 8
            pick[slot * 32 + 8 + channel, first : first + 8] = -1.0
    return np.concatenate([pick, pick], axis=0)


def observe_kernel(
    rows_ref,
    cells_ref,
    gram_ref,
    pick_ref,
    matrix_ref,
    field_ref,
    to_north_ref,
    to_south_ref,
    index_ref,
    where_ref,
    mask_ref,
    columns_ref,
    values_ref,
    index_semaphore,
    *sums,
):
    index_ref[...] = rows_ref[:, :LANES].astype(jnp.int32)
    copy = pltpu.make_async_copy(index_ref, where_ref, index_semaphore)
    copy.start()
    zero_rows = 256

    def clear(step, carry):
        for total in sums:
            total[pl.ds(pl.multiple_of(step * zero_rows, zero_rows), zero_rows), :] = jnp.zeros((zero_rows, LANES), F32)
        return carry

    lax.fori_loop(0, CELL_ROWS // zero_rows, clear, 0)
    lane_level = (lax.broadcasted_iota(jnp.int32, (1, LANES), 1) % 8).astype(F32)
    gram_head, gram_tail = split(gram_ref[...])
    gram_both = jnp.concatenate([gram_head, gram_tail], axis=0)

    def prepare(tile, carry):
        data = rows_ref[:, pl.ds(pl.multiple_of((tile + 1) * LANES, LANES), LANES)]
        values = mm(jnp.concatenate(split(data), axis=1), pick_ref[...])
        for slot in range(4):
            values_ref[tile * 4 + slot] = values[:, slot * LANES : (slot + 1) * LANES]
            for point in range(4):
                weight = data[:, slot * 32 + point : slot * 32 + point + 1]
                level = data[:, slot * 32 + 4 + point : slot * 32 + 5 + point]
                mask_ref[point, tile * 4 + slot] = jnp.where(level == lane_level, weight, 0.0)
        return carry

    lax.fori_loop(0, 8, prepare, 0)
    copy.wait()
    chunk = 16

    def move(fetch, store):
        def source(step, carry):
            for slot in range(SLOTS):
                if fetch is not None:
                    taken = fetch * chunk + step
                    interp = None
                    for point in range(4):
                        cell = where_ref[taken, point * 32 + slot]
                        term = cells_ref[pl.ds(cell, 1), :] * mask_ref[point, slot, pl.ds(taken, 1), :]
                        interp = term if interp is None else interp + term
                if store is not None:
                    given = store * chunk + step
                    column = columns_ref[slot, pl.ds(given, 1), :]
                    cells = [where_ref[given, point * 32 + slot] for point in range(4)]
                    fresh = [
                        sums[point][pl.ds(cells[point], 1), :] + mask_ref[point, slot, pl.ds(given, 1), :] * column
                        for point in range(4)
                    ]
                    for point in range(4):
                        sums[point][pl.ds(cells[point], 1), :] = fresh[point]
                if fetch is not None:
                    columns_ref[slot, pl.ds(taken, 1), :] = interp
            return carry

        lax.fori_loop(0, chunk, source, 0)

    def weigh(index):
        rows = pl.ds(pl.multiple_of(index * chunk, chunk), chunk)
        interp = columns_ref[:, rows, :].reshape(SLOTS * chunk, LANES)
        head, tail = split(interp)
        columns = mm(head, gram_head) + mm(jnp.concatenate([tail, head], axis=1), gram_both)
        columns_ref[:, rows, :] = columns.reshape(SLOTS, chunk, LANES) + values_ref[:, rows, :]

    move(0, None)
    weigh(0)

    def rounds(index, carry):
        move(index, index - 1)
        weigh(index)
        return carry

    last = TILES // chunk - 1
    lax.fori_loop(1, last + 1, rounds, 0)
    move(None, last)

    def turn(tile, carry):
        first = pl.multiple_of(tile * LANES, LANES)
        for group in range(8):
            piece = sums[0][pl.ds(group * 1024 + first, LANES), :]
            for total in sums[1:]:
                piece = piece + total[pl.ds(group * 1024 + first, LANES), :]
            field_ref[:, group * 8 : (group + 1) * 8, pl.ds(first, LANES)] = piece.T.reshape(CH, 8, LANES)
        return carry

    lax.fori_loop(0, 8, turn, 0)

    for channel in range(CH):
        result = dot3(matrix_ref[channel].T[RLAT : RLAT + 16], field_ref[channel])
        to_north_ref[channel] = result[0:2, :CLON]
        to_south_ref[channel] = result[8:10, :CLON]


def observe(rows, cells, gram, backward):
    edge = jax.ShapeDtypeStruct((CH, 2, CLON), F32)
    return pl.pallas_call(
        observe_kernel,
        out_shape=(jax.ShapeDtypeStruct((CH, RLAT, 1024), F32), edge, edge),
        in_specs=[VM] * 5,
        out_specs=(VM, VM, VM),
        scratch_shapes=[
            pltpu.VMEM((TILES, LANES), jnp.int32),
            pltpu.SMEM((TILES, LANES), jnp.int32),
            pltpu.VMEM((4, SLOTS, TILES, LANES), F32),
            pltpu.VMEM((SLOTS, TILES, LANES), F32),
            pltpu.VMEM((SLOTS, TILES, LANES), F32),
            pltpu.SemaphoreType.DMA,
        ]
        + [pltpu.VMEM((CELL_ROWS, LANES), F32)] * ACCS,
        compiler_params=params(52),
        name="observe",
    )(rows, cells, gram, jnp.asarray(pick_table(), BF16), backward)


def adjoint_kernel(field_ref, control_ref, matrix_ref, north_ref, south_ref, coupling_ref, local_ref):
    column = lax.broadcasted_iota(jnp.int32, (RLAT, LANES), 1)
    for inner in range(4):
        matrix = matrix_ref[inner]
        coupling = coupling_ref[pl.program_id(0) * 4 + inner]
        alpha_north = north_ref[inner, 2:3, 0:1] * coupling
        alpha_south = south_ref[inner, 2:3, 0:1] * coupling
        matrix = (
            matrix
            + jnp.where(column == 0, matrix[:, 64:65] * alpha_north, 0.0)
            + jnp.where(column == RLAT - 1, matrix[:, 72:73] * alpha_south, 0.0)
        )
        local_ref[inner] = control_ref[inner] + dot3(matrix.T[:RLAT], field_ref[inner])[:, :CLON]


def adjoint_diffusion(field, control, backward, from_north, from_south, coupling):
    def four(*shape):
        return pl.BlockSpec((4,) + shape, lambda i: (i, 0, 0))

    return pl.pallas_call(
        adjoint_kernel,
        grid=(4,),
        out_shape=jax.ShapeDtypeStruct((CH, RLAT, CLON), F32),
        in_specs=[four(RLAT, 1024), four(RLAT, CLON), four(RLAT, LANES), four(8, LANES), four(8, LANES), SM],
        out_specs=four(RLAT, CLON),
        cost_estimate=pl.CostEstimate(flops=6 * 64 * 64 * 16 * 1024, bytes_accessed=12 << 20, transcendentals=0),
        compiler_params=params(20),
        name="adjoint",
    )(field, control, backward, from_north, from_south, coupling)


ANY = pl.BlockSpec(memory_space=pl.ANY)
DFT_COST = pl.CostEstimate(flops=6 * 256 * 1024 * 1024, bytes_accessed=8 << 20, transcendentals=0)


def spectra_kernel(base, added, outputs, order_ref, local_any, north_ref, south_ref, mend_ref, head_ref, tail_ref, turn_ref, *refs):
    if added:
        add_ref, refs = refs[0], refs[1:]
    gradient_any, refs = refs[0], refs[1:]
    out_refs, (field_ref, in_semaphores, out_semaphores) = refs[:outputs], refs[outputs:]
    channels = [order_ref[base + i] for i in range(4)]
    loads = [
        pltpu.make_async_copy(local_any.at[channels[i]], field_ref.at[i], in_semaphores.at[i]) for i in range(4)
    ]
    for load in loads:
        load.start()
    for load in loads:
        load.wait()
    for here, channel in enumerate(channels):
        mend = mend_ref[channel]
        north, south = north_ref[channel], south_ref[channel]
        field_ref[here] = (
            field_ref[here]
            + mend[:, 0:1] * north[0:1]
            + mend[:, 1:2] * north[1:2]
            + mend[:, 2:3] * south[0:1]
            + mend[:, 3:4] * south[1:2]
        )
    saves = [
        pltpu.make_async_copy(field_ref.at[i], gradient_any.at[channels[i]], out_semaphores.at[i]) for i in range(4)
    ]
    for save in saves:
        save.start()
    rows = 256
    head, tail = split(field_ref[...].reshape(rows, CLON))
    both = mm(jnp.concatenate([head, tail], axis=0), head_ref[...])
    result = both[:rows] + both[rows:] + mm(head, tail_ref[...])
    cos, sin = result[:, :KEEP], result[:, KEEP:]
    turn_cos, turn_sin = turn_ref[0:1, :], turn_ref[1:2, :]
    turned = (cos * turn_cos - sin * turn_sin, sin * turn_cos + cos * turn_sin)
    for part in range(2):
        lanes = slice(part * KEEP, (part + 1) * KEEP)
        for here in range(4):
            piece = turned[part][here * RLAT : (here + 1) * RLAT]
            if added:
                piece = piece + add_ref[here, :, lanes]
            out_refs[here * outputs // 4][here % (4 // outputs), :, lanes] = piece
    for save in saves:
        save.wait()


def spectra(base, order, local, north, south, mend, tables, turns, add=None):
    operands = [order, local, north, south, mend, *tables, turns]
    specs = [SM, ANY] + [VM] * 6
    outputs = 1
    if add is not None:
        operands.append(add)
        specs.append(VM)
        outputs = 2
    block = jax.ShapeDtypeStruct((4 // outputs, RLAT, 2 * KEEP), F32)
    return pl.pallas_call(
        functools.partial(spectra_kernel, base, add is not None, outputs),
        out_shape=(jax.ShapeDtypeStruct((CH, RLAT, CLON), F32),) + (block,) * outputs,
        in_specs=specs,
        out_specs=(ANY,) + (VM,) * outputs,
        scratch_shapes=[
            pltpu.VMEM((4, RLAT, CLON), F32),
            pltpu.SemaphoreType.DMA((4,)),
            pltpu.SemaphoreType.DMA((4,)),
        ],
        input_output_aliases={1: 0},
        cost_estimate=DFT_COST,
        compiler_params=params(24),
        name="spectra",
    )(*operands)


def synthesis_kernel(place, resumed, order_ref, head_ref, tail_ref, turn_ref, *refs):
    if resumed:
        refs = refs[1:]
    pieces, (out_any, field_ref, semaphores) = refs[:-3], refs[-3:]
    values = jnp.concatenate([piece[...] for piece in pieces], axis=0)
    cos, sin = values[:, :KEEP], values[:, KEEP:]
    turn_cos, turn_sin = turn_ref[0:1, :], turn_ref[1:2, :]
    values = jnp.concatenate([cos * turn_cos + sin * turn_sin, sin * turn_cos - cos * turn_sin], axis=1)
    head, tail = split(values)
    rows = 256
    both = mm(jnp.concatenate([head, tail], axis=0), head_ref[...])
    result = both[:rows] + both[rows:] + mm(head, tail_ref[...])
    field_ref[...] = result.reshape(4, RLAT, CLON)
    saves = [
        pltpu.make_async_copy(
            field_ref.at[pl.ds(2 * i, 2)], out_any.at[pl.ds(order_ref[place + 8 * (1 - i)], 2)], semaphores.at[i]
        )
        for i in range(2)
    ]
    for save in saves:
        save.start()
    for save in saves:
        save.wait()


def synthesis(place, order, tables, turns, pieces, before=None):
    operands = [order, *tables, turns]
    specs = [SM] + [VM] * 3
    if before is not None:
        operands.append(before)
        specs.append(ANY)
    return pl.pallas_call(
        functools.partial(synthesis_kernel, place, before is not None),
        out_shape=jax.ShapeDtypeStruct((CH, RLAT, CLON), F32),
        in_specs=specs + [VM] * len(pieces),
        out_specs=ANY,
        scratch_shapes=[pltpu.VMEM((4, RLAT, CLON), F32), pltpu.SemaphoreType.DMA((2,))],
        input_output_aliases={} if before is None else {4: 0},
        cost_estimate=DFT_COST,
        compiler_params=params(24),
        name="synthesis",
    )(*operands, *pieces)


def body(
    control,
    inverse,
    coupling,
    jacobian,
    error_weight,
    response,
    obs_values,
    obs_tile,
    obs_points,
    obs_weights,
    live_rows,
):
    lon = lax.axis_index("lon")
    ring, core = lon // 2, lon % 2
    partner = [(i, i ^ 1) for i in range(8)]
    onward = [(i, (i + 2) % 8) for i in range(8)]
    back = [(i, (i - 2) % 8) for i in range(8)]

    forward, backward, mend, north, south = bands(control, inverse, coupling)
    from_north, from_south = send_edges(north, south)

    routed = route(live_rows, obs_values, obs_tile, obs_points, obs_weights, jacobian, error_weight)
    rows = lax.all_to_all(routed, ("lat", "lon"), split_axis=0, concat_axis=0, tiled=True)

    state, cells = forward_diffusion(control, from_north, from_south, forward)
    gram = jnp.dot(jacobian * error_weight, jacobian.T, precision=EXACT)
    gram = jnp.repeat(jnp.repeat(gram, 8, axis=0), 8, axis=1)
    field, north, south = observe(
        rows.reshape(TILES, WORDS), cells.reshape(CELL_ROWS, LANES), gram, backward
    )
    edge_north, edge_south = send_edges(north, south)
    gradient = adjoint_diffusion(field, control, backward, from_north, from_south, coupling)

    head, tail = base_tables()
    tables = (jnp.asarray(head), jnp.asarray(tail))
    across_tables = (jnp.asarray(np.ascontiguousarray(head.T)), jnp.asarray(np.ascontiguousarray(tail.T)))
    turns = lax.dynamic_index_in_dim(jnp.asarray(turn_tables()), lon, 0, keepdims=False)
    chips = (ring + jnp.array([2, 1, 2, 3, 1, 3, 0, 0], jnp.int32)) % 4
    halves = jnp.array([0, 1, 1, 0, 0, 1, 0, 1], jnp.int32)
    order = jnp.concatenate([chips * 4 + 2 * (1 - core) + halves, chips * 4 + 2 * core + halves]).astype(jnp.int32)

    def analyse(base, gradient, add=None):
        return spectra(base, order, gradient, edge_north, edge_south, mend, tables, turns, add)

    def swap(piece):
        return lax.ppermute(piece, "lon", partner)

    gradient, ahead = analyse(0, gradient)
    ahead = swap(ahead)
    gradient, behind = analyse(4, gradient)
    behind = swap(behind)
    gradient, to_next, to_prior = analyse(8, gradient, ahead)
    from_prior = lax.ppermute(to_next, "lon", onward)
    from_next = lax.ppermute(to_prior, "lon", back)
    gradient, sides, own = analyse(12, gradient, behind)
    last_prior = lax.ppermute(sides[0] + from_prior[0], "lon", onward)
    last_next = lax.ppermute(sides[1] + from_next[0], "lon", back)
    wavenumber = jnp.arange(KEEP, dtype=jnp.int32)
    factor = jnp.where(wavenumber == 0, 1.0, 2.0).astype(F32) * response / NLON
    spectrum = jnp.concatenate(
        [own[0] + last_prior + from_next[1], own[1] + from_prior[1] + last_next]
    ) * jnp.concatenate([factor, factor])

    from_prior = lax.ppermute(spectrum, "lon", onward)
    from_next = lax.ppermute(spectrum, "lon", back)
    direction = synthesis(6, order, across_tables, turns, [spectrum, swap(spectrum)])
    from_prior, from_next, direction = lax.optimization_barrier((from_prior, from_next, direction))
    far_a = lax.ppermute(from_prior[:64], "lon", onward)
    far_b = lax.ppermute(from_next[64:], "lon", back)
    direction = synthesis(3, order, across_tables, turns, [from_prior, swap(from_prior)], direction)
    direction = synthesis(4, order, across_tables, turns, [from_next, swap(from_next)], direction)
    far_a, far_b, direction = lax.optimization_barrier((far_a, far_b, direction))
    direction = synthesis(0, order, across_tables, turns, [far_a, far_b, swap(far_a), swap(far_b)], direction)
    return (state, gradient, direction)


def solution(mesh):
    return jax.shard_map(
        body,
        mesh=mesh,
        in_specs=(
            P(None, "lat", "lon"),
            P("lat", None, None, None),
            P(),
            P(),
            P(),
            P(),
            P(("lat", "lon"), None),
            P(("lat", "lon"), None),
            P(("lat", "lon"), None),
            P(("lat", "lon"), None),
            P(("lat", "lon")),
        ),
        out_specs=(P(None, "lat", "lon"), P(None, "lat", "lon"), P(None, "lat", "lon")),
        check_vma=False,
    )
```

time: 240 us -> 194 us (0.81); the launches traced: 236 us -> 194 us
  waiting for transfers between devices: 33.6 us -> 22 us
  local copies, waits for them, and re-layouts: 24.8 us -> 13.4 us
  other arithmetic: 10.3 us -> 0.56 us
  starting transfers between devices: 46.5 us -> 40.9 us
  Pallas kernels: 118 us -> 115 us
    ppermute x9 -> x11, waiting for transfers between devices: 24.3 us -> 13.2 us  [the longest x1 6.56 us: body(): from_prior = lax.ppermute(to_next, 'lon', onward)]
    concatenate x5 -> x0, local copies, waits for them, and re-layouts: 9.55 us -> none  [the longest x1 2.86 us: band_matrices(): jnp.concatenate([twice, c * step_first, c * first, pad, c * step_last, c...]
    unnamed x48 -> x50, local copies, waits for them, and re-layouts: 6.85 us -> 12.3 us
    mul x4 -> x1, other arithmetic: 5.39 us -> 0.05 us  [body(): jnp.concatenate([own[0] + last_prior + from_next[1], own[1] + from_prior[...]
    ppermute x9 -> x11, starting transfers between devices: 15 us -> 11.1 us  [the longest x7 4.9 us: swap(): return lax.ppermute(piece, 'lon', partner)]
    pallas_call x1, Pallas kernels: 56.1 us -> 53.1 us  [observe(): pl.pallas_call(observe_kernel, out_shape=(jax.ShapeDtypeStruct((CH, RLAT,...]
    add x6 -> x4, other arithmetic: 3.26 us -> 0.22 us  [the longest x1 0.12 us: body(): own[0] + last_prior + from_next[1]]
    transpose x3 -> x0, local copies, waits for them, and re-layouts: 3.02 us -> none  [the longest x1 1.69 us: make_tables(): return pl.pallas_call(table_kernel, out_shape=(jax.ShapeDtypeStruct((CLON...]
  transfers between devices with their start and end apart: 18 -> 20, of which waited for: 6 -> 5; matrix products, arithmetic and copies ran while one was open for 11% -> 1% of each run, Pallas kernels for 14% -> 24%
where the time goes in v2:
time: 194 us
  Pallas kernels  115 us (59%)
  starting transfers between devices  40.9 us (21%)
  waiting for transfers between devices  22 us (11%)
  local copies, waits for them, and re-layouts  13.4 us (7%)
    pallas_call x1, Pallas kernels, observe(): pl.pallas_call(observe_kernel, out_shape=(jax.ShapeDtypeStruct((CH, RLAT,...  53.1 us
    pallas_call x4, Pallas kernels, spectra(): pl.pallas_call(functools.partial(spectra_kernel, base, add is not None, o...  17.3 us
    pallas_call x4, Pallas kernels, synthesis(): pl.pallas_call(functools.partial(synthesis_kernel, place, before is not N...  13.3 us
    unnamed x50, local copies, waits for them, and re-layouts  12.3 us
    pallas_call x1, Pallas kernels, route(): pl.pallas_call(route_kernel, out_shape=jax.ShapeDtypeStruct((TILES, 1, WO...  9.43 us
    pallas_call x1, Pallas kernels, forward_diffusion(): pl.pallas_call(forward_kernel, grid=(4,), out_shape=(jax.ShapeDtypeStruct...  9.08 us
    all_to_all x1, starting transfers between devices, body(): lax.all_to_all(routed, ('lat', 'lon'), split_axis=0, concat_axis=0, tiled...  9.06 us
    ppermute x1, waiting for transfers between devices, body(): from_prior = lax.ppermute(spectrum, 'lon', onward)  8.73 us
  transfers between devices with their start and end apart: 20, of which 5 were waited for; matrix products, arithmetic and copies ran while one was open for 1% of the time, Pallas kernels for 24%

profile of v2, /device:TPU:5, one launch (start us, length us, event | category | flops | bytes accessed | tf_op | source)
XLA Modules:
  0.0 193.8 jit_solution(2961087427519486459)
XLA Ops:
  0.6 0.0 copy-start.22
  0.6 0.0 copy-start.23
  0.7 0.0 copy-start
  0.7 2.2 %copy-done = f32[16,64,900]{2,1,0:T(8,128)S(1)} copy-done((f32[16,64,900]{2,1,0:T(8,128)S(1)}, f32[16,64,900]{2,1,0:T(8,128)}, u32[]{:S(2)}) %copy-start) | copy-done | bytes 3686424
  2.9 1.0 copy-done.10
  3.9 0.7 copy-done.17
  4.6 7.8 %bands.1 = (f32[16,64,128]{2,1,0:T(8,128)S(1)}, f32[16,64,128]{2,1,0:T(8,128)S(1)}, f32[16,64,128]{2,1,0:T(8,128)S(1)}, f32[16,8,900]{2,1,0:T(8,128)}, f32[16,8,900]{2,1,0:T(8,128)}) custom-call(f32[16,64,900]{2,1,0:T(8,128)S(1)} %copy-done, f32[2,16,32,32]{3,2,1,0:T(8,128)S(1)} %copy-done.10, f32[16]{0:T(128)S(1)} %copy-done.17), custom_call_target="tpu_custom_call" | custom-call | tf_op jit(solution)/shard_map/bands/pallas_call | solution.py:141
  12.4 0.8 copy-done.11
  13.2 3.5 %collective-permute-start = (f32[16,8,900]{2,1,0:T(8,128)}, f32[16,8,900]{2,1,0:T(8,128)S(1)}, u32[]{:S(2)}, u32[]{:S(2)}) collective-permute-start(f32[16,8,900]{2,1,0:T(8,128)} %get-tuple-element.29), channel_id=1, source_target_pairs={{0,8},{8,16},{16,24},{24,32},{32,40},{40,48},{48,56},{56,64},{64,7... | collective-permute-start | bytes 1382408 | tf_op jit(solution)/shard_map/ppermute | solution.py:154
  16.7 4.2 %collective-permute-start.1 = (f32[16,8,900]{2,1,0:T(8,128)}, f32[16,8,900]{2,1,0:T(8,128)S(1)}, u32[]{:S(2)}, u32[]{:S(2)}) collective-permute-start(f32[16,8,900]{2,1,0:T(8,128)} %get-tuple-element.30), channel_id=1, source_target_pairs={{8,0},{16,8},{24,16},{32,24},{40,32},{48,40},{56,48},{64,56},{72,6... | collective-permute-start | bytes 1382408 | tf_op jit(solution)/shard_map/ppermute | solution.py:153
  20.9 0.1 copy.39
  21.0 0.1 multiply_bitcast_fusion
  21.1 0.1 pad.4
  21.2 0.1 pad_maximum_fusion.project_ref
  22.0 9.4 %route.1 = f32[128,1,1152]{2,1,0:T(1,128)} custom-call(s32[1]{0:T(128)S(6)} %copy.52.live_ref, f32[2048,128]{1,0:T(8,128)S(1)} %copy-done.9, s32[1,2048]{1,0:T(1,128)S(1)} %bitcast.36, s32[4,2048]{1,0:T(4,128)S(1)} %bitcast.34, f32[4,2048]{1,0:T(4,128)S(1)} %bitcast.35, f32[128,128]{1,0:T(8,128)S(1)} %pad_maximum_fusion.project_ref), custom_call_target="tpu_custom_call" | custom-call | tf_op jit(solution)/shard_map/route/pallas_call | solution.py:252
  31.4 9.1 %all-to-all-start = ((f32[128,1,1152]{2,1,0:T(1,128)}), f32[128,1,1152]{2,1,0:T(1,128)S(1)}, u32[]{:S(2)}, u32[]{:S(2)}) async-start(f32[128,1,1152]{2,1,0:T(1,128)} %route.1), calls=%async_computation | async-start | bytes 1179648 | tf_op jit(solution)/shard_map/all_to_all | solution.py:580
  40.5 0.3 fusion.5
  40.8 0.1 broadcast_bitcast_fusion.1
  40.9 0.1 copy.40
  40.9 0.7 dynamic-slice_bitcast_fusion.turn_ref
  41.7 0.1 copy.41.gram_ref
  41.8 0.0 copy-start.1
  41.8 2.2 %copy-done.1 = f32[16,64,900]{2,1,0:T(8,128)S(1)} copy-done((f32[16,64,900]{2,1,0:T(8,128)S(1)}, f32[16,64,900]{2,1,0:T(8,128)}, u32[]{:S(2)}) %copy-start.1) | copy-done | bytes 3686424
  44.0 1.0 copy-done.12
  45.1 9.1 %forward.1 = (f32[16,64,900]{2,1,0:T(8,128)}, f32[8,1024,128]{2,1,0:T(8,128)S(1)}) custom-call(f32[16,64,900]{2,1,0:T(8,128)S(1)} %copy-done.1, f32[16,8,900]{2,1,0:T(8,128)S(1)} %collective-permute-done.north_ref, f32[16,8,900]{2,1,0:T(8,128)S(1)} %collective-permute-done.1.south_ref, f32[16,64,128]{2,1,0:T(8,128)S(1)} %copy-done.12), custom_call_target="tpu_custom_call" | custom-call | tf_op jit(solution)/shard_map/forward/pallas_call | solution.py:180
  54.2 2.0 %copy-done.7 = f32[8,1024,128]{2,1,0:T(8,128)} copy-done((f32[8,1024,128]{2,1,0:T(8,128)}, f32[8,1024,128]{2,1,0:T(8,128)S(1)}, u32[]{:S(2)}) %copy-start.7) | copy-done | bytes 4194328
  56.2 53.1 %observe.1 = (f32[16,64,1024]{2,1,0:T(8,128)}, f32[16,2,900]{2,1,0:T(2,128)S(1)}, f32[16,2,900]{2,1,0:T(2,128)S(1)}) custom-call(f32[128,1152]{1,0:T(8,128)S(1)} %bitcast.33, f32[8192,128]{1,0:T(8,128)} %bitcast.32, f32[128,128]{1,0:T(8,128)S(1)} %copy.41.gram_ref, bf16[256,512]{1,0:T(8,128)(2,1)S(1)} %copy-done.13, ...), custom_call_target="tpu_custom_call" | custom-call | tf_op jit(solution)/shard_map/observe/pallas_call | solution.py:387
  109.3 3.3 %collective-permute-start.2 = (f32[16,2,900]{2,1,0:T(2,128)S(1)}, f32[16,2,900]{2,1,0:T(2,128)S(1)}, u32[]{:S(2)}, u32[]{:S(2)}) collective-permute-start(f32[16,2,900]{2,1,0:T(2,128)S(1)} %get-tuple-element.36), channel_id=1, source_target_pairs={{0,8},{8,16},{16,24},{24,32},{32,40},{40,48},{48,56},{56,64},{64,7... | collective-permute-start | bytes 345608 | tf_op jit(solution)/shard_map/ppermute | solution.py:154
  112.7 4.0 %collective-permute-start.3 = (f32[16,2,900]{2,1,0:T(2,128)S(1)}, f32[16,2,900]{2,1,0:T(2,128)S(1)}, u32[]{:S(2)}, u32[]{:S(2)}) collective-permute-start(f32[16,2,900]{2,1,0:T(2,128)S(1)} %get-tuple-element.37), channel_id=1, source_target_pairs={{8,0},{16,8},{24,16},{32,24},{40,32},{48,40},{56,48},{64,56},{72,6... | collective-permute-start | bytes 345608 | tf_op jit(solution)/shard_map/ppermute | solution.py:153
  116.7 0.1 pad_add_fusion.order_ref
  116.8 2.2 %copy-done.8 = f32[16,64,1024]{2,1,0:T(8,128)S(1)} copy-done((f32[16,64,1024]{2,1,0:T(8,128)S(1)}, f32[16,64,1024]{2,1,0:T(8,128)}, u32[]{:S(2)}) %copy-start.8) | copy-done | bytes 4194328
  119.0 4.9 %adjoint.1.local_any = f32[16,64,900]{2,1,0:T(8,128)} custom-call(f32[16,64,1024]{2,1,0:T(8,128)S(1)} %copy-done.8, f32[16,64,900]{2,1,0:T(8,128)S(1)} %copy-done.2, f32[16,64,128]{2,1,0:T(8,128)S(1)} %get-tuple-element.34.matrix_ref, f32[16,8,900]{2,1,0:T(8,128)S(1)} %collective-permute-done.north_ref, f32[16,8,900]{2,1,0:T(8,128)S(1)} %collective-permute-done.1.south_ref, ...), custom_call_target="tpu_custom_call" | custom-call | flops 402653184 | bytes 12582912 | tf_op jit(solution)/shard_map/adjoint/pallas_call | solution.py:425
  123.9 4.0 %spectra.4 = (f32[16,64,900]{2,1,0:T(8,128)}, f32[4,64,1024]{2,1,0:T(8,128)S(1)}) custom-call(s32[16]{0:T(128)S(1)} %pad_add_fusion.order_ref, f32[16,64,900]{2,1,0:T(8,128)} %adjoint.1.local_any, f32[16,2,900]{2,1,0:T(2,128)S(1)} %collective-permute-done.2.north_ref, ...), custom_call_target="tpu_custom_call", output_to_operand_aliasing={{0}: (1, {})} | custom-call | flops 1610612736 | bytes 8388608 | tf_op jit(solution)/shard_map/spectra/pallas_call | solution.py:496
  127.9 0.8 collective-permute-start.4
  128.7 4.0 %spectra.5 = (f32[16,64,900]{2,1,0:T(8,128)}, f32[4,64,1024]{2,1,0:T(8,128)S(1)}) custom-call(s32[16]{0:T(128)S(1)} %pad_add_fusion.order_ref, f32[16,64,900]{2,1,0:T(8,128)} %get-tuple-element.39.local_any, f32[16,2,900]{2,1,0:T(2,128)S(1)} %collective-permute-done.2.north_ref, ...), custom_call_target="tpu_custom_call", output_to_operand_aliasing={{0}: (1, {})} | custom-call | flops 1610612736 | bytes 8388608 | tf_op jit(solution)/shard_map/spectra/pallas_call | solution.py:496
  132.6 0.1 collective-permute-start.5
  132.7 4.7 %spectra.6 = (f32[16,64,900]{2,1,0:T(8,128)}, f32[2,64,1024]{2,1,0:T(8,128)S(1)}, f32[2,64,1024]{2,1,0:T(8,128)S(1)}) custom-call(s32[16]{0:T(128)S(1)} %pad_add_fusion.order_ref, f32[16,64,900]{2,1,0:T(8,128)} %get-tuple-element.40.local_any, f32[16,2,900]{2,1,0:T(2,128)S(1)} %collective-permute-done.2.north_ref, ...), custom_call_target="tpu_custom_call", output_to_operand_aliasing={{0}: (1, {})} | custom-call | flops 1610612736 | bytes 8388608 | tf_op jit(solution)/shard_map/spectra/pallas_call | solution.py:496
  137.4 0.8 collective-permute-start.6
  138.3 2.3 %collective-permute-start.8 = (f32[2,64,1024]{2,1,0:T(8,128)S(1)}, f32[2,64,1024]{2,1,0:T(8,128)S(1)}, u32[]{:S(2)}, u32[]{:S(2)}) collective-permute-start(f32[2,64,1024]{2,1,0:T(8,128)S(1)} %get-tuple-element.48), channel_id=1, source_target_pairs={{0,6},{1,7},{2,0},{3,1},{4,2},{5,3},{6,4},{7,5},{8,14},{9,15},{10,... | collective-permute-start | bytes 1572872 | tf_op jit(solution)/shard_map/ppermute | solution.py:611
  140.6 4.7 %spectra.7 = (f32[16,64,900]{2,1,0:T(8,128)}, f32[2,64,1024]{2,1,0:T(8,128)S(1)}, f32[2,64,1024]{2,1,0:T(8,128)S(1)}) custom-call(s32[16]{0:T(128)S(1)} %pad_add_fusion.order_ref, f32[16,64,900]{2,1,0:T(8,128)} %get-tuple-element.42.local_any, f32[16,2,900]{2,1,0:T(2,128)S(1)} %collective-permute-done.2.north_ref, ...), custom_call_target="tpu_custom_call", output_to_operand_aliasing={{0}: (1, {})} | custom-call | flops 1610612736 | bytes 8388608 | tf_op jit(solution)/shard_map/spectra/pallas_call | solution.py:496
  145.2 0.0 copy-start.3
  145.2 0.0 copy-start.4
  145.3 6.6 %collective-permute-done.6 = f32[2,64,1024]{2,1,0:T(8,128)S(1)} collective-permute-done((f32[2,64,1024]{2,1,0:T(8,128)S(1)}, f32[2,64,1024]{2,1,0:T(8,128)S(1)}, u32[]{:S(2)}, u32[]{:S(2)}) %collective-permute-start.6) | collective-permute-done | bytes 524320 | tf_op jit(solution)/shard_map/ppermute | solution.py:610
  151.8 0.1 fusion.4
  151.9 0.9 collective-permute-start.7
  152.8 2.2 %collective-permute-start.9 = (f32[64,1024]{1,0:T(8,128)S(1)}, f32[64,1024]{1,0:T(8,128)S(1)}, u32[]{:S(2)}, u32[]{:S(2)}) collective-permute-start(f32[64,1024]{1,0:T(8,128)S(1)} %get-tuple-element.60), channel_id=1, source_target_pairs={{0,6},{1,7},{2,0},{3,1},{4,2},{5,3},{6,4},{7,5},{8,14},{9,15},{10,... | collective-permute-start | bytes 786440 | tf_op jit(solution)/shard_map/ppermute | solution.py:614
  155.0 5.2 %collective-permute-done.7 = f32[64,1024]{1,0:T(8,128)S(1)} collective-permute-done((f32[64,1024]{1,0:T(8,128)S(1)}, f32[64,1024]{1,0:T(8,128)S(1)}, u32[]{:S(2)}, u32[]{:S(2)}) %collective-permute-start.7) | collective-permute-done | bytes 262176 | tf_op jit(solution)/shard_map/ppermute | solution.py:613
  160.2 0.1 fusion.3
  160.4 2.0 %collective-permute-start.12 = (f32[128,1024]{1,0:T(8,128)S(1)}, f32[128,1024]{1,0:T(8,128)S(1)}, u32[]{:S(2)}, u32[]{:S(2)}) collective-permute-start(f32[128,1024]{1,0:T(8,128)S(1)} %maximum_multiply_fusion.refs_0_), channel_id=1, source_target_pairs={{0,1},{1,0},{2,3},{3,2},{4,5},{5,4},{6,7},{7,6},{8,9},{9,8},{10,11... | collective-permute-start | bytes 1572872 | tf_op jit(solution)/shard_map/ppermute | solution.py:603
  162.4 0.9 collective-permute-start.10
  163.3 1.9 collective-permute-start.11
  165.2 3.3 %synthesis.4.refs_0_ = f32[16,64,900]{2,1,0:T(8,128)} custom-call(s32[16]{0:T(128)S(1)} %pad_add_fusion.order_ref, bf16[1024,900]{1,0:T(8,128)(2,1)S(1)} %copy-done.3, bf16[1024,900]{1,0:T(8,128)(2,1)S(1)} %copy-done.4, f32[8,512]{1,0:T(8,128)S(1)} %dynamic-slice_bitcast_fusion.turn_ref, f32[128,1024]{1,0:T(8,128)S(1)} %maximum_multiply_fusion.refs_0_, ...), custom_call_target="tpu_custom_call" | custom-call | flops 1610612736 | bytes 8388608 | tf_op jit(solution)/shard_map/synthesis/pallas_call | solution.py:544
  168.5 8.7 %collective-permute-done.10.refs_1_ = f32[128,1024]{1,0:T(8,128)S(1)} collective-permute-done((f32[128,1024]{1,0:T(8,128)S(1)}, f32[128,1024]{1,0:T(8,128)S(1)}, u32[]{:S(2)}, u32[]{:S(2)}) %collective-permute-start.10) | collective-permute-done | bytes 524320 | tf_op jit(solution)/shard_map/ppermute | solution.py:621
  177.3 0.8 collective-permute-start.15
  178.1 0.0 collective-permute-start.16
  178.1 1.1 collective-permute-start.13
  179.2 1.7 collective-permute-start.14
  181.0 3.3 %synthesis.5.refs_0_ = f32[16,64,900]{2,1,0:T(8,128)} custom-call(s32[16]{0:T(128)S(1)} %pad_add_fusion.order_ref, bf16[1024,900]{1,0:T(8,128)(2,1)S(1)} %copy-done.3, bf16[1024,900]{1,0:T(8,128)(2,1)S(1)} %copy-done.4, f32[8,512]{1,0:T(8,128)S(1)} %dynamic-slice_bitcast_fusion.turn_ref, ...), custom_call_target="tpu_custom_call", output_to_operand_aliasing={{}: (4, {})} | custom-call | flops 1610612736 | bytes 8388608 | tf_op jit(solution)/shard_map/synthesis/pallas_call | solution.py:544
  184.3 3.3 %synthesis.6.refs_0_ = f32[16,64,900]{2,1,0:T(8,128)} custom-call(s32[16]{0:T(128)S(1)} %pad_add_fusion.order_ref, bf16[1024,900]{1,0:T(8,128)(2,1)S(1)} %copy-done.3, bf16[1024,900]{1,0:T(8,128)(2,1)S(1)} %copy-done.4, f32[8,512]{1,0:T(8,128)S(1)} %dynamic-slice_bitcast_fusion.turn_ref, ...), custom_call_target="tpu_custom_call", output_to_operand_aliasing={{}: (4, {})} | custom-call | flops 1610612736 | bytes 8388608 | tf_op jit(solution)/shard_map/synthesis/pallas_call | solution.py:544
  187.7 1.1 collective-permute-start.17
  188.7 0.1 collective-permute-start.18
  188.8 1.1 collective-permute-done.17.refs_3_
  189.9 0.4 collective-permute-done.18.refs_4_
  190.3 3.3 %synthesis.7 = f32[16,64,900]{2,1,0:T(8,128)} custom-call(s32[16]{0:T(128)S(1)} %pad_add_fusion.order_ref, bf16[1024,900]{1,0:T(8,128)(2,1)S(1)} %copy-done.3, bf16[1024,900]{1,0:T(8,128)(2,1)S(1)} %copy-done.4, f32[8,512]{1,0:T(8,128)S(1)} %dynamic-slice_bitcast_fusion.turn_ref, f32[16,64,900]{2,1,0:T(8,128)} %synthesis.6.refs_0_, ...), custom_call_target="tpu_custom_call", output_to_operand_aliasing={{}: (4, {})} | custom-call | flops 1610612736 | bytes 8388608 | tf_op jit(solution)/shard_map/synthesis/pallas_call | solution.py:544
  (58 shorter events, 0.3 us)
Async XLA Ops:
  0.6 41.1 %copy-start.22 = (s32[8]{0:T(128)S(1)}, s32[8]{0:T(128)}, u32[]{:S(2)}) copy-start(s32[8]{0:T(128)} %constant.83.clone) | copy-start | bytes 100
  0.6 41.1 %copy-start.23 = (s32[8]{0:T(128)S(1)}, s32[8]{0:T(128)}, u32[]{:S(2)}) copy-start(s32[8]{0:T(128)} %constant.82.clone) | copy-start | bytes 100
  0.7 2.2 %copy-start = (f32[16,64,900]{2,1,0:T(8,128)S(1)}, f32[16,64,900]{2,1,0:T(8,128)}, u32[]{:S(2)}) copy-start(f32[16,64,900]{2,1,0:T(8,128)} %control_ref.1) | copy-start | bytes 11059204
  2.9 1.0 copy-start.10
  3.9 0.7 copy-start.17
  4.6 16.4 %copy-start.19 = (f32[16,128]{1,0:T(8,128)S(1)}, f32[16,128]{1,0:T(8,128)}, u32[]{:S(2)}) copy-start(f32[16,128]{1,0:T(8,128)} %param.22) | copy-start | bytes 24580
  4.6 16.5 %copy-start.20 = (f32[128]{0:T(128)S(1)}, f32[128]{0:T(128)}, u32[]{:S(2)}) copy-start(f32[128]{0:T(128)} %param.23) | copy-start | bytes 1540
  4.6 17.4 %copy-start.9 = (f32[2048,128]{1,0:T(8,128)S(1)}, f32[2048,128]{1,0:T(8,128)}, u32[]{:S(2)}) copy-start(f32[2048,128]{1,0:T(8,128)} %values_ref.1) | copy-start | bytes 3145732
  4.6 17.4 %copy-start.14 = (s32[2048,4]{0,1:T(4,128)S(1)}, s32[2048,4]{0,1:T(4,128)}, u32[]{:S(2)}) copy-start(s32[2048,4]{0,1:T(4,128)} %param.27) | copy-start | bytes 98308
  4.6 17.4 %copy-start.15 = (f32[2048,4]{0,1:T(4,128)S(1)}, f32[2048,4]{0,1:T(4,128)}, u32[]{:S(2)}) copy-start(f32[2048,4]{0,1:T(4,128)} %param.28) | copy-start | bytes 98308
  4.6 17.4 %copy-start.16 = (s32[2048,1]{0,1:T(1,128)S(1)}, s32[2048,1]{0,1:T(1,128)}, u32[]{:S(2)}) copy-start(s32[2048,1]{0,1:T(1,128)} %param.26) | copy-start | bytes 24580
  12.4 0.8 copy-start.11
  13.2 28.6 %collective-permute-start = (f32[16,8,900]{2,1,0:T(8,128)}, f32[16,8,900]{2,1,0:T(8,128)S(1)}, u32[]{:S(2)}, u32[]{:S(2)}) collective-permute-start(f32[16,8,900]{2,1,0:T(8,128)} %get-tuple-element.29), channel_id=1, source_target_pairs={{0,8},{8,16},{16,24},{24,32},{32,40},{40,48},{48,56},{56,64},{64,7... | collective-permute-start | bytes 1382408 | tf_op jit(solution)/shard_map/ppermute | solution.py:154
  16.7 25.1 %collective-permute-start.1 = (f32[16,8,900]{2,1,0:T(8,128)}, f32[16,8,900]{2,1,0:T(8,128)S(1)}, u32[]{:S(2)}, u32[]{:S(2)}) collective-permute-start(f32[16,8,900]{2,1,0:T(8,128)} %get-tuple-element.30), channel_id=1, source_target_pairs={{8,0},{16,8},{24,16},{32,24},{40,32},{48,40},{56,48},{64,56},{72,6... | collective-permute-start | bytes 1382408 | tf_op jit(solution)/shard_map/ppermute | solution.py:153
  31.4 24.8 %copy-start.13 = (bf16[256,512]{1,0:T(8,128)(2,1)S(1)}, bf16[256,512]{1,0:T(8,128)(2,1)}, u32[]{:S(2)}) copy-start(bf16[256,512]{1,0:T(8,128)(2,1)} %constant.76.clone.pick_ref) | copy-start | bytes 786436
  31.4 24.7 %all-to-all-start = ((f32[128,1,1152]{2,1,0:T(1,128)}), f32[128,1,1152]{2,1,0:T(1,128)S(1)}, u32[]{:S(2)}, u32[]{:S(2)}) async-start(f32[128,1,1152]{2,1,0:T(1,128)} %route.1), calls=%async_computation | async-start | bytes 1179648 | tf_op jit(solution)/shard_map/all_to_all | solution.py:580
  41.8 2.2 %copy-start.1 = (f32[16,64,900]{2,1,0:T(8,128)S(1)}, f32[16,64,900]{2,1,0:T(8,128)}, u32[]{:S(2)}) copy-start(f32[16,64,900]{2,1,0:T(8,128)} %control_ref.1) | copy-start | bytes 11059204
  44.0 1.0 copy-start.12
  54.2 2.0 %copy-start.7 = (f32[8,1024,128]{2,1,0:T(8,128)}, f32[8,1024,128]{2,1,0:T(8,128)S(1)}, u32[]{:S(2)}) copy-start(f32[8,1024,128]{2,1,0:T(8,128)S(1)} %get-tuple-element.33) | copy-start | bytes 12582916
  56.2 60.6 %copy-start.18 = (f32[16]{0:T(128)S(1)}, f32[16]{0:T(128)}, u32[]{:S(2)}) copy-start(f32[16]{0:T(128)} %coupling_ref.3) | copy-start | bytes 196
  56.2 60.6 %copy-start.2 = (f32[16,64,900]{2,1,0:T(8,128)S(1)}, f32[16,64,900]{2,1,0:T(8,128)}, u32[]{:S(2)}) copy-start(f32[16,64,900]{2,1,0:T(8,128)} %control_ref.1) | copy-start | bytes 11059204
  109.3 14.6 %collective-permute-start.2 = (f32[16,2,900]{2,1,0:T(2,128)S(1)}, f32[16,2,900]{2,1,0:T(2,128)S(1)}, u32[]{:S(2)}, u32[]{:S(2)}) collective-permute-start(f32[16,2,900]{2,1,0:T(2,128)S(1)} %get-tuple-element.36), channel_id=1, source_target_pairs={{0,8},{8,16},{16,24},{24,32},{32,40},{40,48},{48,56},{56,64},{64,7... | collective-permute-start | bytes 345608 | tf_op jit(solution)/shard_map/ppermute | solution.py:154
  112.7 11.2 %collective-permute-start.3 = (f32[16,2,900]{2,1,0:T(2,128)S(1)}, f32[16,2,900]{2,1,0:T(2,128)S(1)}, u32[]{:S(2)}, u32[]{:S(2)}) collective-permute-start(f32[16,2,900]{2,1,0:T(2,128)S(1)} %get-tuple-element.37), channel_id=1, source_target_pairs={{8,0},{16,8},{24,16},{32,24},{40,32},{48,40},{56,48},{64,56},{72,6... | collective-permute-start | bytes 345608 | tf_op jit(solution)/shard_map/ppermute | solution.py:153
  116.8 2.2 %copy-start.8 = (f32[16,64,1024]{2,1,0:T(8,128)S(1)}, f32[16,64,1024]{2,1,0:T(8,128)}, u32[]{:S(2)}) copy-start(f32[16,64,1024]{2,1,0:T(8,128)} %get-tuple-element.35.field_ref) | copy-start | bytes 12582916
  119.0 4.9 %copy-start.5 = (bf16[900,1024]{1,0:T(8,128)(2,1)S(1)}, bf16[900,1024]{1,0:T(8,128)(2,1)}, u32[]{:S(2)}) copy-start(bf16[900,1024]{1,0:T(8,128)(2,1)} %constant.77.clone.head_ref) | copy-start | bytes 5529604
  119.0 4.9 %copy-start.6 = (bf16[900,1024]{1,0:T(8,128)(2,1)S(1)}, bf16[900,1024]{1,0:T(8,128)(2,1)}, u32[]{:S(2)}) copy-start(bf16[900,1024]{1,0:T(8,128)(2,1)} %constant.78.clone.tail_ref) | copy-start | bytes 5529604
  127.9 4.9 %collective-permute-start.4 = (f32[4,64,1024]{2,1,0:T(8,128)S(1)}, f32[4,64,1024]{2,1,0:T(8,128)S(1)}, u32[]{:S(2)}, u32[]{:S(2)}) collective-permute-start(f32[4,64,1024]{2,1,0:T(8,128)S(1)} %get-tuple-element.41), channel_id=1, source_target_pairs={{0,1},{1,0},{2,3},{3,2},{4,5},{5,4},{6,7},{7,6},{8,9},{9,8},{10,11... | collective-permute-start | bytes 3145736 | tf_op jit(solution)/shard_map/ppermute | solution.py:603
  132.6 7.9 %collective-permute-start.5 = (f32[4,64,1024]{2,1,0:T(8,128)S(1)}, f32[4,64,1024]{2,1,0:T(8,128)S(1)}, u32[]{:S(2)}, u32[]{:S(2)}) collective-permute-start(f32[4,64,1024]{2,1,0:T(8,128)S(1)} %get-tuple-element.43), channel_id=1, source_target_pairs={{0,1},{1,0},{2,3},{3,2},{4,5},{5,4},{6,7},{7,6},{8,9},{9,8},{10,11... | collective-permute-start | bytes 3145736 | tf_op jit(solution)/shard_map/ppermute | solution.py:603
  137.4 14.4 %collective-permute-start.6 = (f32[2,64,1024]{2,1,0:T(8,128)S(1)}, f32[2,64,1024]{2,1,0:T(8,128)S(1)}, u32[]{:S(2)}, u32[]{:S(2)}) collective-permute-start(f32[2,64,1024]{2,1,0:T(8,128)S(1)} %get-tuple-element.47), channel_id=1, source_target_pairs={{0,2},{1,3},{2,4},{3,5},{4,6},{5,7},{6,0},{7,1},{8,10},{9,11},{10,... | collective-permute-start | bytes 1572872 | tf_op jit(solution)/shard_map/ppermute | solution.py:610
  138.3 13.6 %collective-permute-start.8 = (f32[2,64,1024]{2,1,0:T(8,128)S(1)}, f32[2,64,1024]{2,1,0:T(8,128)S(1)}, u32[]{:S(2)}, u32[]{:S(2)}) collective-permute-start(f32[2,64,1024]{2,1,0:T(8,128)S(1)} %get-tuple-element.48), channel_id=1, source_target_pairs={{0,6},{1,7},{2,0},{3,1},{4,2},{5,3},{6,4},{7,5},{8,14},{9,15},{10,... | collective-permute-start | bytes 1572872 | tf_op jit(solution)/shard_map/ppermute | solution.py:611
  140.6 14.5 %copy-start.21 = (f32[512]{0:T(512)S(1)}, f32[512]{0:T(512)}, u32[]{:S(2)}) copy-start(f32[512]{0:T(512)} %param.24) | copy-start | bytes 6148
  145.2 20.0 %copy-start.3 = (bf16[1024,900]{1,0:T(8,128)(2,1)S(1)}, bf16[1024,900]{1,0:T(8,128)(2,1)}, u32[]{:S(2)}) copy-start(bf16[1024,900]{1,0:T(8,128)(2,1)} %constant.79.clone.head_ref) | copy-start | bytes 5529604
  145.2 20.0 %copy-start.4 = (bf16[1024,900]{1,0:T(8,128)(2,1)S(1)}, bf16[1024,900]{1,0:T(8,128)(2,1)}, u32[]{:S(2)}) copy-start(bf16[1024,900]{1,0:T(8,128)(2,1)} %constant.80.clone.tail_ref) | copy-start | bytes 5529604
  151.9 8.3 %collective-permute-start.7 = (f32[64,1024]{1,0:T(8,128)S(1)}, f32[64,1024]{1,0:T(8,128)S(1)}, u32[]{:S(2)}, u32[]{:S(2)}) collective-permute-start(f32[64,1024]{1,0:T(8,128)S(1)} %get-tuple-element.59), channel_id=1, source_target_pairs={{0,2},{1,3},{2,4},{3,5},{4,6},{5,7},{6,0},{7,1},{8,10},{9,11},{10,... | collective-permute-start | bytes 786440 | tf_op jit(solution)/shard_map/ppermute | solution.py:613
  152.8 7.4 %collective-permute-start.9 = (f32[64,1024]{1,0:T(8,128)S(1)}, f32[64,1024]{1,0:T(8,128)S(1)}, u32[]{:S(2)}, u32[]{:S(2)}) collective-permute-start(f32[64,1024]{1,0:T(8,128)S(1)} %get-tuple-element.60), channel_id=1, source_target_pairs={{0,6},{1,7},{2,0},{3,1},{4,2},{5,3},{6,4},{7,5},{8,14},{9,15},{10,... | collective-permute-start | bytes 786440 | tf_op jit(solution)/shard_map/ppermute | solution.py:614
  160.4 4.8 %collective-permute-start.12 = (f32[128,1024]{1,0:T(8,128)S(1)}, f32[128,1024]{1,0:T(8,128)S(1)}, u32[]{:S(2)}, u32[]{:S(2)}) collective-permute-start(f32[128,1024]{1,0:T(8,128)S(1)} %maximum_multiply_fusion.refs_0_), channel_id=1, source_target_pairs={{0,1},{1,0},{2,3},{3,2},{4,5},{5,4},{6,7},{7,6},{8,9},{9,8},{10,11... | collective-permute-start | bytes 1572872 | tf_op jit(solution)/shard_map/ppermute | solution.py:603
  162.4 14.8 %collective-permute-start.10 = (f32[128,1024]{1,0:T(8,128)S(1)}, f32[128,1024]{1,0:T(8,128)S(1)}, u32[]{:S(2)}, u32[]{:S(2)}) collective-permute-start(f32[128,1024]{1,0:T(8,128)S(1)} %maximum_multiply_fusion.refs_0_), channel_id=1, source_target_pairs={{0,2},{1,3},{2,4},{3,5},{4,6},{5,7},{6,0},{7,1},{8,10},{9,11},{10,... | collective-permute-start | bytes 1572872 | tf_op jit(solution)/shard_map/ppermute | solution.py:621
  163.3 14.0 %collective-permute-start.11 = (f32[128,1024]{1,0:T(8,128)S(1)}, f32[128,1024]{1,0:T(8,128)S(1)}, u32[]{:S(2)}, u32[]{:S(2)}) collective-permute-start(f32[128,1024]{1,0:T(8,128)S(1)} %maximum_multiply_fusion.refs_0_), channel_id=1, source_target_pairs={{0,6},{1,7},{2,0},{3,1},{4,2},{5,3},{6,4},{7,5},{8,14},{9,15},{10,... | collective-permute-start | bytes 1572872 | tf_op jit(solution)/shard_map/ppermute | solution.py:622
  177.3 3.7 %collective-permute-start.15 = (f32[128,1024]{1,0:T(8,128)S(1)}, f32[128,1024]{1,0:T(8,128)S(1)}, u32[]{:S(2)}, u32[]{:S(2)}) collective-permute-start(f32[128,1024]{1,0:T(8,128)S(1)} %collective-permute-done.10.refs_1_), channel_id=1, source_target_pairs={{0,1},{1,0},{2,3},{3,2},{4,5},{5,4},{6,7},{7,6},{8,9},{9,8},{10,11... | collective-permute-start | bytes 1572872 | tf_op jit(solution)/shard_map/ppermute | solution.py:603
  178.1 6.2 %collective-permute-start.16 = (f32[128,1024]{1,0:T(8,128)S(1)}, f32[128,1024]{1,0:T(8,128)S(1)}, u32[]{:S(2)}, u32[]{:S(2)}) collective-permute-start(f32[128,1024]{1,0:T(8,128)S(1)} %collective-permute-done.11.refs_1_), channel_id=1, source_target_pairs={{0,1},{1,0},{2,3},{3,2},{4,5},{5,4},{6,7},{7,6},{8,9},{9,8},{10,11... | collective-permute-start | bytes 1572872 | tf_op jit(solution)/shard_map/ppermute | solution.py:603
  178.1 9.5 %collective-permute-start.13 = (f32[64,1024]{1,0:T(8,128)S(1)}, f32[64,1024]{1,0:T(8,128)S(1)}, u32[]{:S(2)}, u32[]{:S(2)}) collective-permute-start(f32[64,1024]{1,0:T(8,128)S(1)} %slice.38), channel_id=1, source_target_pairs={{0,2},{1,3},{2,4},{3,5},{4,6},{5,7},{6,0},{7,1},{8,10},{9,11},{10,... | collective-permute-start | bytes 786440 | tf_op jit(solution)/shard_map/ppermute | solution.py:625
  179.2 8.4 %collective-permute-start.14 = (f32[64,1024]{1,0:T(8,128)S(1)}, f32[64,1024]{1,0:T(8,128)S(1)}, u32[]{:S(2)}, u32[]{:S(2)}) collective-permute-start(f32[64,1024]{1,0:T(8,128)S(1)} %slice.39), channel_id=1, source_target_pairs={{0,6},{1,7},{2,0},{3,1},{4,2},{5,3},{6,4},{7,5},{8,14},{9,15},{10,... | collective-permute-start | bytes 786440 | tf_op jit(solution)/shard_map/ppermute | solution.py:626
  187.7 2.2 %collective-permute-start.17 = (f32[64,1024]{1,0:T(8,128)S(1)}, f32[64,1024]{1,0:T(8,128)S(1)}, u32[]{:S(2)}, u32[]{:S(2)}) collective-permute-start(f32[64,1024]{1,0:T(8,128)S(1)} %collective-permute-done.13.refs_1_), channel_id=1, source_target_pairs={{0,1},{1,0},{2,3},{3,2},{4,5},{5,4},{6,7},{7,6},{8,9},{9,8},{10,11... | collective-permute-start | bytes 786440 | tf_op jit(solution)/shard_map/ppermute | solution.py:603
  188.7 1.5 collective-permute-start.18

commit v3 on v2

--- a/solution.py
+++ b/solution.py
@@ -75,20 +75,25 @@
         return lax.broadcasted_iota(jnp.int32, shape, axis)
 
     half = (HALF, LANES)
-    upper_place = (at(half, 1) == at(half, 0)).astype(F32)
-    lower_place = (at(half, 1) == at(half, 0) + HALF).astype(F32)
+    upper_place = (at(half, 1) == at(half, 0)).astype(F32).astype(BF16)
+    lower_place = (at(half, 1) == at(half, 0) + HALF).astype(F32).astype(BF16)
+
+    def put(block, place):
+        both = mm(jnp.concatenate(split(block), axis=0), place)
+        return both[:HALF] + both[HALF:]
+
     full = (RLAT, LANES)
     column, row = at(full, 1), at(full, 0)
     few = (16, RLAT)
     few_column, few_row = at(few, 1), at(few, 0)
     few_place = at((16, 1), 0)
     last_row = RLAT - 1
-    for channel in range(CH):
-        c = coupling_ref[channel]
+    for channel in range(4):
+        c = coupling_ref[pl.program_id(0) * 4 + channel]
         blocks = jnp.concatenate(
             [
-                jnp.dot(inverse_ref[0, channel], upper_place, precision=EXACT, preferred_element_type=F32),
-                jnp.dot(inverse_ref[1, channel], lower_place, precision=EXACT, preferred_element_type=F32),
+                put(inverse_ref[0, channel], upper_place),
+                put(inverse_ref[1, channel], lower_place),
             ],
             axis=0,
         )
@@ -104,7 +109,7 @@
             ],
             axis=1,
         )
-        product = jnp.dot(step[:, :RLAT], right, precision=EXACT, preferred_element_type=F32)
+        product = dot3(step[:, :RLAT], right)
         forward_ref[channel] = (
             product[:, :LANES]
             + jnp.where(column == 65, c * first, 0.0)
@@ -141,9 +146,16 @@
     return pl.pallas_call(
         bands_kernel,
         out_shape=(matrix, matrix, matrix, edge, edge),
-        in_specs=[VM, VM, SM],
-        out_specs=(VM,) * 5,
-        compiler_params=params(24),
+        grid=(4,),
+        in_specs=[
+            pl.BlockSpec((4, RLAT, CLON), lambda i: (i, 0, 0)),
+            pl.BlockSpec((2, 4, HALF, HALF), lambda i: (0, i, 0, 0)),
+            SM,
+        ],
+        out_specs=tuple(
+            pl.BlockSpec((4,) + shape, lambda i: (i, 0, 0)) for shape in ((RLAT, LANES),) * 3 + ((8, CLON),) * 2
+        ),
+        compiler_params=params(60),
         name="bands",
     )(control, inverse, coupling)
 
@@ -259,7 +271,7 @@
             pltpu.VMEM((ROWS, LANES), F32),
             pltpu.VMEM((ROWS, LANES), F32),
         ],
-        compiler_params=params(32),
+        compiler_params=params(20),
         name="route",
     )(live_rows, obs_values, obs_tile.T, obs_points.T, obs_weights.T, project)
 
@@ -285,11 +297,13 @@
     index_ref,
     where_ref,
     mask_ref,
-    columns_ref,
+    got_ref,
+    give_ref,
     values_ref,
     index_semaphore,
     *sums,
 ):
+    cells_ref = cells_ref.reshape(CELL_ROWS, LANES)
     index_ref[...] = rows_ref[:, :LANES].astype(jnp.int32)
     copy = pltpu.make_async_copy(index_ref, where_ref, index_semaphore)
     copy.start()
@@ -323,35 +337,37 @@
     def move(fetch, store):
         def source(step, carry):
             for slot in range(SLOTS):
+                if store is not None:
+                    cells = [where_ref[store * chunk + step, point * 32 + slot] for point in range(4)]
                 if fetch is not None:
-                    taken = fetch * chunk + step
-                    interp = None
-                    for point in range(4):
-                        cell = where_ref[taken, point * 32 + slot]
-                        term = cells_ref[pl.ds(cell, 1), :] * mask_ref[point, slot, pl.ds(taken, 1), :]
-                        interp = term if interp is None else interp + term
+                    taken = [
+                        cells_ref[pl.ds(where_ref[fetch * chunk + step, point * 32 + slot], 1), :]
+                        for point in range(4)
+                    ]
                 if store is not None:
-                    given = store * chunk + step
-                    column = columns_ref[slot, pl.ds(given, 1), :]
-                    cells = [where_ref[given, point * 32 + slot] for point in range(4)]
                     fresh = [
-                        sums[point][pl.ds(cells[point], 1), :] + mask_ref[point, slot, pl.ds(given, 1), :] * column
+                        sums[point][pl.ds(cells[point], 1), :] + give_ref[point, slot, pl.ds(step, 1), :]
                         for point in range(4)
                     ]
                     for point in range(4):
                         sums[point][pl.ds(cells[point], 1), :] = fresh[point]
                 if fetch is not None:
-                    columns_ref[slot, pl.ds(taken, 1), :] = interp
+                    for point in range(4):
+                        got_ref[point, slot, pl.ds(step, 1), :] = taken[point]
             return carry
 
         lax.fori_loop(0, chunk, source, 0)
 
     def weigh(index):
         rows = pl.ds(pl.multiple_of(index * chunk, chunk), chunk)
-        interp = columns_ref[:, rows, :].reshape(SLOTS * chunk, LANES)
+        masks = [mask_ref[point, :, rows, :].reshape(SLOTS * chunk, LANES) for point in range(4)]
+        got = [got_ref[point].reshape(SLOTS * chunk, LANES) for point in range(4)]
+        interp = masks[0] * got[0] + masks[1] * got[1] + masks[2] * got[2] + masks[3] * got[3]
         head, tail = split(interp)
         columns = mm(head, gram_head) + mm(jnp.concatenate([tail, head], axis=1), gram_both)
-        columns_ref[:, rows, :] = columns.reshape(SLOTS, chunk, LANES) + values_ref[:, rows, :]
+        columns = columns + values_ref[:, rows, :].reshape(SLOTS * chunk, LANES)
+        for point in range(4):
+            give_ref[point] = (masks[point] * columns).reshape(SLOTS, chunk, LANES)
 
     move(0, None)
     weigh(0)
@@ -393,12 +409,13 @@
             pltpu.VMEM((TILES, LANES), jnp.int32),
             pltpu.SMEM((TILES, LANES), jnp.int32),
             pltpu.VMEM((4, SLOTS, TILES, LANES), F32),
-            pltpu.VMEM((SLOTS, TILES, LANES), F32),
+            pltpu.VMEM((4, SLOTS, 16, LANES), F32),
+            pltpu.VMEM((4, SLOTS, 16, LANES), F32),
             pltpu.VMEM((SLOTS, TILES, LANES), F32),
             pltpu.SemaphoreType.DMA,
         ]
         + [pltpu.VMEM((CELL_ROWS, LANES), F32)] * ACCS,
-        compiler_params=params(52),
+        compiler_params=params(42),
         name="observe",
     )(rows, cells, gram, jnp.asarray(pick_table(), BF16), backward)
 
@@ -583,7 +600,7 @@
     gram = jnp.dot(jacobian * error_weight, jacobian.T, precision=EXACT)
     gram = jnp.repeat(jnp.repeat(gram, 8, axis=0), 8, axis=1)
     field, north, south = observe(
-        rows.reshape(TILES, WORDS), cells.reshape(CELL_ROWS, LANES), gram, backward
+        rows.reshape(TILES, WORDS), cells, gram, backward
     )
     edge_north, edge_south = send_edges(north, south)
     gradient = adjoint_diffusion(field, control, backward, from_north, from_south, coupling)

time: 194 us -> 180 us (0.928)
  Pallas kernels: 115 us -> 107 us
  local copies, waits for them, and re-layouts: 13.4 us -> 7.81 us
    pallas_call x1, Pallas kernels: 53.1 us -> 44.6 us  [observe(): pl.pallas_call(observe_kernel, out_shape=(jax.ShapeDtypeStruct((CH, RLAT,...]
    unnamed x50 -> x46, local copies, waits for them, and re-layouts: 12.3 us -> 6.75 us
  transfers between devices with their start and end apart: 20 -> 20, of which waited for: 5 -> 5; matrix products, arithmetic and copies ran while one was open for 1% -> 1% of each run, Pallas kernels for 24% -> 26%
where the time goes in v3:
time: 180 us; the launch traced here: 179 us
  Pallas kernels  107 us (59%)
  starting transfers between devices  40.5 us (22%)
  waiting for transfers between devices  21.9 us (12%)
  local copies, waits for them, and re-layouts  7.81 us (4%)
  between operations  1.93 us (1%)
    pallas_call x1, Pallas kernels, observe(): pl.pallas_call(observe_kernel, out_shape=(jax.ShapeDtypeStruct((CH, RLAT,...  44.6 us
    pallas_call x4, Pallas kernels, spectra(): pl.pallas_call(functools.partial(spectra_kernel, base, add is not None, o...  17.3 us
    pallas_call x4, Pallas kernels, synthesis(): pl.pallas_call(functools.partial(synthesis_kernel, place, before is not N...  13.3 us
    pallas_call x1, Pallas kernels, route(): pl.pallas_call(route_kernel, out_shape=jax.ShapeDtypeStruct((TILES, 1, WO...  9.43 us
    ppermute x2, starting transfers between devices, send_edges(): lax.ppermute(north, 'lat', [(i + 1, i) for i in range(count - 1)])  9.42 us
    all_to_all x1, starting transfers between devices, body(): lax.all_to_all(routed, ('lat', 'lon'), split_axis=0, concat_axis=0, tiled...  9.1 us
    pallas_call x1, Pallas kernels, forward_diffusion(): pl.pallas_call(forward_kernel, grid=(4,), out_shape=(jax.ShapeDtypeStruct...  9.08 us
    ppermute x1, waiting for transfers between devices, body(): from_prior = lax.ppermute(spectrum, 'lon', onward)  8.66 us
  transfers between devices with their start and end apart: 20, of which 5 were waited for; matrix products, arithmetic and copies ran while one was open for 1% of the time, Pallas kernels for 26%

profile of v3, /device:TPU:5, one launch (start us, length us, event | category | flops | bytes accessed | tf_op | source)
XLA Modules:
  0.0 179.4 jit_solution(2139046619534245732)
XLA Ops:
  0.6 0.0 copy-start.20
  0.6 0.0 copy-start.21
  0.7 7.9 %bands.1 = (f32[16,64,128]{2,1,0:T(8,128)}, f32[16,64,128]{2,1,0:T(8,128)}, f32[16,64,128]{2,1,0:T(8,128)}, f32[16,8,900]{2,1,0:T(8,128)}, f32[16,8,900]{2,1,0:T(8,128)}) custom-call(f32[16,64,900]{2,1,0:T(8,128)} %control_ref.1, f32[2,16,32,32]{3,2,1,0:T(8,128)} %inverse_ref.1, f32[16]{0:T(128)} %coupling_ref.3), custom_call_target="tpu_custom_call" | custom-call | tf_op jit(solution)/shard_map/bands/pallas_call | solution.py:146
  8.7 3.7 %collective-permute-start = (f32[16,8,900]{2,1,0:T(8,128)}, f32[16,8,900]{2,1,0:T(8,128)S(1)}, u32[]{:S(2)}, u32[]{:S(2)}) collective-permute-start(f32[16,8,900]{2,1,0:T(8,128)} %get-tuple-element.29), channel_id=1, source_target_pairs={{0,8},{8,16},{16,24},{24,32},{32,40},{40,48},{48,56},{56,64},{64,7... | collective-permute-start | bytes 1382408 | tf_op jit(solution)/shard_map/ppermute | solution.py:166
  12.3 4.0 %collective-permute-start.1 = (f32[16,8,900]{2,1,0:T(8,128)}, f32[16,8,900]{2,1,0:T(8,128)S(1)}, u32[]{:S(2)}, u32[]{:S(2)}) collective-permute-start(f32[16,8,900]{2,1,0:T(8,128)} %get-tuple-element.30), channel_id=1, source_target_pairs={{8,0},{16,8},{24,16},{32,24},{40,32},{48,40},{56,48},{64,56},{72,6... | collective-permute-start | bytes 1382408 | tf_op jit(solution)/shard_map/ppermute | solution.py:165
  16.4 0.1 copy.39
  16.5 0.1 multiply_bitcast_fusion
  16.6 0.1 pad.4
  16.6 0.1 pad_maximum_fusion.project_ref
  17.5 9.4 %route.1 = f32[128,1,1152]{2,1,0:T(1,128)} custom-call(s32[1]{0:T(128)S(6)} %copy.52.live_ref, f32[2048,128]{1,0:T(8,128)S(1)} %copy-done.10, s32[1,2048]{1,0:T(1,128)S(1)} %bitcast.34, s32[4,2048]{1,0:T(4,128)S(1)} %bitcast.32, f32[4,2048]{1,0:T(4,128)S(1)} %bitcast.33, f32[128,128]{1,0:T(8,128)S(1)} %pad_maximum_fusion.project_ref), custom_call_target="tpu_custom_call" | custom-call | tf_op jit(solution)/shard_map/route/pallas_call | solution.py:264
  26.9 9.1 %all-to-all-start = ((f32[128,1,1152]{2,1,0:T(1,128)}), f32[128,1,1152]{2,1,0:T(1,128)S(1)}, u32[]{:S(2)}, u32[]{:S(2)}) async-start(f32[128,1,1152]{2,1,0:T(1,128)} %route.1), calls=%async_computation | async-start | bytes 1179648 | tf_op jit(solution)/shard_map/all_to_all | solution.py:597
  36.0 0.3 fusion.5
  36.3 0.1 broadcast_bitcast_fusion.1
  36.3 0.1 copy.40
  36.4 0.7 dynamic-slice_bitcast_fusion.turn_ref
  37.1 0.1 copy.41.gram_ref
  37.3 0.0 collective-permute-done.north_ref
  37.3 0.0 copy-start
  37.3 2.2 %copy-done = f32[16,64,900]{2,1,0:T(8,128)S(1)} copy-done((f32[16,64,900]{2,1,0:T(8,128)S(1)}, f32[16,64,900]{2,1,0:T(8,128)}, u32[]{:S(2)}) %copy-start) | copy-done | bytes 3686424
  39.5 9.1 %forward.1 = (f32[16,64,900]{2,1,0:T(8,128)}, f32[8,1024,128]{2,1,0:T(8,128)S(1)}) custom-call(f32[16,64,900]{2,1,0:T(8,128)S(1)} %copy-done, f32[16,8,900]{2,1,0:T(8,128)S(1)} %collective-permute-done.north_ref, f32[16,8,900]{2,1,0:T(8,128)S(1)} %collective-permute-done.1.south_ref, f32[16,64,128]{2,1,0:T(8,128)S(1)} %copy-done.11), custom_call_target="tpu_custom_call" | custom-call | tf_op jit(solution)/shard_map/forward/pallas_call | solution.py:192
  48.6 2.0 %copy-done.7 = f32[8,1024,128]{2,1,0:T(8,128)} copy-done((f32[8,1024,128]{2,1,0:T(8,128)}, f32[8,1024,128]{2,1,0:T(8,128)S(1)}, u32[]{:S(2)}) %copy-start.7) | copy-done | bytes 4194328
  50.6 0.0 all-to-all-done
  50.7 0.0 copy-start.8
  50.7 2.3 %copy-done.8 = f32[8,1024,128]{2,1,0:T(8,128)S(1)} copy-done((f32[8,1024,128]{2,1,0:T(8,128)S(1)}, f32[8,1024,128]{2,1,0:T(8,128)}, u32[]{:S(2)}) %copy-start.8) | copy-done | bytes 4194328
  53.0 44.6 %observe.1 = (f32[16,64,1024]{2,1,0:T(8,128)S(1)}, f32[16,2,900]{2,1,0:T(2,128)S(1)}, f32[16,2,900]{2,1,0:T(2,128)S(1)}) custom-call(f32[128,1152]{1,0:T(8,128)S(1)} %bitcast.31, f32[8,1024,128]{2,1,0:T(8,128)S(1)} %copy-done.8, f32[128,128]{1,0:T(8,128)S(1)} %copy.41.gram_ref, bf16[256,512]{1,0:T(8,128)(2,1)S(1)} %copy-done.12, f32[16,64,128]{2,1,0:T(8,128)S(1)} %copy-done.9), custom_call_target="tpu_custom_call" | custom-call | tf_op jit(solution)/shard_map/observe/pallas_call | solution.py:403
  97.6 2.0 %collective-permute-start.2 = (f32[16,2,900]{2,1,0:T(2,128)S(1)}, f32[16,2,900]{2,1,0:T(2,128)S(1)}, u32[]{:S(2)}, u32[]{:S(2)}) collective-permute-start(f32[16,2,900]{2,1,0:T(2,128)S(1)} %get-tuple-element.36), channel_id=1, source_target_pairs={{0,8},{8,16},{16,24},{24,32},{32,40},{40,48},{48,56},{56,64},{64,7... | collective-permute-start | bytes 345608 | tf_op jit(solution)/shard_map/ppermute | solution.py:166
  99.6 5.4 %collective-permute-start.3 = (f32[16,2,900]{2,1,0:T(2,128)S(1)}, f32[16,2,900]{2,1,0:T(2,128)S(1)}, u32[]{:S(2)}, u32[]{:S(2)}) collective-permute-start(f32[16,2,900]{2,1,0:T(2,128)S(1)} %get-tuple-element.37), channel_id=1, source_target_pairs={{8,0},{16,8},{24,16},{32,24},{40,32},{48,40},{56,48},{64,56},{72,6... | collective-permute-start | bytes 345608 | tf_op jit(solution)/shard_map/ppermute | solution.py:165
  105.0 0.1 pad_add_fusion.order_ref
  105.1 4.9 %adjoint.1.local_any = f32[16,64,900]{2,1,0:T(8,128)} custom-call(f32[16,64,1024]{2,1,0:T(8,128)S(1)} %get-tuple-element.35.field_ref, f32[16,64,900]{2,1,0:T(8,128)S(1)} %copy-done.1, f32[16,64,128]{2,1,0:T(8,128)S(1)} %copy-done.9, f32[16,8,900]{2,1,0:T(8,128)S(1)} %collective-permute-done.north_ref, f32[16,8,900]{2,1,0:T(8,128)S(1)} %collective-permute-done.1.south_ref, ...), custom_call_target="tpu_custom_call" | custom-call | flops 402653184 | bytes 12582912 | tf_op jit(solution)/shard_map/adjoint/pallas_call | solution.py:442
  110.0 0.0 collective-permute-done.2.north_ref
  110.0 4.0 %spectra.4 = (f32[16,64,900]{2,1,0:T(8,128)}, f32[4,64,1024]{2,1,0:T(8,128)S(1)}) custom-call(s32[16]{0:T(128)S(1)} %pad_add_fusion.order_ref, f32[16,64,900]{2,1,0:T(8,128)} %adjoint.1.local_any, f32[16,2,900]{2,1,0:T(2,128)S(1)} %collective-permute-done.2.north_ref, ...), custom_call_target="tpu_custom_call", output_to_operand_aliasing={{0}: (1, {})} | custom-call | flops 1610612736 | bytes 8388608 | tf_op jit(solution)/shard_map/spectra/pallas_call | solution.py:513
  114.0 0.7 collective-permute-start.4
  114.7 4.0 %spectra.5 = (f32[16,64,900]{2,1,0:T(8,128)}, f32[4,64,1024]{2,1,0:T(8,128)S(1)}) custom-call(s32[16]{0:T(128)S(1)} %pad_add_fusion.order_ref, f32[16,64,900]{2,1,0:T(8,128)} %get-tuple-element.39.local_any, f32[16,2,900]{2,1,0:T(2,128)S(1)} %collective-permute-done.2.north_ref, ...), custom_call_target="tpu_custom_call", output_to_operand_aliasing={{0}: (1, {})} | custom-call | flops 1610612736 | bytes 8388608 | tf_op jit(solution)/shard_map/spectra/pallas_call | solution.py:513
  118.7 0.1 collective-permute-start.5
  118.8 4.7 %spectra.6 = (f32[16,64,900]{2,1,0:T(8,128)}, f32[2,64,1024]{2,1,0:T(8,128)S(1)}, f32[2,64,1024]{2,1,0:T(8,128)S(1)}) custom-call(s32[16]{0:T(128)S(1)} %pad_add_fusion.order_ref, f32[16,64,900]{2,1,0:T(8,128)} %get-tuple-element.40.local_any, f32[16,2,900]{2,1,0:T(2,128)S(1)} %collective-permute-done.2.north_ref, ...), custom_call_target="tpu_custom_call", output_to_operand_aliasing={{0}: (1, {})} | custom-call | flops 1610612736 | bytes 8388608 | tf_op jit(solution)/shard_map/spectra/pallas_call | solution.py:513
  123.5 0.8 collective-permute-start.6
  124.3 2.1 %collective-permute-start.8 = (f32[2,64,1024]{2,1,0:T(8,128)S(1)}, f32[2,64,1024]{2,1,0:T(8,128)S(1)}, u32[]{:S(2)}, u32[]{:S(2)}) collective-permute-start(f32[2,64,1024]{2,1,0:T(8,128)S(1)} %get-tuple-element.48), channel_id=1, source_target_pairs={{0,6},{1,7},{2,0},{3,1},{4,2},{5,3},{6,4},{7,5},{8,14},{9,15},{10,... | collective-permute-start | bytes 1572872 | tf_op jit(solution)/shard_map/ppermute | solution.py:628
  126.4 0.0 collective-permute-done.5.refs_0_
  126.4 4.7 %spectra.7 = (f32[16,64,900]{2,1,0:T(8,128)}, f32[2,64,1024]{2,1,0:T(8,128)S(1)}, f32[2,64,1024]{2,1,0:T(8,128)S(1)}) custom-call(s32[16]{0:T(128)S(1)} %pad_add_fusion.order_ref, f32[16,64,900]{2,1,0:T(8,128)} %get-tuple-element.42.local_any, f32[16,2,900]{2,1,0:T(2,128)S(1)} %collective-permute-done.2.north_ref, ...), custom_call_target="tpu_custom_call", output_to_operand_aliasing={{0}: (1, {})} | custom-call | flops 1610612736 | bytes 8388608 | tf_op jit(solution)/shard_map/spectra/pallas_call | solution.py:513
  131.0 0.0 copy-start.2
  131.0 0.0 copy-start.3
  131.1 6.7 %collective-permute-done.6 = f32[2,64,1024]{2,1,0:T(8,128)S(1)} collective-permute-done((f32[2,64,1024]{2,1,0:T(8,128)S(1)}, f32[2,64,1024]{2,1,0:T(8,128)S(1)}, u32[]{:S(2)}, u32[]{:S(2)}) %collective-permute-start.6) | collective-permute-done | bytes 524320 | tf_op jit(solution)/shard_map/ppermute | solution.py:627
  137.8 0.1 fusion.4
  137.9 0.7 collective-permute-start.7
  138.6 2.0 %collective-permute-start.9 = (f32[64,1024]{1,0:T(8,128)S(1)}, f32[64,1024]{1,0:T(8,128)S(1)}, u32[]{:S(2)}, u32[]{:S(2)}) collective-permute-start(f32[64,1024]{1,0:T(8,128)S(1)} %get-tuple-element.60), channel_id=1, source_target_pairs={{0,6},{1,7},{2,0},{3,1},{4,2},{5,3},{6,4},{7,5},{8,14},{9,15},{10,... | collective-permute-start | bytes 786440 | tf_op jit(solution)/shard_map/ppermute | solution.py:631
  140.6 5.0 %collective-permute-done.7 = f32[64,1024]{1,0:T(8,128)S(1)} collective-permute-done((f32[64,1024]{1,0:T(8,128)S(1)}, f32[64,1024]{1,0:T(8,128)S(1)}, u32[]{:S(2)}, u32[]{:S(2)}) %collective-permute-start.7) | collective-permute-done | bytes 262176 | tf_op jit(solution)/shard_map/ppermute | solution.py:630
  145.6 0.1 fusion.3
  145.8 2.3 %collective-permute-start.12 = (f32[128,1024]{1,0:T(8,128)S(1)}, f32[128,1024]{1,0:T(8,128)S(1)}, u32[]{:S(2)}, u32[]{:S(2)}) collective-permute-start(f32[128,1024]{1,0:T(8,128)S(1)} %maximum_multiply_fusion.refs_0_), channel_id=1, source_target_pairs={{0,1},{1,0},{2,3},{3,2},{4,5},{5,4},{6,7},{7,6},{8,9},{9,8},{10,11... | collective-permute-start | bytes 1572872 | tf_op jit(solution)/shard_map/ppermute | solution.py:620
  148.1 0.8 collective-permute-start.10
  148.9 1.9 %collective-permute-start.11 = (f32[128,1024]{1,0:T(8,128)S(1)}, f32[128,1024]{1,0:T(8,128)S(1)}, u32[]{:S(2)}, u32[]{:S(2)}) collective-permute-start(f32[128,1024]{1,0:T(8,128)S(1)} %maximum_multiply_fusion.refs_0_), channel_id=1, source_target_pairs={{0,6},{1,7},{2,0},{3,1},{4,2},{5,3},{6,4},{7,5},{8,14},{9,15},{10,... | collective-permute-start | bytes 1572872 | tf_op jit(solution)/shard_map/ppermute | solution.py:639
  150.8 0.0 collective-permute-done.12.refs_1_
  150.8 3.3 %synthesis.4.refs_0_ = f32[16,64,900]{2,1,0:T(8,128)} custom-call(s32[16]{0:T(128)S(1)} %pad_add_fusion.order_ref, bf16[1024,900]{1,0:T(8,128)(2,1)S(1)} %copy-done.2, bf16[1024,900]{1,0:T(8,128)(2,1)S(1)} %copy-done.3, f32[8,512]{1,0:T(8,128)S(1)} %dynamic-slice_bitcast_fusion.turn_ref, f32[128,1024]{1,0:T(8,128)S(1)} %maximum_multiply_fusion.refs_0_, ...), custom_call_target="tpu_custom_call" | custom-call | flops 1610612736 | bytes 8388608 | tf_op jit(solution)/shard_map/synthesis/pallas_call | solution.py:561
  154.2 8.7 %collective-permute-done.10.refs_1_ = f32[128,1024]{1,0:T(8,128)S(1)} collective-permute-done((f32[128,1024]{1,0:T(8,128)S(1)}, f32[128,1024]{1,0:T(8,128)S(1)}, u32[]{:S(2)}, u32[]{:S(2)}) %collective-permute-start.10) | collective-permute-done | bytes 524320 | tf_op jit(solution)/shard_map/ppermute | solution.py:638
  162.8 0.9 collective-permute-start.15
  163.7 0.0 collective-permute-start.16
  163.7 1.1 collective-permute-start.13
  164.8 1.8 collective-permute-start.14
  166.6 3.3 %synthesis.5.refs_0_ = f32[16,64,900]{2,1,0:T(8,128)} custom-call(s32[16]{0:T(128)S(1)} %pad_add_fusion.order_ref, bf16[1024,900]{1,0:T(8,128)(2,1)S(1)} %copy-done.2, bf16[1024,900]{1,0:T(8,128)(2,1)S(1)} %copy-done.3, f32[8,512]{1,0:T(8,128)S(1)} %dynamic-slice_bitcast_fusion.turn_ref, ...), custom_call_target="tpu_custom_call", output_to_operand_aliasing={{}: (4, {})} | custom-call | flops 1610612736 | bytes 8388608 | tf_op jit(solution)/shard_map/synthesis/pallas_call | solution.py:561
  169.9 3.3 %synthesis.6.refs_0_ = f32[16,64,900]{2,1,0:T(8,128)} custom-call(s32[16]{0:T(128)S(1)} %pad_add_fusion.order_ref, bf16[1024,900]{1,0:T(8,128)(2,1)S(1)} %copy-done.2, bf16[1024,900]{1,0:T(8,128)(2,1)S(1)} %copy-done.3, f32[8,512]{1,0:T(8,128)S(1)} %dynamic-slice_bitcast_fusion.turn_ref, ...), custom_call_target="tpu_custom_call", output_to_operand_aliasing={{}: (4, {})} | custom-call | flops 1610612736 | bytes 8388608 | tf_op jit(solution)/shard_map/synthesis/pallas_call | solution.py:561
  173.3 1.1 collective-permute-start.17
  174.3 0.1 collective-permute-start.18
  174.4 1.1 collective-permute-done.17.refs_3_
  175.5 0.4 collective-permute-done.18.refs_4_
  175.9 3.3 %synthesis.7 = f32[16,64,900]{2,1,0:T(8,128)} custom-call(s32[16]{0:T(128)S(1)} %pad_add_fusion.order_ref, bf16[1024,900]{1,0:T(8,128)(2,1)S(1)} %copy-done.2, bf16[1024,900]{1,0:T(8,128)(2,1)S(1)} %copy-done.3, f32[8,512]{1,0:T(8,128)S(1)} %dynamic-slice_bitcast_fusion.turn_ref, f32[16,64,900]{2,1,0:T(8,128)} %synthesis.6.refs_0_, ...), custom_call_target="tpu_custom_call", output_to_operand_aliasing={{}: (4, {})} | custom-call | flops 1610612736 | bytes 8388608 | tf_op jit(solution)/shard_map/synthesis/pallas_call | solution.py:561
  (54 shorter events, 0.3 us)
Async XLA Ops:
  0.6 36.6 %copy-start.20 = (s32[8]{0:T(128)S(1)}, s32[8]{0:T(128)}, u32[]{:S(2)}) copy-start(s32[8]{0:T(128)} %constant.83.clone) | copy-start | bytes 100
  0.6 36.6 %copy-start.21 = (s32[8]{0:T(128)S(1)}, s32[8]{0:T(128)}, u32[]{:S(2)}) copy-start(s32[8]{0:T(128)} %constant.82.clone) | copy-start | bytes 100
  0.7 15.7 %copy-start.17 = (f32[16,128]{1,0:T(8,128)S(1)}, f32[16,128]{1,0:T(8,128)}, u32[]{:S(2)}) copy-start(f32[16,128]{1,0:T(8,128)} %param.22) | copy-start | bytes 24580
  0.7 15.8 %copy-start.18 = (f32[128]{0:T(128)S(1)}, f32[128]{0:T(128)}, u32[]{:S(2)}) copy-start(f32[128]{0:T(128)} %param.23) | copy-start | bytes 1540
  0.7 16.7 %copy-start.15 = (s32[2048,1]{0,1:T(1,128)S(1)}, s32[2048,1]{0,1:T(1,128)}, u32[]{:S(2)}) copy-start(s32[2048,1]{0,1:T(1,128)} %param.26) | copy-start | bytes 24580
  0.7 16.7 %copy-start.13 = (s32[2048,4]{0,1:T(4,128)S(1)}, s32[2048,4]{0,1:T(4,128)}, u32[]{:S(2)}) copy-start(s32[2048,4]{0,1:T(4,128)} %param.27) | copy-start | bytes 98308
  0.7 16.7 %copy-start.14 = (f32[2048,4]{0,1:T(4,128)S(1)}, f32[2048,4]{0,1:T(4,128)}, u32[]{:S(2)}) copy-start(f32[2048,4]{0,1:T(4,128)} %param.28) | copy-start | bytes 98308
  0.7 16.7 %copy-start.10 = (f32[2048,128]{1,0:T(8,128)S(1)}, f32[2048,128]{1,0:T(8,128)}, u32[]{:S(2)}) copy-start(f32[2048,128]{1,0:T(8,128)} %values_ref.1) | copy-start | bytes 3145732
  8.7 28.7 %copy-start.11 = (f32[16,64,128]{2,1,0:T(8,128)S(1)}, f32[16,64,128]{2,1,0:T(8,128)}, u32[]{:S(2)}) copy-start(f32[16,64,128]{2,1,0:T(8,128)} %get-tuple-element.31.matrix_ref) | copy-start | bytes 1572868
  8.7 28.6 %collective-permute-start = (f32[16,8,900]{2,1,0:T(8,128)}, f32[16,8,900]{2,1,0:T(8,128)S(1)}, u32[]{:S(2)}, u32[]{:S(2)}) collective-permute-start(f32[16,8,900]{2,1,0:T(8,128)} %get-tuple-element.29), channel_id=1, source_target_pairs={{0,8},{8,16},{16,24},{24,32},{32,40},{40,48},{48,56},{56,64},{64,7... | collective-permute-start | bytes 1382408 | tf_op jit(solution)/shard_map/ppermute | solution.py:166
  12.3 25.0 %collective-permute-start.1 = (f32[16,8,900]{2,1,0:T(8,128)}, f32[16,8,900]{2,1,0:T(8,128)S(1)}, u32[]{:S(2)}, u32[]{:S(2)}) collective-permute-start(f32[16,8,900]{2,1,0:T(8,128)} %get-tuple-element.30), channel_id=1, source_target_pairs={{8,0},{16,8},{24,16},{32,24},{40,32},{48,40},{56,48},{64,56},{72,6... | collective-permute-start | bytes 1382408 | tf_op jit(solution)/shard_map/ppermute | solution.py:165
  26.9 23.8 %copy-start.9 = (f32[16,64,128]{2,1,0:T(8,128)S(1)}, f32[16,64,128]{2,1,0:T(8,128)}, u32[]{:S(2)}) copy-start(f32[16,64,128]{2,1,0:T(8,128)} %get-tuple-element.34.matrix_ref) | copy-start | bytes 1572868
  26.9 23.8 %copy-start.12 = (bf16[256,512]{1,0:T(8,128)(2,1)S(1)}, bf16[256,512]{1,0:T(8,128)(2,1)}, u32[]{:S(2)}) copy-start(bf16[256,512]{1,0:T(8,128)(2,1)} %constant.76.clone.pick_ref) | copy-start | bytes 786436
  26.9 23.7 %all-to-all-start = ((f32[128,1,1152]{2,1,0:T(1,128)}), f32[128,1,1152]{2,1,0:T(1,128)S(1)}, u32[]{:S(2)}, u32[]{:S(2)}) async-start(f32[128,1,1152]{2,1,0:T(1,128)} %route.1), calls=%async_computation | async-start | bytes 1179648 | tf_op jit(solution)/shard_map/all_to_all | solution.py:597
  37.3 2.2 %copy-start = (f32[16,64,900]{2,1,0:T(8,128)S(1)}, f32[16,64,900]{2,1,0:T(8,128)}, u32[]{:S(2)}) copy-start(f32[16,64,900]{2,1,0:T(8,128)} %control_ref.1) | copy-start | bytes 11059204
  39.5 65.6 %copy-start.16 = (f32[16]{0:T(128)S(1)}, f32[16]{0:T(128)}, u32[]{:S(2)}) copy-start(f32[16]{0:T(128)} %coupling_ref.3) | copy-start | bytes 196
  48.6 2.0 %copy-start.7 = (f32[8,1024,128]{2,1,0:T(8,128)}, f32[8,1024,128]{2,1,0:T(8,128)S(1)}, u32[]{:S(2)}) copy-start(f32[8,1024,128]{2,1,0:T(8,128)S(1)} %get-tuple-element.33.cells_ref) | copy-start | bytes 12582916
  50.6 54.5 %copy-start.1 = (f32[16,64,900]{2,1,0:T(8,128)S(1)}, f32[16,64,900]{2,1,0:T(8,128)}, u32[]{:S(2)}) copy-start(f32[16,64,900]{2,1,0:T(8,128)} %control_ref.1) | copy-start | bytes 11059204
  50.7 2.3 %copy-start.8 = (f32[8,1024,128]{2,1,0:T(8,128)S(1)}, f32[8,1024,128]{2,1,0:T(8,128)}, u32[]{:S(2)}) copy-start(f32[8,1024,128]{2,1,0:T(8,128)} %copy-done.7) | copy-start | bytes 12582916
  97.6 12.4 %collective-permute-start.2 = (f32[16,2,900]{2,1,0:T(2,128)S(1)}, f32[16,2,900]{2,1,0:T(2,128)S(1)}, u32[]{:S(2)}, u32[]{:S(2)}) collective-permute-start(f32[16,2,900]{2,1,0:T(2,128)S(1)} %get-tuple-element.36), channel_id=1, source_target_pairs={{0,8},{8,16},{16,24},{24,32},{32,40},{40,48},{48,56},{56,64},{64,7... | collective-permute-start | bytes 345608 | tf_op jit(solution)/shard_map/ppermute | solution.py:166
  99.6 10.4 %collective-permute-start.3 = (f32[16,2,900]{2,1,0:T(2,128)S(1)}, f32[16,2,900]{2,1,0:T(2,128)S(1)}, u32[]{:S(2)}, u32[]{:S(2)}) collective-permute-start(f32[16,2,900]{2,1,0:T(2,128)S(1)} %get-tuple-element.37), channel_id=1, source_target_pairs={{8,0},{16,8},{24,16},{32,24},{40,32},{48,40},{56,48},{64,56},{72,6... | collective-permute-start | bytes 345608 | tf_op jit(solution)/shard_map/ppermute | solution.py:165
  105.1 4.9 %copy-start.4 = (bf16[900,1024]{1,0:T(8,128)(2,1)S(1)}, bf16[900,1024]{1,0:T(8,128)(2,1)}, u32[]{:S(2)}) copy-start(bf16[900,1024]{1,0:T(8,128)(2,1)} %constant.77.clone.head_ref) | copy-start | bytes 5529604
  105.1 4.9 %copy-start.5 = (bf16[900,1024]{1,0:T(8,128)(2,1)S(1)}, bf16[900,1024]{1,0:T(8,128)(2,1)}, u32[]{:S(2)}) copy-start(bf16[900,1024]{1,0:T(8,128)(2,1)} %constant.78.clone.tail_ref) | copy-start | bytes 5529604
  105.1 4.9 %copy-start.6 = (f32[16,64,128]{2,1,0:T(8,128)S(1)}, f32[16,64,128]{2,1,0:T(8,128)}, u32[]{:S(2)}) copy-start(f32[16,64,128]{2,1,0:T(8,128)} %get-tuple-element.38.mend_ref) | copy-start | bytes 1572868
  114.0 4.8 %collective-permute-start.4 = (f32[4,64,1024]{2,1,0:T(8,128)S(1)}, f32[4,64,1024]{2,1,0:T(8,128)S(1)}, u32[]{:S(2)}, u32[]{:S(2)}) collective-permute-start(f32[4,64,1024]{2,1,0:T(8,128)S(1)} %get-tuple-element.41), channel_id=1, source_target_pairs={{0,1},{1,0},{2,3},{3,2},{4,5},{5,4},{6,7},{7,6},{8,9},{9,8},{10,11... | collective-permute-start | bytes 3145736 | tf_op jit(solution)/shard_map/ppermute | solution.py:620
  118.7 7.6 %collective-permute-start.5 = (f32[4,64,1024]{2,1,0:T(8,128)S(1)}, f32[4,64,1024]{2,1,0:T(8,128)S(1)}, u32[]{:S(2)}, u32[]{:S(2)}) collective-permute-start(f32[4,64,1024]{2,1,0:T(8,128)S(1)} %get-tuple-element.43), channel_id=1, source_target_pairs={{0,1},{1,0},{2,3},{3,2},{4,5},{5,4},{6,7},{7,6},{8,9},{9,8},{10,11... | collective-permute-start | bytes 3145736 | tf_op jit(solution)/shard_map/ppermute | solution.py:620
  123.5 14.3 %collective-permute-start.6 = (f32[2,64,1024]{2,1,0:T(8,128)S(1)}, f32[2,64,1024]{2,1,0:T(8,128)S(1)}, u32[]{:S(2)}, u32[]{:S(2)}) collective-permute-start(f32[2,64,1024]{2,1,0:T(8,128)S(1)} %get-tuple-element.47), channel_id=1, source_target_pairs={{0,2},{1,3},{2,4},{3,5},{4,6},{5,7},{6,0},{7,1},{8,10},{9,11},{10,... | collective-permute-start | bytes 1572872 | tf_op jit(solution)/shard_map/ppermute | solution.py:627
  124.3 13.5 %collective-permute-start.8 = (f32[2,64,1024]{2,1,0:T(8,128)S(1)}, f32[2,64,1024]{2,1,0:T(8,128)S(1)}, u32[]{:S(2)}, u32[]{:S(2)}) collective-permute-start(f32[2,64,1024]{2,1,0:T(8,128)S(1)} %get-tuple-element.48), channel_id=1, source_target_pairs={{0,6},{1,7},{2,0},{3,1},{4,2},{5,3},{6,4},{7,5},{8,14},{9,15},{10,... | collective-permute-start | bytes 1572872 | tf_op jit(solution)/shard_map/ppermute | solution.py:628
  126.4 14.3 %copy-start.19 = (f32[512]{0:T(512)S(1)}, f32[512]{0:T(512)}, u32[]{:S(2)}) copy-start(f32[512]{0:T(512)} %param.24) | copy-start | bytes 6148
  131.0 19.8 %copy-start.2 = (bf16[1024,900]{1,0:T(8,128)(2,1)S(1)}, bf16[1024,900]{1,0:T(8,128)(2,1)}, u32[]{:S(2)}) copy-start(bf16[1024,900]{1,0:T(8,128)(2,1)} %constant.79.clone.head_ref) | copy-start | bytes 5529604
  131.0 19.8 %copy-start.3 = (bf16[1024,900]{1,0:T(8,128)(2,1)S(1)}, bf16[1024,900]{1,0:T(8,128)(2,1)}, u32[]{:S(2)}) copy-start(bf16[1024,900]{1,0:T(8,128)(2,1)} %constant.80.clone.tail_ref) | copy-start | bytes 5529604
  137.9 7.7 %collective-permute-start.7 = (f32[64,1024]{1,0:T(8,128)S(1)}, f32[64,1024]{1,0:T(8,128)S(1)}, u32[]{:S(2)}, u32[]{:S(2)}) collective-permute-start(f32[64,1024]{1,0:T(8,128)S(1)} %get-tuple-element.59), channel_id=1, source_target_pairs={{0,2},{1,3},{2,4},{3,5},{4,6},{5,7},{6,0},{7,1},{8,10},{9,11},{10,... | collective-permute-start | bytes 786440 | tf_op jit(solution)/shard_map/ppermute | solution.py:630
  138.6 7.0 %collective-permute-start.9 = (f32[64,1024]{1,0:T(8,128)S(1)}, f32[64,1024]{1,0:T(8,128)S(1)}, u32[]{:S(2)}, u32[]{:S(2)}) collective-permute-start(f32[64,1024]{1,0:T(8,128)S(1)} %get-tuple-element.60), channel_id=1, source_target_pairs={{0,6},{1,7},{2,0},{3,1},{4,2},{5,3},{6,4},{7,5},{8,14},{9,15},{10,... | collective-permute-start | bytes 786440 | tf_op jit(solution)/shard_map/ppermute | solution.py:631
  145.8 5.0 %collective-permute-start.12 = (f32[128,1024]{1,0:T(8,128)S(1)}, f32[128,1024]{1,0:T(8,128)S(1)}, u32[]{:S(2)}, u32[]{:S(2)}) collective-permute-start(f32[128,1024]{1,0:T(8,128)S(1)} %maximum_multiply_fusion.refs_0_), channel_id=1, source_target_pairs={{0,1},{1,0},{2,3},{3,2},{4,5},{5,4},{6,7},{7,6},{8,9},{9,8},{10,11... | collective-permute-start | bytes 1572872 | tf_op jit(solution)/shard_map/ppermute | solution.py:620
  148.1 14.7 %collective-permute-start.10 = (f32[128,1024]{1,0:T(8,128)S(1)}, f32[128,1024]{1,0:T(8,128)S(1)}, u32[]{:S(2)}, u32[]{:S(2)}) collective-permute-start(f32[128,1024]{1,0:T(8,128)S(1)} %maximum_multiply_fusion.refs_0_), channel_id=1, source_target_pairs={{0,2},{1,3},{2,4},{3,5},{4,6},{5,7},{6,0},{7,1},{8,10},{9,11},{10,... | collective-permute-start | bytes 1572872 | tf_op jit(solution)/shard_map/ppermute | solution.py:638
  148.9 13.9 %collective-permute-start.11 = (f32[128,1024]{1,0:T(8,128)S(1)}, f32[128,1024]{1,0:T(8,128)S(1)}, u32[]{:S(2)}, u32[]{:S(2)}) collective-permute-start(f32[128,1024]{1,0:T(8,128)S(1)} %maximum_multiply_fusion.refs_0_), channel_id=1, source_target_pairs={{0,6},{1,7},{2,0},{3,1},{4,2},{5,3},{6,4},{7,5},{8,14},{9,15},{10,... | collective-permute-start | bytes 1572872 | tf_op jit(solution)/shard_map/ppermute | solution.py:639
  162.8 3.7 %collective-permute-start.15 = (f32[128,1024]{1,0:T(8,128)S(1)}, f32[128,1024]{1,0:T(8,128)S(1)}, u32[]{:S(2)}, u32[]{:S(2)}) collective-permute-start(f32[128,1024]{1,0:T(8,128)S(1)} %collective-permute-done.10.refs_1_), channel_id=1, source_target_pairs={{0,1},{1,0},{2,3},{3,2},{4,5},{5,4},{6,7},{7,6},{8,9},{9,8},{10,11... | collective-permute-start | bytes 1572872 | tf_op jit(solution)/shard_map/ppermute | solution.py:620
  163.7 6.2 %collective-permute-start.16 = (f32[128,1024]{1,0:T(8,128)S(1)}, f32[128,1024]{1,0:T(8,128)S(1)}, u32[]{:S(2)}, u32[]{:S(2)}) collective-permute-start(f32[128,1024]{1,0:T(8,128)S(1)} %collective-permute-done.11.refs_1_), channel_id=1, source_target_pairs={{0,1},{1,0},{2,3},{3,2},{4,5},{5,4},{6,7},{7,6},{8,9},{9,8},{10,11... | collective-permute-start | bytes 1572872 | tf_op jit(solution)/shard_map/ppermute | solution.py:620
  163.7 9.5 %collective-permute-start.13 = (f32[64,1024]{1,0:T(8,128)S(1)}, f32[64,1024]{1,0:T(8,128)S(1)}, u32[]{:S(2)}, u32[]{:S(2)}) collective-permute-start(f32[64,1024]{1,0:T(8,128)S(1)} %slice.38), channel_id=1, source_target_pairs={{0,2},{1,3},{2,4},{3,5},{4,6},{5,7},{6,0},{7,1},{8,10},{9,11},{10,... | collective-permute-start | bytes 786440 | tf_op jit(solution)/shard_map/ppermute | solution.py:642
  164.8 8.5 %collective-permute-start.14 = (f32[64,1024]{1,0:T(8,128)S(1)}, f32[64,1024]{1,0:T(8,128)S(1)}, u32[]{:S(2)}, u32[]{:S(2)}) collective-permute-start(f32[64,1024]{1,0:T(8,128)S(1)} %slice.39), channel_id=1, source_target_pairs={{0,6},{1,7},{2,0},{3,1},{4,2},{5,3},{6,4},{7,5},{8,14},{9,15},{10,... | collective-permute-start | bytes 786440 | tf_op jit(solution)/shard_map/ppermute | solution.py:643
  173.3 2.2 %collective-permute-start.17 = (f32[64,1024]{1,0:T(8,128)S(1)}, f32[64,1024]{1,0:T(8,128)S(1)}, u32[]{:S(2)}, u32[]{:S(2)}) collective-permute-start(f32[64,1024]{1,0:T(8,128)S(1)} %collective-permute-done.13.refs_1_), channel_id=1, source_target_pairs={{0,1},{1,0},{2,3},{3,2},{4,5},{5,4},{6,7},{7,6},{8,9},{9,8},{10,11... | collective-permute-start | bytes 786440 | tf_op jit(solution)/shard_map/ppermute | solution.py:620
  174.3 1.5 collective-permute-start.18

commit v4 on v3

--- a/solution.py
+++ b/solution.py
@@ -84,9 +84,7 @@
 
     full = (RLAT, LANES)
     column, row = at(full, 1), at(full, 0)
-    few = (16, RLAT)
-    few_column, few_row = at(few, 1), at(few, 0)
-    few_place = at((16, 1), 0)
+    few_place = at((8, 1), 0)
     last_row = RLAT - 1
     for channel in range(4):
         c = coupling_ref[pl.program_id(0) * 4 + channel]
@@ -125,19 +123,16 @@
             + jnp.where(column == 2, turned[:, last_row : last_row + 1], 0.0)
             + jnp.where((column == 3) & (row == last_row), 1.0, 0.0)
         )
-        edges = (
-            jnp.where((few_row == 0) & (few_column == 0), 1.0, 0.0)
-            + jnp.where(few_row == 1, step[0:1, :RLAT], 0.0)
-            + jnp.where((few_row == 8) & (few_column == last_row), 1.0, 0.0)
-            + jnp.where(few_row == 9, step[last_row : last_row + 1, :RLAT], 0.0)
-        )
-        rows = (
-            dot3(edges, field_ref[channel])
-            + jnp.where(few_place == 2, c * blocks[0:1, 0:1], 0.0)
-            + jnp.where(few_place == 10, c * blocks[last_row : last_row + 1, last_row : last_row + 1], 0.0)
-        )
-        north_ref[channel] = rows[:8]
-        south_ref[channel] = rows[8:]
+        field = field_ref[channel]
+        top = jnp.sum(turned[:, 0:1] * field, axis=0, keepdims=True)
+        bottom = jnp.sum(turned[:, last_row : last_row + 1] * field, axis=0, keepdims=True)
+        for out_ref, edge, mixed, corner in (
+            (north_ref, field[0:1], top, blocks[0:1, 0:1]),
+            (south_ref, field[last_row:], bottom, blocks[last_row:, last_row : last_row + 1]),
+        ):
+            out_ref[channel] = jnp.where(
+                few_place == 0, edge, jnp.where(few_place == 1, mixed, jnp.where(few_place == 2, c * corner, 0.0))
+            )
 
 
 def bands(control, inverse, coupling):
@@ -206,7 +201,7 @@
             pl.BlockSpec((CH, RLAT, width), lambda i: (0, 0, i)),
             pl.BlockSpec((8, width, LANES), lambda i: (0, i, 0)),
         ),
-        compiler_params=params(28),
+        compiler_params=params(60),
         name="forward",
     )(control, from_north, from_south, forward)
 
@@ -287,7 +282,7 @@
 
 def observe_kernel(
     rows_ref,
-    cells_ref,
+    cells_hbm,
     gram_ref,
     pick_ref,
     matrix_ref,
@@ -301,9 +296,12 @@
     give_ref,
     values_ref,
     index_semaphore,
+    cells_ref,
+    cells_semaphore,
     *sums,
 ):
-    cells_ref = cells_ref.reshape(CELL_ROWS, LANES)
+    cells_copy = pltpu.make_async_copy(cells_hbm, cells_ref, cells_semaphore)
+    cells_copy.start()
     index_ref[...] = rows_ref[:, :LANES].astype(jnp.int32)
     copy = pltpu.make_async_copy(index_ref, where_ref, index_semaphore)
     copy.start()
@@ -315,23 +313,24 @@
         return carry
 
     lax.fori_loop(0, CELL_ROWS // zero_rows, clear, 0)
-    lane_level = (lax.broadcasted_iota(jnp.int32, (1, LANES), 1) % 8).astype(F32)
+    twice_level = (lax.broadcasted_iota(jnp.int32, (1, LANES), 1) % 8).astype(F32) * 2.0
     gram_head, gram_tail = split(gram_ref[...])
     gram_both = jnp.concatenate([gram_head, gram_tail], axis=0)
 
     def prepare(tile, carry):
         data = rows_ref[:, pl.ds(pl.multiple_of((tile + 1) * LANES, LANES), LANES)]
         values = mm(jnp.concatenate(split(data), axis=1), pick_ref[...])
+        marked = data + 2.0 * pltpu.roll(data, LANES - 4, 1)
         for slot in range(4):
             values_ref[tile * 4 + slot] = values[:, slot * LANES : (slot + 1) * LANES]
             for point in range(4):
-                weight = data[:, slot * 32 + point : slot * 32 + point + 1]
-                level = data[:, slot * 32 + 4 + point : slot * 32 + 5 + point]
-                mask_ref[point, tile * 4 + slot] = jnp.where(level == lane_level, weight, 0.0)
+                mask = marked[:, slot * 32 + point : slot * 32 + point + 1] - twice_level
+                mask_ref[point, tile * 4 + slot] = jnp.where(jnp.abs(mask - 0.5) <= 0.5, mask, 0.0)
         return carry
 
     lax.fori_loop(0, 8, prepare, 0)
     copy.wait()
+    cells_copy.wait()
     chunk = 16
 
     def move(fetch, store):
@@ -403,7 +402,7 @@
     return pl.pallas_call(
         observe_kernel,
         out_shape=(jax.ShapeDtypeStruct((CH, RLAT, 1024), F32), edge, edge),
-        in_specs=[VM] * 5,
+        in_specs=[VM, pl.BlockSpec(memory_space=pltpu.HBM), VM, VM, VM],
         out_specs=(VM, VM, VM),
         scratch_shapes=[
             pltpu.VMEM((TILES, LANES), jnp.int32),
@@ -413,9 +412,11 @@
             pltpu.VMEM((4, SLOTS, 16, LANES), F32),
             pltpu.VMEM((SLOTS, TILES, LANES), F32),
             pltpu.SemaphoreType.DMA,
+            pltpu.VMEM((CELL_ROWS, LANES), F32),
+            pltpu.SemaphoreType.DMA,
         ]
         + [pltpu.VMEM((CELL_ROWS, LANES), F32)] * ACCS,
-        compiler_params=params(42),
+        compiler_params=params(46),
         name="observe",
     )(rows, cells, gram, jnp.asarray(pick_table(), BF16), backward)
 
@@ -600,7 +601,7 @@
     gram = jnp.dot(jacobian * error_weight, jacobian.T, precision=EXACT)
     gram = jnp.repeat(jnp.repeat(gram, 8, axis=0), 8, axis=1)
     field, north, south = observe(
-        rows.reshape(TILES, WORDS), cells, gram, backward
+        rows.reshape(TILES, WORDS), cells.reshape(CELL_ROWS, LANES), gram, backward
     )
     edge_north, edge_south = send_edges(north, south)
     gradient = adjoint_diffusion(field, control, backward, from_north, from_south, coupling)

time: 180 us -> 173 us (0.961)
  local copies, waits for them, and re-layouts: 7.81 us -> 2.25 us
  Pallas kernels: 107 us -> 104 us
    unnamed x46, local copies, waits for them, and re-layouts: 6.75 us -> 1.2 us
    pallas_call x1, Pallas kernels: 44.6 us -> 41.7 us  [observe(): pl.pallas_call(observe_kernel, out_shape=(jax.ShapeDtypeStruct((CH, RLAT,...]
  transfers between devices with their start and end apart: 20 -> 20, of which waited for: 5 -> 5; matrix products, arithmetic and copies ran while one was open for 1% -> 1% of each run, Pallas kernels for 26% -> 28%
where the time goes in v4:
time: 173 us; the launch traced here: 172 us
  Pallas kernels  104 us (60%)
  starting transfers between devices  40.9 us (24%)
  waiting for transfers between devices  22.3 us (13%)
  local copies, waits for them, and re-layouts  2.25 us (1%)
  between operations  1.98 us (1%)
    pallas_call x1, Pallas kernels, observe(): pl.pallas_call(observe_kernel, out_shape=(jax.ShapeDtypeStruct((CH, RLAT,...  41.7 us
    pallas_call x4, Pallas kernels, spectra(): pl.pallas_call(functools.partial(spectra_kernel, base, add is not None, o...  17.3 us
    pallas_call x4, Pallas kernels, synthesis(): pl.pallas_call(functools.partial(synthesis_kernel, place, before is not N...  13.3 us
    pallas_call x1, Pallas kernels, forward_diffusion(): pl.pallas_call(forward_kernel, grid=(4,), out_shape=(jax.ShapeDtypeStruct...  10.5 us
    ppermute x2, starting transfers between devices, send_edges(): lax.ppermute(north, 'lat', [(i + 1, i) for i in range(count - 1)])  9.49 us
    pallas_call x1, Pallas kernels, route(): pl.pallas_call(route_kernel, out_shape=jax.ShapeDtypeStruct((TILES, 1, WO...  9.43 us
    all_to_all x1, starting transfers between devices, body(): lax.all_to_all(routed, ('lat', 'lon'), split_axis=0, concat_axis=0, tiled...  9.1 us
    ppermute x1, waiting for transfers between devices, body(): from_prior = lax.ppermute(spectrum, 'lon', onward)  8.72 us
  transfers between devices with their start and end apart: 20, of which 5 were waited for; matrix products, arithmetic and copies ran while one was open for 1% of the time, Pallas kernels for 28%

profile of v4, /device:TPU:5, one launch (start us, length us, event | category | flops | bytes accessed | tf_op | source)
XLA Modules:
  0.0 172.0 jit_solution(1130704287718483566)
XLA Ops:
  0.6 0.0 copy-start.20
  0.6 0.0 copy-start.21
  0.7 6.8 %bands.1 = (f32[16,64,128]{2,1,0:T(8,128)}, f32[16,64,128]{2,1,0:T(8,128)}, f32[16,64,128]{2,1,0:T(8,128)}, f32[16,8,900]{2,1,0:T(8,128)}, f32[16,8,900]{2,1,0:T(8,128)}) custom-call(f32[16,64,900]{2,1,0:T(8,128)} %control_ref.1, f32[2,16,32,32]{3,2,1,0:T(8,128)} %inverse_ref.1, f32[16]{0:T(128)} %coupling_ref.3), custom_call_target="tpu_custom_call" | custom-call | tf_op jit(solution)/shard_map/bands/pallas_call | solution.py:141
  7.5 3.5 %collective-permute-start = (f32[16,8,900]{2,1,0:T(8,128)}, f32[16,8,900]{2,1,0:T(8,128)S(1)}, u32[]{:S(2)}, u32[]{:S(2)}) collective-permute-start(f32[16,8,900]{2,1,0:T(8,128)} %get-tuple-element.29), channel_id=1, source_target_pairs={{0,8},{8,16},{16,24},{24,32},{32,40},{40,48},{48,56},{56,64},{64,7... | collective-permute-start | bytes 1382408 | tf_op jit(solution)/shard_map/ppermute | solution.py:161
  11.0 4.0 %collective-permute-start.1 = (f32[16,8,900]{2,1,0:T(8,128)}, f32[16,8,900]{2,1,0:T(8,128)S(1)}, u32[]{:S(2)}, u32[]{:S(2)}) collective-permute-start(f32[16,8,900]{2,1,0:T(8,128)} %get-tuple-element.30), channel_id=1, source_target_pairs={{8,0},{16,8},{24,16},{32,24},{40,32},{48,40},{56,48},{64,56},{72,6... | collective-permute-start | bytes 1382408 | tf_op jit(solution)/shard_map/ppermute | solution.py:160
  15.0 0.1 copy.39
  15.2 0.1 multiply_bitcast_fusion
  15.2 0.1 pad.4
  15.3 0.1 pad_maximum_fusion.project_ref
  16.1 9.4 %route.1 = f32[128,1,1152]{2,1,0:T(1,128)} custom-call(s32[1]{0:T(128)S(6)} %copy.52.live_ref, f32[2048,128]{1,0:T(8,128)S(1)} %copy-done.11, s32[1,2048]{1,0:T(1,128)S(1)} %bitcast.35, s32[4,2048]{1,0:T(4,128)S(1)} %bitcast.33, f32[4,2048]{1,0:T(4,128)S(1)} %bitcast.34, f32[128,128]{1,0:T(8,128)S(1)} %pad_maximum_fusion.project_ref), custom_call_target="tpu_custom_call" | custom-call | tf_op jit(solution)/shard_map/route/pallas_call | solution.py:259
  25.6 9.1 %all-to-all-start = ((f32[128,1,1152]{2,1,0:T(1,128)}), f32[128,1,1152]{2,1,0:T(1,128)S(1)}, u32[]{:S(2)}, u32[]{:S(2)}) async-start(f32[128,1,1152]{2,1,0:T(1,128)} %route.1), calls=%async_computation | async-start | bytes 1179648 | tf_op jit(solution)/shard_map/all_to_all | solution.py:598
  34.7 0.3 fusion.5
  35.0 0.1 broadcast_bitcast_fusion.1
  35.0 0.1 copy.40
  35.1 0.7 dynamic-slice_bitcast_fusion.turn_ref
  35.8 0.1 copy.41.gram_ref
  36.0 0.0 collective-permute-done.1.south_ref
  36.0 0.8 copy-done.7
  36.8 0.2 copy-done.9
  37.0 10.5 %forward.1 = (f32[16,64,900]{2,1,0:T(8,128)}, f32[8,1024,128]{2,1,0:T(8,128)}) custom-call(f32[16,64,900]{2,1,0:T(8,128)} %control_ref.1, f32[16,8,900]{2,1,0:T(8,128)} %copy-done.7, f32[16,8,900]{2,1,0:T(8,128)} %copy-done.9, f32[16,64,128]{2,1,0:T(8,128)} %get-tuple-element.31.matrix_ref), custom_call_target="tpu_custom_call" | custom-call | tf_op jit(solution)/shard_map/forward/pallas_call | solution.py:187
  47.4 0.0 copy-start.16
  47.5 0.0 all-to-all-done
  47.5 0.0 copy-start
  47.6 41.7 %observe.1 = (f32[16,64,1024]{2,1,0:T(8,128)S(1)}, f32[16,2,900]{2,1,0:T(2,128)S(1)}, f32[16,2,900]{2,1,0:T(2,128)S(1)}) custom-call(f32[128,1152]{1,0:T(8,128)S(1)} %bitcast.32, f32[8192,128]{1,0:T(8,128)} %bitcast.36, f32[128,128]{1,0:T(8,128)S(1)} %copy.41.gram_ref, bf16[256,512]{1,0:T(8,128)(2,1)S(1)} %copy-done.12, f32[16,64,128]{2,1,0:T(8,128)S(1)} %copy-done.6), custom_call_target="tpu_custom_call" | custom-call | tf_op jit(solution)/shard_map/observe/pallas_call | solution.py:402
  89.2 1.9 %collective-permute-start.2 = (f32[16,2,900]{2,1,0:T(2,128)S(1)}, f32[16,2,900]{2,1,0:T(2,128)S(1)}, u32[]{:S(2)}, u32[]{:S(2)}) collective-permute-start(f32[16,2,900]{2,1,0:T(2,128)S(1)} %get-tuple-element.36), channel_id=1, source_target_pairs={{0,8},{8,16},{16,24},{24,32},{32,40},{40,48},{48,56},{56,64},{64,7... | collective-permute-start | bytes 345608 | tf_op jit(solution)/shard_map/ppermute | solution.py:161
  91.1 5.5 %collective-permute-start.3 = (f32[16,2,900]{2,1,0:T(2,128)S(1)}, f32[16,2,900]{2,1,0:T(2,128)S(1)}, u32[]{:S(2)}, u32[]{:S(2)}) collective-permute-start(f32[16,2,900]{2,1,0:T(2,128)S(1)} %get-tuple-element.37), channel_id=1, source_target_pairs={{8,0},{16,8},{24,16},{32,24},{40,32},{48,40},{56,48},{64,56},{72,6... | collective-permute-start | bytes 345608 | tf_op jit(solution)/shard_map/ppermute | solution.py:160
  96.6 0.1 pad_add_fusion.order_ref
  96.7 0.0 copy-start.3
  96.7 0.0 copy-start.4
  96.7 4.9 %adjoint.1.local_any = f32[16,64,900]{2,1,0:T(8,128)} custom-call(f32[16,64,1024]{2,1,0:T(8,128)S(1)} %get-tuple-element.35.field_ref, f32[16,64,900]{2,1,0:T(8,128)S(1)} %copy-done, f32[16,64,128]{2,1,0:T(8,128)S(1)} %copy-done.6, f32[16,8,900]{2,1,0:T(8,128)S(1)} %copy-done.8, f32[16,8,900]{2,1,0:T(8,128)S(1)} %copy-done.10, f32[16]{0:T(128)S(1)} %copy-done.16), custom_call_target="tpu_custom_call" | custom-call | flops 402653184 | bytes 12582912 | tf_op jit(solution)/shard_map/adjoint/pallas_call | solution.py:443
  101.6 0.0 collective-permute-done.3.south_ref
  101.7 4.0 %spectra.4 = (f32[16,64,900]{2,1,0:T(8,128)}, f32[4,64,1024]{2,1,0:T(8,128)S(1)}) custom-call(s32[16]{0:T(128)S(1)} %pad_add_fusion.order_ref, f32[16,64,900]{2,1,0:T(8,128)} %adjoint.1.local_any, f32[16,2,900]{2,1,0:T(2,128)S(1)} %collective-permute-done.2.north_ref, ...), custom_call_target="tpu_custom_call", output_to_operand_aliasing={{0}: (1, {})} | custom-call | flops 1610612736 | bytes 8388608 | tf_op jit(solution)/shard_map/spectra/pallas_call | solution.py:514
  105.6 0.1 collective-permute-start.4
  105.7 4.0 %spectra.5 = (f32[16,64,900]{2,1,0:T(8,128)}, f32[4,64,1024]{2,1,0:T(8,128)S(1)}) custom-call(s32[16]{0:T(128)S(1)} %pad_add_fusion.order_ref, f32[16,64,900]{2,1,0:T(8,128)} %get-tuple-element.39.local_any, f32[16,2,900]{2,1,0:T(2,128)S(1)} %collective-permute-done.2.north_ref, ...), custom_call_target="tpu_custom_call", output_to_operand_aliasing={{0}: (1, {})} | custom-call | flops 1610612736 | bytes 8388608 | tf_op jit(solution)/shard_map/spectra/pallas_call | solution.py:514
  109.7 0.6 collective-permute-start.5
  110.3 4.7 %spectra.6 = (f32[16,64,900]{2,1,0:T(8,128)}, f32[2,64,1024]{2,1,0:T(8,128)S(1)}, f32[2,64,1024]{2,1,0:T(8,128)S(1)}) custom-call(s32[16]{0:T(128)S(1)} %pad_add_fusion.order_ref, f32[16,64,900]{2,1,0:T(8,128)} %get-tuple-element.40.local_any, f32[16,2,900]{2,1,0:T(2,128)S(1)} %collective-permute-done.2.north_ref, ...), custom_call_target="tpu_custom_call", output_to_operand_aliasing={{0}: (1, {})} | custom-call | flops 1610612736 | bytes 8388608 | tf_op jit(solution)/shard_map/spectra/pallas_call | solution.py:514
  115.0 1.4 collective-permute-start.6
  116.4 2.4 %collective-permute-start.8 = (f32[2,64,1024]{2,1,0:T(8,128)S(1)}, f32[2,64,1024]{2,1,0:T(8,128)S(1)}, u32[]{:S(2)}, u32[]{:S(2)}) collective-permute-start(f32[2,64,1024]{2,1,0:T(8,128)S(1)} %get-tuple-element.48), channel_id=1, source_target_pairs={{0,6},{1,7},{2,0},{3,1},{4,2},{5,3},{6,4},{7,5},{8,14},{9,15},{10,... | collective-permute-start | bytes 1572872 | tf_op jit(solution)/shard_map/ppermute | solution.py:629
  118.8 0.0 collective-permute-done.5.refs_0_
  118.8 4.7 %spectra.7 = (f32[16,64,900]{2,1,0:T(8,128)}, f32[2,64,1024]{2,1,0:T(8,128)S(1)}, f32[2,64,1024]{2,1,0:T(8,128)S(1)}) custom-call(s32[16]{0:T(128)S(1)} %pad_add_fusion.order_ref, f32[16,64,900]{2,1,0:T(8,128)} %get-tuple-element.42.local_any, f32[16,2,900]{2,1,0:T(2,128)S(1)} %collective-permute-done.2.north_ref, ...), custom_call_target="tpu_custom_call", output_to_operand_aliasing={{0}: (1, {})} | custom-call | flops 1610612736 | bytes 8388608 | tf_op jit(solution)/shard_map/spectra/pallas_call | solution.py:514
  123.4 0.0 copy-start.1
  123.5 0.0 copy-start.2
  123.5 6.9 %collective-permute-done.6 = f32[2,64,1024]{2,1,0:T(8,128)S(1)} collective-permute-done((f32[2,64,1024]{2,1,0:T(8,128)S(1)}, f32[2,64,1024]{2,1,0:T(8,128)S(1)}, u32[]{:S(2)}, u32[]{:S(2)}) %collective-permute-start.6) | collective-permute-done | bytes 524320 | tf_op jit(solution)/shard_map/ppermute | solution.py:628
  130.3 0.1 fusion.4
  130.4 0.6 collective-permute-start.7
  131.0 2.2 %collective-permute-start.9 = (f32[64,1024]{1,0:T(8,128)S(1)}, f32[64,1024]{1,0:T(8,128)S(1)}, u32[]{:S(2)}, u32[]{:S(2)}) collective-permute-start(f32[64,1024]{1,0:T(8,128)S(1)} %get-tuple-element.60), channel_id=1, source_target_pairs={{0,6},{1,7},{2,0},{3,1},{4,2},{5,3},{6,4},{7,5},{8,14},{9,15},{10,... | collective-permute-start | bytes 786440 | tf_op jit(solution)/shard_map/ppermute | solution.py:632
  133.2 5.2 %collective-permute-done.7 = f32[64,1024]{1,0:T(8,128)S(1)} collective-permute-done((f32[64,1024]{1,0:T(8,128)S(1)}, f32[64,1024]{1,0:T(8,128)S(1)}, u32[]{:S(2)}, u32[]{:S(2)}) %collective-permute-start.7) | collective-permute-done | bytes 262176 | tf_op jit(solution)/shard_map/ppermute | solution.py:631
  138.4 0.1 fusion.3
  138.6 2.0 %collective-permute-start.12 = (f32[128,1024]{1,0:T(8,128)S(1)}, f32[128,1024]{1,0:T(8,128)S(1)}, u32[]{:S(2)}, u32[]{:S(2)}) collective-permute-start(f32[128,1024]{1,0:T(8,128)S(1)} %maximum_multiply_fusion.refs_0_), channel_id=1, source_target_pairs={{0,1},{1,0},{2,3},{3,2},{4,5},{5,4},{6,7},{7,6},{8,9},{9,8},{10,11... | collective-permute-start | bytes 1572872 | tf_op jit(solution)/shard_map/ppermute | solution.py:621
  140.7 0.8 collective-permute-start.10
  141.5 1.9 %collective-permute-start.11 = (f32[128,1024]{1,0:T(8,128)S(1)}, f32[128,1024]{1,0:T(8,128)S(1)}, u32[]{:S(2)}, u32[]{:S(2)}) collective-permute-start(f32[128,1024]{1,0:T(8,128)S(1)} %maximum_multiply_fusion.refs_0_), channel_id=1, source_target_pairs={{0,6},{1,7},{2,0},{3,1},{4,2},{5,3},{6,4},{7,5},{8,14},{9,15},{10,... | collective-permute-start | bytes 1572872 | tf_op jit(solution)/shard_map/ppermute | solution.py:640
  143.4 3.3 %synthesis.4.refs_0_ = f32[16,64,900]{2,1,0:T(8,128)} custom-call(s32[16]{0:T(128)S(1)} %pad_add_fusion.order_ref, bf16[1024,900]{1,0:T(8,128)(2,1)S(1)} %copy-done.1, bf16[1024,900]{1,0:T(8,128)(2,1)S(1)} %copy-done.2, f32[8,512]{1,0:T(8,128)S(1)} %dynamic-slice_bitcast_fusion.turn_ref, f32[128,1024]{1,0:T(8,128)S(1)} %maximum_multiply_fusion.refs_0_, ...), custom_call_target="tpu_custom_call" | custom-call | flops 1610612736 | bytes 8388608 | tf_op jit(solution)/shard_map/synthesis/pallas_call | solution.py:562
  146.7 8.7 %collective-permute-done.10.refs_1_ = f32[128,1024]{1,0:T(8,128)S(1)} collective-permute-done((f32[128,1024]{1,0:T(8,128)S(1)}, f32[128,1024]{1,0:T(8,128)S(1)}, u32[]{:S(2)}, u32[]{:S(2)}) %collective-permute-start.10) | collective-permute-done | bytes 524320 | tf_op jit(solution)/shard_map/ppermute | solution.py:639
  155.5 0.8 collective-permute-start.15
  156.3 0.0 collective-permute-start.16
  156.3 1.1 collective-permute-start.13
  157.4 1.7 collective-permute-start.14
  159.1 3.3 %synthesis.5.refs_0_ = f32[16,64,900]{2,1,0:T(8,128)} custom-call(s32[16]{0:T(128)S(1)} %pad_add_fusion.order_ref, bf16[1024,900]{1,0:T(8,128)(2,1)S(1)} %copy-done.1, bf16[1024,900]{1,0:T(8,128)(2,1)S(1)} %copy-done.2, f32[8,512]{1,0:T(8,128)S(1)} %dynamic-slice_bitcast_fusion.turn_ref, ...), custom_call_target="tpu_custom_call", output_to_operand_aliasing={{}: (4, {})} | custom-call | flops 1610612736 | bytes 8388608 | tf_op jit(solution)/shard_map/synthesis/pallas_call | solution.py:562
  162.5 3.3 %synthesis.6.refs_0_ = f32[16,64,900]{2,1,0:T(8,128)} custom-call(s32[16]{0:T(128)S(1)} %pad_add_fusion.order_ref, bf16[1024,900]{1,0:T(8,128)(2,1)S(1)} %copy-done.1, bf16[1024,900]{1,0:T(8,128)(2,1)S(1)} %copy-done.2, f32[8,512]{1,0:T(8,128)S(1)} %dynamic-slice_bitcast_fusion.turn_ref, ...), custom_call_target="tpu_custom_call", output_to_operand_aliasing={{}: (4, {})} | custom-call | flops 1610612736 | bytes 8388608 | tf_op jit(solution)/shard_map/synthesis/pallas_call | solution.py:562
  165.9 1.1 collective-permute-start.17
  166.9 0.1 collective-permute-start.18
  167.0 1.1 collective-permute-done.17.refs_3_
  168.1 0.4 collective-permute-done.18.refs_4_
  168.5 3.3 %synthesis.7 = f32[16,64,900]{2,1,0:T(8,128)} custom-call(s32[16]{0:T(128)S(1)} %pad_add_fusion.order_ref, bf16[1024,900]{1,0:T(8,128)(2,1)S(1)} %copy-done.1, bf16[1024,900]{1,0:T(8,128)(2,1)S(1)} %copy-done.2, f32[8,512]{1,0:T(8,128)S(1)} %dynamic-slice_bitcast_fusion.turn_ref, f32[16,64,900]{2,1,0:T(8,128)} %synthesis.6.refs_0_, ...), custom_call_target="tpu_custom_call", output_to_operand_aliasing={{}: (4, {})} | custom-call | flops 1610612736 | bytes 8388608 | tf_op jit(solution)/shard_map/synthesis/pallas_call | solution.py:562
  (54 shorter events, 0.3 us)
Async XLA Ops:
  0.6 35.3 %copy-start.20 = (s32[8]{0:T(128)S(1)}, s32[8]{0:T(128)}, u32[]{:S(2)}) copy-start(s32[8]{0:T(128)} %constant.83.clone) | copy-start | bytes 100
  0.6 35.3 %copy-start.21 = (s32[8]{0:T(128)S(1)}, s32[8]{0:T(128)}, u32[]{:S(2)}) copy-start(s32[8]{0:T(128)} %constant.82.clone) | copy-start | bytes 100
  0.7 14.4 %copy-start.17 = (f32[16,128]{1,0:T(8,128)S(1)}, f32[16,128]{1,0:T(8,128)}, u32[]{:S(2)}) copy-start(f32[16,128]{1,0:T(8,128)} %param.22) | copy-start | bytes 24580
  0.7 14.5 %copy-start.18 = (f32[128]{0:T(128)S(1)}, f32[128]{0:T(128)}, u32[]{:S(2)}) copy-start(f32[128]{0:T(128)} %param.23) | copy-start | bytes 1540
  0.7 15.4 %copy-start.15 = (s32[2048,1]{0,1:T(1,128)S(1)}, s32[2048,1]{0,1:T(1,128)}, u32[]{:S(2)}) copy-start(s32[2048,1]{0,1:T(1,128)} %param.26) | copy-start | bytes 24580
  0.7 15.4 %copy-start.13 = (s32[2048,4]{0,1:T(4,128)S(1)}, s32[2048,4]{0,1:T(4,128)}, u32[]{:S(2)}) copy-start(s32[2048,4]{0,1:T(4,128)} %param.27) | copy-start | bytes 98308
  0.7 15.4 %copy-start.14 = (f32[2048,4]{0,1:T(4,128)S(1)}, f32[2048,4]{0,1:T(4,128)}, u32[]{:S(2)}) copy-start(f32[2048,4]{0,1:T(4,128)} %param.28) | copy-start | bytes 98308
  0.7 15.4 %copy-start.11 = (f32[2048,128]{1,0:T(8,128)S(1)}, f32[2048,128]{1,0:T(8,128)}, u32[]{:S(2)}) copy-start(f32[2048,128]{1,0:T(8,128)} %values_ref.1) | copy-start | bytes 3145732
  7.5 28.5 %collective-permute-start = (f32[16,8,900]{2,1,0:T(8,128)}, f32[16,8,900]{2,1,0:T(8,128)S(1)}, u32[]{:S(2)}, u32[]{:S(2)}) collective-permute-start(f32[16,8,900]{2,1,0:T(8,128)} %get-tuple-element.29), channel_id=1, source_target_pairs={{0,8},{8,16},{16,24},{24,32},{32,40},{40,48},{48,56},{56,64},{64,7... | collective-permute-start | bytes 1382408 | tf_op jit(solution)/shard_map/ppermute | solution.py:161
  11.0 25.0 %collective-permute-start.1 = (f32[16,8,900]{2,1,0:T(8,128)}, f32[16,8,900]{2,1,0:T(8,128)S(1)}, u32[]{:S(2)}, u32[]{:S(2)}) collective-permute-start(f32[16,8,900]{2,1,0:T(8,128)} %get-tuple-element.30), channel_id=1, source_target_pairs={{8,0},{16,8},{24,16},{32,24},{40,32},{48,40},{56,48},{64,56},{72,6... | collective-permute-start | bytes 1382408 | tf_op jit(solution)/shard_map/ppermute | solution.py:160
  25.6 22.0 %copy-start.6 = (f32[16,64,128]{2,1,0:T(8,128)S(1)}, f32[16,64,128]{2,1,0:T(8,128)}, u32[]{:S(2)}) copy-start(f32[16,64,128]{2,1,0:T(8,128)} %get-tuple-element.34.matrix_ref) | copy-start | bytes 1572868
  25.6 22.0 %copy-start.12 = (bf16[256,512]{1,0:T(8,128)(2,1)S(1)}, bf16[256,512]{1,0:T(8,128)(2,1)}, u32[]{:S(2)}) copy-start(bf16[256,512]{1,0:T(8,128)(2,1)} %constant.76.clone.pick_ref) | copy-start | bytes 786436
  25.6 21.9 %all-to-all-start = ((f32[128,1,1152]{2,1,0:T(1,128)}), f32[128,1,1152]{2,1,0:T(1,128)S(1)}, u32[]{:S(2)}, u32[]{:S(2)}) async-start(f32[128,1,1152]{2,1,0:T(1,128)} %route.1), calls=%async_computation | async-start | bytes 1179648 | tf_op jit(solution)/shard_map/all_to_all | solution.py:598
  36.0 0.8 copy-start.7
  36.0 1.0 copy-start.9
  47.4 49.3 %copy-start.8 = (f32[16,8,900]{2,1,0:T(8,128)S(1)}, f32[16,8,900]{2,1,0:T(8,128)}, u32[]{:S(2)}) copy-start(f32[16,8,900]{2,1,0:T(8,128)} %copy-done.7) | copy-start | bytes 1382404
  47.4 49.3 %copy-start.10 = (f32[16,8,900]{2,1,0:T(8,128)S(1)}, f32[16,8,900]{2,1,0:T(8,128)}, u32[]{:S(2)}) copy-start(f32[16,8,900]{2,1,0:T(8,128)} %copy-done.9) | copy-start | bytes 1382404
  47.4 49.3 %copy-start.16 = (f32[16]{0:T(128)S(1)}, f32[16]{0:T(128)}, u32[]{:S(2)}) copy-start(f32[16]{0:T(128)} %coupling_ref.3) | copy-start | bytes 196
  47.5 49.2 %copy-start = (f32[16,64,900]{2,1,0:T(8,128)S(1)}, f32[16,64,900]{2,1,0:T(8,128)}, u32[]{:S(2)}) copy-start(f32[16,64,900]{2,1,0:T(8,128)} %control_ref.1) | copy-start | bytes 11059204
  89.2 12.4 %collective-permute-start.2 = (f32[16,2,900]{2,1,0:T(2,128)S(1)}, f32[16,2,900]{2,1,0:T(2,128)S(1)}, u32[]{:S(2)}, u32[]{:S(2)}) collective-permute-start(f32[16,2,900]{2,1,0:T(2,128)S(1)} %get-tuple-element.36), channel_id=1, source_target_pairs={{0,8},{8,16},{16,24},{24,32},{32,40},{40,48},{48,56},{56,64},{64,7... | collective-permute-start | bytes 345608 | tf_op jit(solution)/shard_map/ppermute | solution.py:161
  91.1 10.5 %collective-permute-start.3 = (f32[16,2,900]{2,1,0:T(2,128)S(1)}, f32[16,2,900]{2,1,0:T(2,128)S(1)}, u32[]{:S(2)}, u32[]{:S(2)}) collective-permute-start(f32[16,2,900]{2,1,0:T(2,128)S(1)} %get-tuple-element.37), channel_id=1, source_target_pairs={{8,0},{16,8},{24,16},{32,24},{40,32},{48,40},{56,48},{64,56},{72,6... | collective-permute-start | bytes 345608 | tf_op jit(solution)/shard_map/ppermute | solution.py:160
  96.7 4.9 %copy-start.3 = (bf16[900,1024]{1,0:T(8,128)(2,1)S(1)}, bf16[900,1024]{1,0:T(8,128)(2,1)}, u32[]{:S(2)}) copy-start(bf16[900,1024]{1,0:T(8,128)(2,1)} %constant.77.clone.head_ref) | copy-start | bytes 5529604
  96.7 4.9 %copy-start.4 = (bf16[900,1024]{1,0:T(8,128)(2,1)S(1)}, bf16[900,1024]{1,0:T(8,128)(2,1)}, u32[]{:S(2)}) copy-start(bf16[900,1024]{1,0:T(8,128)(2,1)} %constant.78.clone.tail_ref) | copy-start | bytes 5529604
  96.7 4.9 %copy-start.5 = (f32[16,64,128]{2,1,0:T(8,128)S(1)}, f32[16,64,128]{2,1,0:T(8,128)}, u32[]{:S(2)}) copy-start(f32[16,64,128]{2,1,0:T(8,128)} %get-tuple-element.38.mend_ref) | copy-start | bytes 1572868
  105.6 4.7 %collective-permute-start.4 = (f32[4,64,1024]{2,1,0:T(8,128)S(1)}, f32[4,64,1024]{2,1,0:T(8,128)S(1)}, u32[]{:S(2)}, u32[]{:S(2)}) collective-permute-start(f32[4,64,1024]{2,1,0:T(8,128)S(1)} %get-tuple-element.41), channel_id=1, source_target_pairs={{0,1},{1,0},{2,3},{3,2},{4,5},{5,4},{6,7},{7,6},{8,9},{9,8},{10,11... | collective-permute-start | bytes 3145736 | tf_op jit(solution)/shard_map/ppermute | solution.py:621
  109.7 9.0 %collective-permute-start.5 = (f32[4,64,1024]{2,1,0:T(8,128)S(1)}, f32[4,64,1024]{2,1,0:T(8,128)S(1)}, u32[]{:S(2)}, u32[]{:S(2)}) collective-permute-start(f32[4,64,1024]{2,1,0:T(8,128)S(1)} %get-tuple-element.43), channel_id=1, source_target_pairs={{0,1},{1,0},{2,3},{3,2},{4,5},{5,4},{6,7},{7,6},{8,9},{9,8},{10,11... | collective-permute-start | bytes 3145736 | tf_op jit(solution)/shard_map/ppermute | solution.py:621
  115.0 15.4 %collective-permute-start.6 = (f32[2,64,1024]{2,1,0:T(8,128)S(1)}, f32[2,64,1024]{2,1,0:T(8,128)S(1)}, u32[]{:S(2)}, u32[]{:S(2)}) collective-permute-start(f32[2,64,1024]{2,1,0:T(8,128)S(1)} %get-tuple-element.47), channel_id=1, source_target_pairs={{0,2},{1,3},{2,4},{3,5},{4,6},{5,7},{6,0},{7,1},{8,10},{9,11},{10,... | collective-permute-start | bytes 1572872 | tf_op jit(solution)/shard_map/ppermute | solution.py:628
  116.4 13.9 %collective-permute-start.8 = (f32[2,64,1024]{2,1,0:T(8,128)S(1)}, f32[2,64,1024]{2,1,0:T(8,128)S(1)}, u32[]{:S(2)}, u32[]{:S(2)}) collective-permute-start(f32[2,64,1024]{2,1,0:T(8,128)S(1)} %get-tuple-element.48), channel_id=1, source_target_pairs={{0,6},{1,7},{2,0},{3,1},{4,2},{5,3},{6,4},{7,5},{8,14},{9,15},{10,... | collective-permute-start | bytes 1572872 | tf_op jit(solution)/shard_map/ppermute | solution.py:629
  118.8 14.4 %copy-start.19 = (f32[512]{0:T(512)S(1)}, f32[512]{0:T(512)}, u32[]{:S(2)}) copy-start(f32[512]{0:T(512)} %param.24) | copy-start | bytes 6148
  123.4 19.9 %copy-start.1 = (bf16[1024,900]{1,0:T(8,128)(2,1)S(1)}, bf16[1024,900]{1,0:T(8,128)(2,1)}, u32[]{:S(2)}) copy-start(bf16[1024,900]{1,0:T(8,128)(2,1)} %constant.79.clone.head_ref) | copy-start | bytes 5529604
  123.5 19.9 %copy-start.2 = (bf16[1024,900]{1,0:T(8,128)(2,1)S(1)}, bf16[1024,900]{1,0:T(8,128)(2,1)}, u32[]{:S(2)}) copy-start(bf16[1024,900]{1,0:T(8,128)(2,1)} %constant.80.clone.tail_ref) | copy-start | bytes 5529604
  130.4 8.0 %collective-permute-start.7 = (f32[64,1024]{1,0:T(8,128)S(1)}, f32[64,1024]{1,0:T(8,128)S(1)}, u32[]{:S(2)}, u32[]{:S(2)}) collective-permute-start(f32[64,1024]{1,0:T(8,128)S(1)} %get-tuple-element.59), channel_id=1, source_target_pairs={{0,2},{1,3},{2,4},{3,5},{4,6},{5,7},{6,0},{7,1},{8,10},{9,11},{10,... | collective-permute-start | bytes 786440 | tf_op jit(solution)/shard_map/ppermute | solution.py:631
  131.0 7.4 %collective-permute-start.9 = (f32[64,1024]{1,0:T(8,128)S(1)}, f32[64,1024]{1,0:T(8,128)S(1)}, u32[]{:S(2)}, u32[]{:S(2)}) collective-permute-start(f32[64,1024]{1,0:T(8,128)S(1)} %get-tuple-element.60), channel_id=1, source_target_pairs={{0,6},{1,7},{2,0},{3,1},{4,2},{5,3},{6,4},{7,5},{8,14},{9,15},{10,... | collective-permute-start | bytes 786440 | tf_op jit(solution)/shard_map/ppermute | solution.py:632
  138.6 4.8 %collective-permute-start.12 = (f32[128,1024]{1,0:T(8,128)S(1)}, f32[128,1024]{1,0:T(8,128)S(1)}, u32[]{:S(2)}, u32[]{:S(2)}) collective-permute-start(f32[128,1024]{1,0:T(8,128)S(1)} %maximum_multiply_fusion.refs_0_), channel_id=1, source_target_pairs={{0,1},{1,0},{2,3},{3,2},{4,5},{5,4},{6,7},{7,6},{8,9},{9,8},{10,11... | collective-permute-start | bytes 1572872 | tf_op jit(solution)/shard_map/ppermute | solution.py:621
  140.7 14.8 %collective-permute-start.10 = (f32[128,1024]{1,0:T(8,128)S(1)}, f32[128,1024]{1,0:T(8,128)S(1)}, u32[]{:S(2)}, u32[]{:S(2)}) collective-permute-start(f32[128,1024]{1,0:T(8,128)S(1)} %maximum_multiply_fusion.refs_0_), channel_id=1, source_target_pairs={{0,2},{1,3},{2,4},{3,5},{4,6},{5,7},{6,0},{7,1},{8,10},{9,11},{10,... | collective-permute-start | bytes 1572872 | tf_op jit(solution)/shard_map/ppermute | solution.py:639
  141.5 14.0 %collective-permute-start.11 = (f32[128,1024]{1,0:T(8,128)S(1)}, f32[128,1024]{1,0:T(8,128)S(1)}, u32[]{:S(2)}, u32[]{:S(2)}) collective-permute-start(f32[128,1024]{1,0:T(8,128)S(1)} %maximum_multiply_fusion.refs_0_), channel_id=1, source_target_pairs={{0,6},{1,7},{2,0},{3,1},{4,2},{5,3},{6,4},{7,5},{8,14},{9,15},{10,... | collective-permute-start | bytes 1572872 | tf_op jit(solution)/shard_map/ppermute | solution.py:640
  155.5 3.7 %collective-permute-start.15 = (f32[128,1024]{1,0:T(8,128)S(1)}, f32[128,1024]{1,0:T(8,128)S(1)}, u32[]{:S(2)}, u32[]{:S(2)}) collective-permute-start(f32[128,1024]{1,0:T(8,128)S(1)} %collective-permute-done.10.refs_1_), channel_id=1, source_target_pairs={{0,1},{1,0},{2,3},{3,2},{4,5},{5,4},{6,7},{7,6},{8,9},{9,8},{10,11... | collective-permute-start | bytes 1572872 | tf_op jit(solution)/shard_map/ppermute | solution.py:621
  156.3 6.2 %collective-permute-start.16 = (f32[128,1024]{1,0:T(8,128)S(1)}, f32[128,1024]{1,0:T(8,128)S(1)}, u32[]{:S(2)}, u32[]{:S(2)}) collective-permute-start(f32[128,1024]{1,0:T(8,128)S(1)} %collective-permute-done.11.refs_1_), channel_id=1, source_target_pairs={{0,1},{1,0},{2,3},{3,2},{4,5},{5,4},{6,7},{7,6},{8,9},{9,8},{10,11... | collective-permute-start | bytes 1572872 | tf_op jit(solution)/shard_map/ppermute | solution.py:621
  156.3 9.5 %collective-permute-start.13 = (f32[64,1024]{1,0:T(8,128)S(1)}, f32[64,1024]{1,0:T(8,128)S(1)}, u32[]{:S(2)}, u32[]{:S(2)}) collective-permute-start(f32[64,1024]{1,0:T(8,128)S(1)} %slice.38), channel_id=1, source_target_pairs={{0,2},{1,3},{2,4},{3,5},{4,6},{5,7},{6,0},{7,1},{8,10},{9,11},{10,... | collective-permute-start | bytes 786440 | tf_op jit(solution)/shard_map/ppermute | solution.py:643
  157.4 8.4 %collective-permute-start.14 = (f32[64,1024]{1,0:T(8,128)S(1)}, f32[64,1024]{1,0:T(8,128)S(1)}, u32[]{:S(2)}, u32[]{:S(2)}) collective-permute-start(f32[64,1024]{1,0:T(8,128)S(1)} %slice.39), channel_id=1, source_target_pairs={{0,6},{1,7},{2,0},{3,1},{4,2},{5,3},{6,4},{7,5},{8,14},{9,15},{10,... | collective-permute-start | bytes 786440 | tf_op jit(solution)/shard_map/ppermute | solution.py:644
  165.9 2.2 %collective-permute-start.17 = (f32[64,1024]{1,0:T(8,128)S(1)}, f32[64,1024]{1,0:T(8,128)S(1)}, u32[]{:S(2)}, u32[]{:S(2)}) collective-permute-start(f32[64,1024]{1,0:T(8,128)S(1)} %collective-permute-done.13.refs_1_), channel_id=1, source_target_pairs={{0,1},{1,0},{2,3},{3,2},{4,5},{5,4},{6,7},{7,6},{8,9},{9,8},{10,11... | collective-permute-start | bytes 786440 | tf_op jit(solution)/shard_map/ppermute | solution.py:621
  166.9 1.5 collective-permute-start.18

commit v5 on v4

--- a/solution.py
+++ b/solution.py
@@ -460,25 +460,25 @@
     if added:
         add_ref, refs = refs[0], refs[1:]
     gradient_any, refs = refs[0], refs[1:]
-    out_refs, (field_ref, in_semaphores, out_semaphores) = refs[:outputs], refs[outputs:]
+    out_refs, (field_ref, fix_ref, in_semaphores, out_semaphores) = refs[:outputs], refs[outputs:]
     channels = [order_ref[base + i] for i in range(4)]
     loads = [
         pltpu.make_async_copy(local_any.at[channels[i]], field_ref.at[i], in_semaphores.at[i]) for i in range(4)
     ]
     for load in loads:
         load.start()
-    for load in loads:
-        load.wait()
     for here, channel in enumerate(channels):
         mend = mend_ref[channel]
         north, south = north_ref[channel], south_ref[channel]
-        field_ref[here] = (
-            field_ref[here]
-            + mend[:, 0:1] * north[0:1]
+        fix_ref[here] = (
+            mend[:, 0:1] * north[0:1]
             + mend[:, 1:2] * north[1:2]
             + mend[:, 2:3] * south[0:1]
             + mend[:, 3:4] * south[1:2]
         )
+    for load in loads:
+        load.wait()
+    field_ref[...] = field_ref[...] + fix_ref[...]
     saves = [
         pltpu.make_async_copy(field_ref.at[i], gradient_any.at[channels[i]], out_semaphores.at[i]) for i in range(4)
     ]
@@ -518,6 +518,7 @@
         out_specs=(ANY,) + (VM,) * outputs,
         scratch_shapes=[
             pltpu.VMEM((4, RLAT, CLON), F32),
+            pltpu.VMEM((4, RLAT, CLON), F32),
             pltpu.SemaphoreType.DMA((4,)),
             pltpu.SemaphoreType.DMA((4,)),
         ],

time: 173 us -> 172 us (level)
  transfers between devices with their start and end apart: 20 -> 20, of which waited for: 5 -> 5; matrix products, arithmetic and copies ran while one was open for 1% -> 1% of each run, Pallas kernels for 28% -> 27%
where the time goes in v5:
time: 172 us; the launch traced here: 171 us
  Pallas kernels  103 us (60%)
  starting transfers between devices  40.4 us (23%)
  waiting for transfers between devices  22.8 us (13%)
  local copies, waits for them, and re-layouts  2.25 us (1%)
  between operations  1.97 us (1%)
    pallas_call x1, Pallas kernels, observe(): pl.pallas_call(observe_kernel, out_shape=(jax.ShapeDtypeStruct((CH, RLAT,...  42 us
    pallas_call x4, Pallas kernels, spectra(): pl.pallas_call(functools.partial(spectra_kernel, base, add is not None, o...  15.9 us
    pallas_call x4, Pallas kernels, synthesis(): pl.pallas_call(functools.partial(synthesis_kernel, place, before is not N...  13.3 us
    pallas_call x1, Pallas kernels, forward_diffusion(): pl.pallas_call(forward_kernel, grid=(4,), out_shape=(jax.ShapeDtypeStruct...  10.5 us
    ppermute x2, starting transfers between devices, send_edges(): lax.ppermute(north, 'lat', [(i + 1, i) for i in range(count - 1)])  9.49 us
    pallas_call x1, Pallas kernels, route(): pl.pallas_call(route_kernel, out_shape=jax.ShapeDtypeStruct((TILES, 1, WO...  9.43 us
    all_to_all x1, starting transfers between devices, body(): lax.all_to_all(routed, ('lat', 'lon'), split_axis=0, concat_axis=0, tiled...  9.1 us
    ppermute x1, waiting for transfers between devices, body(): from_prior = lax.ppermute(spectrum, 'lon', onward)  8.71 us
  transfers between devices with their start and end apart: 20, of which 5 were waited for; matrix products, arithmetic and copies ran while one was open for 1% of the time, Pallas kernels for 27%

profile of v5, /device:TPU:5, one launch (start us, length us, event | category | flops | bytes accessed | tf_op | source)
XLA Modules:
  0.0 170.9 jit_solution(8252932593318990940)
XLA Ops:
  0.6 0.0 copy-start.20
  0.6 0.0 copy-start.21
  0.7 6.8 %bands.1 = (f32[16,64,128]{2,1,0:T(8,128)}, f32[16,64,128]{2,1,0:T(8,128)}, f32[16,64,128]{2,1,0:T(8,128)}, f32[16,8,900]{2,1,0:T(8,128)}, f32[16,8,900]{2,1,0:T(8,128)}) custom-call(f32[16,64,900]{2,1,0:T(8,128)} %control_ref.1, f32[2,16,32,32]{3,2,1,0:T(8,128)} %inverse_ref.1, f32[16]{0:T(128)} %coupling_ref.3), custom_call_target="tpu_custom_call" | custom-call | tf_op jit(solution)/shard_map/bands/pallas_call | solution.py:141
  7.5 3.5 %collective-permute-start = (f32[16,8,900]{2,1,0:T(8,128)}, f32[16,8,900]{2,1,0:T(8,128)S(1)}, u32[]{:S(2)}, u32[]{:S(2)}) collective-permute-start(f32[16,8,900]{2,1,0:T(8,128)} %get-tuple-element.29), channel_id=1, source_target_pairs={{0,8},{8,16},{16,24},{24,32},{32,40},{40,48},{48,56},{56,64},{64,7... | collective-permute-start | bytes 1382408 | tf_op jit(solution)/shard_map/ppermute | solution.py:161
  11.0 4.0 %collective-permute-start.1 = (f32[16,8,900]{2,1,0:T(8,128)}, f32[16,8,900]{2,1,0:T(8,128)S(1)}, u32[]{:S(2)}, u32[]{:S(2)}) collective-permute-start(f32[16,8,900]{2,1,0:T(8,128)} %get-tuple-element.30), channel_id=1, source_target_pairs={{8,0},{16,8},{24,16},{32,24},{40,32},{48,40},{56,48},{64,56},{72,6... | collective-permute-start | bytes 1382408 | tf_op jit(solution)/shard_map/ppermute | solution.py:160
  15.0 0.1 copy.39
  15.2 0.1 multiply_bitcast_fusion
  15.2 0.1 pad.4
  15.3 0.1 pad_maximum_fusion.project_ref
  16.1 9.4 %route.1 = f32[128,1,1152]{2,1,0:T(1,128)} custom-call(s32[1]{0:T(128)S(6)} %copy.52.live_ref, f32[2048,128]{1,0:T(8,128)S(1)} %copy-done.11, s32[1,2048]{1,0:T(1,128)S(1)} %bitcast.35, s32[4,2048]{1,0:T(4,128)S(1)} %bitcast.33, f32[4,2048]{1,0:T(4,128)S(1)} %bitcast.34, f32[128,128]{1,0:T(8,128)S(1)} %pad_maximum_fusion.project_ref), custom_call_target="tpu_custom_call" | custom-call | tf_op jit(solution)/shard_map/route/pallas_call | solution.py:259
  25.6 9.1 %all-to-all-start = ((f32[128,1,1152]{2,1,0:T(1,128)}), f32[128,1,1152]{2,1,0:T(1,128)S(1)}, u32[]{:S(2)}, u32[]{:S(2)}) async-start(f32[128,1,1152]{2,1,0:T(1,128)} %route.1), calls=%async_computation | async-start | bytes 1179648 | tf_op jit(solution)/shard_map/all_to_all | solution.py:599
  34.7 0.3 fusion.5
  35.0 0.1 broadcast_bitcast_fusion.1
  35.0 0.1 copy.40
  35.1 0.7 dynamic-slice_bitcast_fusion.turn_ref
  35.8 0.1 copy.41.gram_ref
  36.0 0.8 copy-done.7
  36.8 0.2 copy-done.9
  37.0 10.5 %forward.1 = (f32[16,64,900]{2,1,0:T(8,128)}, f32[8,1024,128]{2,1,0:T(8,128)}) custom-call(f32[16,64,900]{2,1,0:T(8,128)} %control_ref.1, f32[16,8,900]{2,1,0:T(8,128)} %copy-done.7, f32[16,8,900]{2,1,0:T(8,128)} %copy-done.9, f32[16,64,128]{2,1,0:T(8,128)} %get-tuple-element.31.matrix_ref), custom_call_target="tpu_custom_call" | custom-call | tf_op jit(solution)/shard_map/forward/pallas_call | solution.py:187
  47.4 0.0 copy-start.16
  47.5 0.0 all-to-all-done
  47.5 0.0 copy-start
  47.6 42.0 %observe.1 = (f32[16,64,1024]{2,1,0:T(8,128)S(1)}, f32[16,2,900]{2,1,0:T(2,128)S(1)}, f32[16,2,900]{2,1,0:T(2,128)S(1)}) custom-call(f32[128,1152]{1,0:T(8,128)S(1)} %bitcast.32, f32[8192,128]{1,0:T(8,128)} %bitcast.36, f32[128,128]{1,0:T(8,128)S(1)} %copy.41.gram_ref, bf16[256,512]{1,0:T(8,128)(2,1)S(1)} %copy-done.12, f32[16,64,128]{2,1,0:T(8,128)S(1)} %copy-done.6), custom_call_target="tpu_custom_call" | custom-call | tf_op jit(solution)/shard_map/observe/pallas_call | solution.py:402
  89.6 1.9 %collective-permute-start.2 = (f32[16,2,900]{2,1,0:T(2,128)S(1)}, f32[16,2,900]{2,1,0:T(2,128)S(1)}, u32[]{:S(2)}, u32[]{:S(2)}) collective-permute-start(f32[16,2,900]{2,1,0:T(2,128)S(1)} %get-tuple-element.36), channel_id=1, source_target_pairs={{0,8},{8,16},{16,24},{24,32},{32,40},{40,48},{48,56},{56,64},{64,7... | collective-permute-start | bytes 345608 | tf_op jit(solution)/shard_map/ppermute | solution.py:161
  91.5 5.5 %collective-permute-start.3 = (f32[16,2,900]{2,1,0:T(2,128)S(1)}, f32[16,2,900]{2,1,0:T(2,128)S(1)}, u32[]{:S(2)}, u32[]{:S(2)}) collective-permute-start(f32[16,2,900]{2,1,0:T(2,128)S(1)} %get-tuple-element.37), channel_id=1, source_target_pairs={{8,0},{16,8},{24,16},{32,24},{40,32},{48,40},{56,48},{64,56},{72,6... | collective-permute-start | bytes 345608 | tf_op jit(solution)/shard_map/ppermute | solution.py:160
  97.0 0.1 pad_add_fusion.order_ref
  97.1 0.0 copy-start.3
  97.1 0.0 copy-start.4
  97.1 4.9 %adjoint.1.local_any = f32[16,64,900]{2,1,0:T(8,128)} custom-call(f32[16,64,1024]{2,1,0:T(8,128)S(1)} %get-tuple-element.35.field_ref, f32[16,64,900]{2,1,0:T(8,128)S(1)} %copy-done, f32[16,64,128]{2,1,0:T(8,128)S(1)} %copy-done.6, f32[16,8,900]{2,1,0:T(8,128)S(1)} %copy-done.8, f32[16,8,900]{2,1,0:T(8,128)S(1)} %copy-done.10, f32[16]{0:T(128)S(1)} %copy-done.16), custom_call_target="tpu_custom_call" | custom-call | flops 402653184 | bytes 12582912 | tf_op jit(solution)/shard_map/adjoint/pallas_call | solution.py:443
  102.0 0.0 collective-permute-done.3.south_ref
  102.0 3.9 %spectra.4 = (f32[16,64,900]{2,1,0:T(8,128)}, f32[4,64,1024]{2,1,0:T(8,128)S(1)}) custom-call(s32[16]{0:T(128)S(1)} %pad_add_fusion.order_ref, f32[16,64,900]{2,1,0:T(8,128)} %adjoint.1.local_any, f32[16,2,900]{2,1,0:T(2,128)S(1)} %collective-permute-done.2.north_ref, ...), custom_call_target="tpu_custom_call", output_to_operand_aliasing={{0}: (1, {})} | custom-call | flops 1610612736 | bytes 8388608 | tf_op jit(solution)/shard_map/spectra/pallas_call | solution.py:514
  106.0 0.2 collective-permute-start.4
  106.2 3.9 %spectra.5 = (f32[16,64,900]{2,1,0:T(8,128)}, f32[4,64,1024]{2,1,0:T(8,128)S(1)}) custom-call(s32[16]{0:T(128)S(1)} %pad_add_fusion.order_ref, f32[16,64,900]{2,1,0:T(8,128)} %get-tuple-element.39.local_any, f32[16,2,900]{2,1,0:T(2,128)S(1)} %collective-permute-done.2.north_ref, ...), custom_call_target="tpu_custom_call", output_to_operand_aliasing={{0}: (1, {})} | custom-call | flops 1610612736 | bytes 8388608 | tf_op jit(solution)/shard_map/spectra/pallas_call | solution.py:514
  110.2 0.4 collective-permute-start.5
  110.6 4.0 %spectra.6 = (f32[16,64,900]{2,1,0:T(8,128)}, f32[2,64,1024]{2,1,0:T(8,128)S(1)}, f32[2,64,1024]{2,1,0:T(8,128)S(1)}) custom-call(s32[16]{0:T(128)S(1)} %pad_add_fusion.order_ref, f32[16,64,900]{2,1,0:T(8,128)} %get-tuple-element.40.local_any, f32[16,2,900]{2,1,0:T(2,128)S(1)} %collective-permute-done.2.north_ref, ...), custom_call_target="tpu_custom_call", output_to_operand_aliasing={{0}: (1, {})} | custom-call | flops 1610612736 | bytes 8388608 | tf_op jit(solution)/shard_map/spectra/pallas_call | solution.py:514
  114.6 1.6 collective-permute-start.6
  116.2 1.6 collective-permute-start.8
  117.7 4.0 %spectra.7 = (f32[16,64,900]{2,1,0:T(8,128)}, f32[2,64,1024]{2,1,0:T(8,128)S(1)}, f32[2,64,1024]{2,1,0:T(8,128)S(1)}) custom-call(s32[16]{0:T(128)S(1)} %pad_add_fusion.order_ref, f32[16,64,900]{2,1,0:T(8,128)} %get-tuple-element.42.local_any, f32[16,2,900]{2,1,0:T(2,128)S(1)} %collective-permute-done.2.north_ref, ...), custom_call_target="tpu_custom_call", output_to_operand_aliasing={{0}: (1, {})} | custom-call | flops 1610612736 | bytes 8388608 | tf_op jit(solution)/shard_map/spectra/pallas_call | solution.py:514
  121.8 0.0 copy-start.1
  121.8 0.0 copy-start.2
  121.8 7.5 %collective-permute-done.6 = f32[2,64,1024]{2,1,0:T(8,128)S(1)} collective-permute-done((f32[2,64,1024]{2,1,0:T(8,128)S(1)}, f32[2,64,1024]{2,1,0:T(8,128)S(1)}, u32[]{:S(2)}, u32[]{:S(2)}) %collective-permute-start.6) | collective-permute-done | bytes 524320 | tf_op jit(solution)/shard_map/ppermute | solution.py:629
  129.3 0.1 fusion.4
  129.4 0.9 collective-permute-start.7
  130.3 1.9 %collective-permute-start.9 = (f32[64,1024]{1,0:T(8,128)S(1)}, f32[64,1024]{1,0:T(8,128)S(1)}, u32[]{:S(2)}, u32[]{:S(2)}) collective-permute-start(f32[64,1024]{1,0:T(8,128)S(1)} %get-tuple-element.60), channel_id=1, source_target_pairs={{0,6},{1,7},{2,0},{3,1},{4,2},{5,3},{6,4},{7,5},{8,14},{9,15},{10,... | collective-permute-start | bytes 786440 | tf_op jit(solution)/shard_map/ppermute | solution.py:633
  132.2 5.0 %collective-permute-done.7 = f32[64,1024]{1,0:T(8,128)S(1)} collective-permute-done((f32[64,1024]{1,0:T(8,128)S(1)}, f32[64,1024]{1,0:T(8,128)S(1)}, u32[]{:S(2)}, u32[]{:S(2)}) %collective-permute-start.7) | collective-permute-done | bytes 262176 | tf_op jit(solution)/shard_map/ppermute | solution.py:632
  137.2 0.0 collective-permute-done.9
  137.2 0.1 fusion.3
  137.4 2.2 %collective-permute-start.12 = (f32[128,1024]{1,0:T(8,128)S(1)}, f32[128,1024]{1,0:T(8,128)S(1)}, u32[]{:S(2)}, u32[]{:S(2)}) collective-permute-start(f32[128,1024]{1,0:T(8,128)S(1)} %maximum_multiply_fusion.refs_0_), channel_id=1, source_target_pairs={{0,1},{1,0},{2,3},{3,2},{4,5},{5,4},{6,7},{7,6},{8,9},{9,8},{10,11... | collective-permute-start | bytes 1572872 | tf_op jit(solution)/shard_map/ppermute | solution.py:622
  139.6 0.8 collective-permute-start.10
  140.5 1.9 %collective-permute-start.11 = (f32[128,1024]{1,0:T(8,128)S(1)}, f32[128,1024]{1,0:T(8,128)S(1)}, u32[]{:S(2)}, u32[]{:S(2)}) collective-permute-start(f32[128,1024]{1,0:T(8,128)S(1)} %maximum_multiply_fusion.refs_0_), channel_id=1, source_target_pairs={{0,6},{1,7},{2,0},{3,1},{4,2},{5,3},{6,4},{7,5},{8,14},{9,15},{10,... | collective-permute-start | bytes 1572872 | tf_op jit(solution)/shard_map/ppermute | solution.py:641
  142.4 3.3 %synthesis.4.refs_0_ = f32[16,64,900]{2,1,0:T(8,128)} custom-call(s32[16]{0:T(128)S(1)} %pad_add_fusion.order_ref, bf16[1024,900]{1,0:T(8,128)(2,1)S(1)} %copy-done.1, bf16[1024,900]{1,0:T(8,128)(2,1)S(1)} %copy-done.2, f32[8,512]{1,0:T(8,128)S(1)} %dynamic-slice_bitcast_fusion.turn_ref, f32[128,1024]{1,0:T(8,128)S(1)} %maximum_multiply_fusion.refs_0_, ...), custom_call_target="tpu_custom_call" | custom-call | flops 1610612736 | bytes 8388608 | tf_op jit(solution)/shard_map/synthesis/pallas_call | solution.py:563
  145.7 8.7 %collective-permute-done.10.refs_1_ = f32[128,1024]{1,0:T(8,128)S(1)} collective-permute-done((f32[128,1024]{1,0:T(8,128)S(1)}, f32[128,1024]{1,0:T(8,128)S(1)}, u32[]{:S(2)}, u32[]{:S(2)}) %collective-permute-start.10) | collective-permute-done | bytes 524320 | tf_op jit(solution)/shard_map/ppermute | solution.py:640
  154.4 0.8 collective-permute-start.15
  155.2 0.0 collective-permute-start.16
  155.3 1.1 collective-permute-start.13
  156.4 1.7 %collective-permute-start.14 = (f32[64,1024]{1,0:T(8,128)S(1)}, f32[64,1024]{1,0:T(8,128)S(1)}, u32[]{:S(2)}, u32[]{:S(2)}) collective-permute-start(f32[64,1024]{1,0:T(8,128)S(1)} %slice.39), channel_id=1, source_target_pairs={{0,6},{1,7},{2,0},{3,1},{4,2},{5,3},{6,4},{7,5},{8,14},{9,15},{10,... | collective-permute-start | bytes 786440 | tf_op jit(solution)/shard_map/ppermute | solution.py:645
  158.1 0.0 collective-permute-done.15.refs_2_
  158.1 3.3 %synthesis.5.refs_0_ = f32[16,64,900]{2,1,0:T(8,128)} custom-call(s32[16]{0:T(128)S(1)} %pad_add_fusion.order_ref, bf16[1024,900]{1,0:T(8,128)(2,1)S(1)} %copy-done.1, bf16[1024,900]{1,0:T(8,128)(2,1)S(1)} %copy-done.2, f32[8,512]{1,0:T(8,128)S(1)} %dynamic-slice_bitcast_fusion.turn_ref, ...), custom_call_target="tpu_custom_call", output_to_operand_aliasing={{}: (4, {})} | custom-call | flops 1610612736 | bytes 8388608 | tf_op jit(solution)/shard_map/synthesis/pallas_call | solution.py:563
  161.5 3.3 %synthesis.6.refs_0_ = f32[16,64,900]{2,1,0:T(8,128)} custom-call(s32[16]{0:T(128)S(1)} %pad_add_fusion.order_ref, bf16[1024,900]{1,0:T(8,128)(2,1)S(1)} %copy-done.1, bf16[1024,900]{1,0:T(8,128)(2,1)S(1)} %copy-done.2, f32[8,512]{1,0:T(8,128)S(1)} %dynamic-slice_bitcast_fusion.turn_ref, ...), custom_call_target="tpu_custom_call", output_to_operand_aliasing={{}: (4, {})} | custom-call | flops 1610612736 | bytes 8388608 | tf_op jit(solution)/shard_map/synthesis/pallas_call | solution.py:563
  164.8 1.1 collective-permute-start.17
  165.9 0.1 collective-permute-start.18
  166.0 1.1 collective-permute-done.17.refs_3_
  167.1 0.4 collective-permute-done.18.refs_4_
  167.4 3.3 %synthesis.7 = f32[16,64,900]{2,1,0:T(8,128)} custom-call(s32[16]{0:T(128)S(1)} %pad_add_fusion.order_ref, bf16[1024,900]{1,0:T(8,128)(2,1)S(1)} %copy-done.1, bf16[1024,900]{1,0:T(8,128)(2,1)S(1)} %copy-done.2, f32[8,512]{1,0:T(8,128)S(1)} %dynamic-slice_bitcast_fusion.turn_ref, f32[16,64,900]{2,1,0:T(8,128)} %synthesis.6.refs_0_, ...), custom_call_target="tpu_custom_call", output_to_operand_aliasing={{}: (4, {})} | custom-call | flops 1610612736 | bytes 8388608 | tf_op jit(solution)/shard_map/synthesis/pallas_call | solution.py:563
  (54 shorter events, 0.3 us)
Async XLA Ops:
  0.6 35.3 %copy-start.20 = (s32[8]{0:T(128)S(1)}, s32[8]{0:T(128)}, u32[]{:S(2)}) copy-start(s32[8]{0:T(128)} %constant.83.clone) | copy-start | bytes 100
  0.6 35.3 %copy-start.21 = (s32[8]{0:T(128)S(1)}, s32[8]{0:T(128)}, u32[]{:S(2)}) copy-start(s32[8]{0:T(128)} %constant.82.clone) | copy-start | bytes 100
  0.7 14.4 %copy-start.17 = (f32[16,128]{1,0:T(8,128)S(1)}, f32[16,128]{1,0:T(8,128)}, u32[]{:S(2)}) copy-start(f32[16,128]{1,0:T(8,128)} %param.22) | copy-start | bytes 24580
  0.7 14.5 %copy-start.18 = (f32[128]{0:T(128)S(1)}, f32[128]{0:T(128)}, u32[]{:S(2)}) copy-start(f32[128]{0:T(128)} %param.23) | copy-start | bytes 1540
  0.7 15.4 %copy-start.15 = (s32[2048,1]{0,1:T(1,128)S(1)}, s32[2048,1]{0,1:T(1,128)}, u32[]{:S(2)}) copy-start(s32[2048,1]{0,1:T(1,128)} %param.26) | copy-start | bytes 24580
  0.7 15.4 %copy-start.13 = (s32[2048,4]{0,1:T(4,128)S(1)}, s32[2048,4]{0,1:T(4,128)}, u32[]{:S(2)}) copy-start(s32[2048,4]{0,1:T(4,128)} %param.27) | copy-start | bytes 98308
  0.7 15.4 %copy-start.14 = (f32[2048,4]{0,1:T(4,128)S(1)}, f32[2048,4]{0,1:T(4,128)}, u32[]{:S(2)}) copy-start(f32[2048,4]{0,1:T(4,128)} %param.28) | copy-start | bytes 98308
  0.7 15.4 %copy-start.11 = (f32[2048,128]{1,0:T(8,128)S(1)}, f32[2048,128]{1,0:T(8,128)}, u32[]{:S(2)}) copy-start(f32[2048,128]{1,0:T(8,128)} %values_ref.1) | copy-start | bytes 3145732
  7.5 28.5 %collective-permute-start = (f32[16,8,900]{2,1,0:T(8,128)}, f32[16,8,900]{2,1,0:T(8,128)S(1)}, u32[]{:S(2)}, u32[]{:S(2)}) collective-permute-start(f32[16,8,900]{2,1,0:T(8,128)} %get-tuple-element.29), channel_id=1, source_target_pairs={{0,8},{8,16},{16,24},{24,32},{32,40},{40,48},{48,56},{56,64},{64,7... | collective-permute-start | bytes 1382408 | tf_op jit(solution)/shard_map/ppermute | solution.py:161
  11.0 25.0 %collective-permute-start.1 = (f32[16,8,900]{2,1,0:T(8,128)}, f32[16,8,900]{2,1,0:T(8,128)S(1)}, u32[]{:S(2)}, u32[]{:S(2)}) collective-permute-start(f32[16,8,900]{2,1,0:T(8,128)} %get-tuple-element.30), channel_id=1, source_target_pairs={{8,0},{16,8},{24,16},{32,24},{40,32},{48,40},{56,48},{64,56},{72,6... | collective-permute-start | bytes 1382408 | tf_op jit(solution)/shard_map/ppermute | solution.py:160
  25.6 22.0 %copy-start.6 = (f32[16,64,128]{2,1,0:T(8,128)S(1)}, f32[16,64,128]{2,1,0:T(8,128)}, u32[]{:S(2)}) copy-start(f32[16,64,128]{2,1,0:T(8,128)} %get-tuple-element.34.matrix_ref) | copy-start | bytes 1572868
  25.6 22.0 %copy-start.12 = (bf16[256,512]{1,0:T(8,128)(2,1)S(1)}, bf16[256,512]{1,0:T(8,128)(2,1)}, u32[]{:S(2)}) copy-start(bf16[256,512]{1,0:T(8,128)(2,1)} %constant.76.clone.pick_ref) | copy-start | bytes 786436
  25.6 21.9 %all-to-all-start = ((f32[128,1,1152]{2,1,0:T(1,128)}), f32[128,1,1152]{2,1,0:T(1,128)S(1)}, u32[]{:S(2)}, u32[]{:S(2)}) async-start(f32[128,1,1152]{2,1,0:T(1,128)} %route.1), calls=%async_computation | async-start | bytes 1179648 | tf_op jit(solution)/shard_map/all_to_all | solution.py:599
  36.0 0.8 copy-start.7
  36.0 1.0 copy-start.9
  47.4 49.6 %copy-start.8 = (f32[16,8,900]{2,1,0:T(8,128)S(1)}, f32[16,8,900]{2,1,0:T(8,128)}, u32[]{:S(2)}) copy-start(f32[16,8,900]{2,1,0:T(8,128)} %copy-done.7) | copy-start | bytes 1382404
  47.4 49.6 %copy-start.10 = (f32[16,8,900]{2,1,0:T(8,128)S(1)}, f32[16,8,900]{2,1,0:T(8,128)}, u32[]{:S(2)}) copy-start(f32[16,8,900]{2,1,0:T(8,128)} %copy-done.9) | copy-start | bytes 1382404
  47.4 49.6 %copy-start.16 = (f32[16]{0:T(128)S(1)}, f32[16]{0:T(128)}, u32[]{:S(2)}) copy-start(f32[16]{0:T(128)} %coupling_ref.3) | copy-start | bytes 196
  47.5 49.6 %copy-start = (f32[16,64,900]{2,1,0:T(8,128)S(1)}, f32[16,64,900]{2,1,0:T(8,128)}, u32[]{:S(2)}) copy-start(f32[16,64,900]{2,1,0:T(8,128)} %control_ref.1) | copy-start | bytes 11059204
  89.6 12.4 %collective-permute-start.2 = (f32[16,2,900]{2,1,0:T(2,128)S(1)}, f32[16,2,900]{2,1,0:T(2,128)S(1)}, u32[]{:S(2)}, u32[]{:S(2)}) collective-permute-start(f32[16,2,900]{2,1,0:T(2,128)S(1)} %get-tuple-element.36), channel_id=1, source_target_pairs={{0,8},{8,16},{16,24},{24,32},{32,40},{40,48},{48,56},{56,64},{64,7... | collective-permute-start | bytes 345608 | tf_op jit(solution)/shard_map/ppermute | solution.py:161
  91.5 10.5 %collective-permute-start.3 = (f32[16,2,900]{2,1,0:T(2,128)S(1)}, f32[16,2,900]{2,1,0:T(2,128)S(1)}, u32[]{:S(2)}, u32[]{:S(2)}) collective-permute-start(f32[16,2,900]{2,1,0:T(2,128)S(1)} %get-tuple-element.37), channel_id=1, source_target_pairs={{8,0},{16,8},{24,16},{32,24},{40,32},{48,40},{56,48},{64,56},{72,6... | collective-permute-start | bytes 345608 | tf_op jit(solution)/shard_map/ppermute | solution.py:160
  97.1 4.9 %copy-start.3 = (bf16[900,1024]{1,0:T(8,128)(2,1)S(1)}, bf16[900,1024]{1,0:T(8,128)(2,1)}, u32[]{:S(2)}) copy-start(bf16[900,1024]{1,0:T(8,128)(2,1)} %constant.77.clone.head_ref) | copy-start | bytes 5529604
  97.1 4.9 %copy-start.4 = (bf16[900,1024]{1,0:T(8,128)(2,1)S(1)}, bf16[900,1024]{1,0:T(8,128)(2,1)}, u32[]{:S(2)}) copy-start(bf16[900,1024]{1,0:T(8,128)(2,1)} %constant.78.clone.tail_ref) | copy-start | bytes 5529604
  97.1 4.9 %copy-start.5 = (f32[16,64,128]{2,1,0:T(8,128)S(1)}, f32[16,64,128]{2,1,0:T(8,128)}, u32[]{:S(2)}) copy-start(f32[16,64,128]{2,1,0:T(8,128)} %get-tuple-element.38.mend_ref) | copy-start | bytes 1572868
  106.0 4.6 %collective-permute-start.4 = (f32[4,64,1024]{2,1,0:T(8,128)S(1)}, f32[4,64,1024]{2,1,0:T(8,128)S(1)}, u32[]{:S(2)}, u32[]{:S(2)}) collective-permute-start(f32[4,64,1024]{2,1,0:T(8,128)S(1)} %get-tuple-element.41), channel_id=1, source_target_pairs={{0,1},{1,0},{2,3},{3,2},{4,5},{5,4},{6,7},{7,6},{8,9},{9,8},{10,11... | collective-permute-start | bytes 3145736 | tf_op jit(solution)/shard_map/ppermute | solution.py:622
  110.2 7.6 %collective-permute-start.5 = (f32[4,64,1024]{2,1,0:T(8,128)S(1)}, f32[4,64,1024]{2,1,0:T(8,128)S(1)}, u32[]{:S(2)}, u32[]{:S(2)}) collective-permute-start(f32[4,64,1024]{2,1,0:T(8,128)S(1)} %get-tuple-element.43), channel_id=1, source_target_pairs={{0,1},{1,0},{2,3},{3,2},{4,5},{5,4},{6,7},{7,6},{8,9},{9,8},{10,11... | collective-permute-start | bytes 3145736 | tf_op jit(solution)/shard_map/ppermute | solution.py:622
  114.6 14.7 %collective-permute-start.6 = (f32[2,64,1024]{2,1,0:T(8,128)S(1)}, f32[2,64,1024]{2,1,0:T(8,128)S(1)}, u32[]{:S(2)}, u32[]{:S(2)}) collective-permute-start(f32[2,64,1024]{2,1,0:T(8,128)S(1)} %get-tuple-element.47), channel_id=1, source_target_pairs={{0,2},{1,3},{2,4},{3,5},{4,6},{5,7},{6,0},{7,1},{8,10},{9,11},{10,... | collective-permute-start | bytes 1572872 | tf_op jit(solution)/shard_map/ppermute | solution.py:629
  116.2 13.1 %collective-permute-start.8 = (f32[2,64,1024]{2,1,0:T(8,128)S(1)}, f32[2,64,1024]{2,1,0:T(8,128)S(1)}, u32[]{:S(2)}, u32[]{:S(2)}) collective-permute-start(f32[2,64,1024]{2,1,0:T(8,128)S(1)} %get-tuple-element.48), channel_id=1, source_target_pairs={{0,6},{1,7},{2,0},{3,1},{4,2},{5,3},{6,4},{7,5},{8,14},{9,15},{10,... | collective-permute-start | bytes 1572872 | tf_op jit(solution)/shard_map/ppermute | solution.py:630
  117.7 14.4 %copy-start.19 = (f32[512]{0:T(512)S(1)}, f32[512]{0:T(512)}, u32[]{:S(2)}) copy-start(f32[512]{0:T(512)} %param.24) | copy-start | bytes 6148
  121.8 20.6 %copy-start.1 = (bf16[1024,900]{1,0:T(8,128)(2,1)S(1)}, bf16[1024,900]{1,0:T(8,128)(2,1)}, u32[]{:S(2)}) copy-start(bf16[1024,900]{1,0:T(8,128)(2,1)} %constant.79.clone.head_ref) | copy-start | bytes 5529604
  121.8 20.6 %copy-start.2 = (bf16[1024,900]{1,0:T(8,128)(2,1)S(1)}, bf16[1024,900]{1,0:T(8,128)(2,1)}, u32[]{:S(2)}) copy-start(bf16[1024,900]{1,0:T(8,128)(2,1)} %constant.80.clone.tail_ref) | copy-start | bytes 5529604
  129.4 7.9 %collective-permute-start.7 = (f32[64,1024]{1,0:T(8,128)S(1)}, f32[64,1024]{1,0:T(8,128)S(1)}, u32[]{:S(2)}, u32[]{:S(2)}) collective-permute-start(f32[64,1024]{1,0:T(8,128)S(1)} %get-tuple-element.59), channel_id=1, source_target_pairs={{0,2},{1,3},{2,4},{3,5},{4,6},{5,7},{6,0},{7,1},{8,10},{9,11},{10,... | collective-permute-start | bytes 786440 | tf_op jit(solution)/shard_map/ppermute | solution.py:632
  130.3 6.9 %collective-permute-start.9 = (f32[64,1024]{1,0:T(8,128)S(1)}, f32[64,1024]{1,0:T(8,128)S(1)}, u32[]{:S(2)}, u32[]{:S(2)}) collective-permute-start(f32[64,1024]{1,0:T(8,128)S(1)} %get-tuple-element.60), channel_id=1, source_target_pairs={{0,6},{1,7},{2,0},{3,1},{4,2},{5,3},{6,4},{7,5},{8,14},{9,15},{10,... | collective-permute-start | bytes 786440 | tf_op jit(solution)/shard_map/ppermute | solution.py:633
  137.4 5.0 %collective-permute-start.12 = (f32[128,1024]{1,0:T(8,128)S(1)}, f32[128,1024]{1,0:T(8,128)S(1)}, u32[]{:S(2)}, u32[]{:S(2)}) collective-permute-start(f32[128,1024]{1,0:T(8,128)S(1)} %maximum_multiply_fusion.refs_0_), channel_id=1, source_target_pairs={{0,1},{1,0},{2,3},{3,2},{4,5},{5,4},{6,7},{7,6},{8,9},{9,8},{10,11... | collective-permute-start | bytes 1572872 | tf_op jit(solution)/shard_map/ppermute | solution.py:622
  139.6 14.8 %collective-permute-start.10 = (f32[128,1024]{1,0:T(8,128)S(1)}, f32[128,1024]{1,0:T(8,128)S(1)}, u32[]{:S(2)}, u32[]{:S(2)}) collective-permute-start(f32[128,1024]{1,0:T(8,128)S(1)} %maximum_multiply_fusion.refs_0_), channel_id=1, source_target_pairs={{0,2},{1,3},{2,4},{3,5},{4,6},{5,7},{6,0},{7,1},{8,10},{9,11},{10,... | collective-permute-start | bytes 1572872 | tf_op jit(solution)/shard_map/ppermute | solution.py:640
  140.5 14.0 %collective-permute-start.11 = (f32[128,1024]{1,0:T(8,128)S(1)}, f32[128,1024]{1,0:T(8,128)S(1)}, u32[]{:S(2)}, u32[]{:S(2)}) collective-permute-start(f32[128,1024]{1,0:T(8,128)S(1)} %maximum_multiply_fusion.refs_0_), channel_id=1, source_target_pairs={{0,6},{1,7},{2,0},{3,1},{4,2},{5,3},{6,4},{7,5},{8,14},{9,15},{10,... | collective-permute-start | bytes 1572872 | tf_op jit(solution)/shard_map/ppermute | solution.py:641
  154.4 3.7 %collective-permute-start.15 = (f32[128,1024]{1,0:T(8,128)S(1)}, f32[128,1024]{1,0:T(8,128)S(1)}, u32[]{:S(2)}, u32[]{:S(2)}) collective-permute-start(f32[128,1024]{1,0:T(8,128)S(1)} %collective-permute-done.10.refs_1_), channel_id=1, source_target_pairs={{0,1},{1,0},{2,3},{3,2},{4,5},{5,4},{6,7},{7,6},{8,9},{9,8},{10,11... | collective-permute-start | bytes 1572872 | tf_op jit(solution)/shard_map/ppermute | solution.py:622
  155.2 6.2 %collective-permute-start.16 = (f32[128,1024]{1,0:T(8,128)S(1)}, f32[128,1024]{1,0:T(8,128)S(1)}, u32[]{:S(2)}, u32[]{:S(2)}) collective-permute-start(f32[128,1024]{1,0:T(8,128)S(1)} %collective-permute-done.11.refs_1_), channel_id=1, source_target_pairs={{0,1},{1,0},{2,3},{3,2},{4,5},{5,4},{6,7},{7,6},{8,9},{9,8},{10,11... | collective-permute-start | bytes 1572872 | tf_op jit(solution)/shard_map/ppermute | solution.py:622
  155.3 9.5 %collective-permute-start.13 = (f32[64,1024]{1,0:T(8,128)S(1)}, f32[64,1024]{1,0:T(8,128)S(1)}, u32[]{:S(2)}, u32[]{:S(2)}) collective-permute-start(f32[64,1024]{1,0:T(8,128)S(1)} %slice.38), channel_id=1, source_target_pairs={{0,2},{1,3},{2,4},{3,5},{4,6},{5,7},{6,0},{7,1},{8,10},{9,11},{10,... | collective-permute-start | bytes 786440 | tf_op jit(solution)/shard_map/ppermute | solution.py:644
  156.4 8.4 %collective-permute-start.14 = (f32[64,1024]{1,0:T(8,128)S(1)}, f32[64,1024]{1,0:T(8,128)S(1)}, u32[]{:S(2)}, u32[]{:S(2)}) collective-permute-start(f32[64,1024]{1,0:T(8,128)S(1)} %slice.39), channel_id=1, source_target_pairs={{0,6},{1,7},{2,0},{3,1},{4,2},{5,3},{6,4},{7,5},{8,14},{9,15},{10,... | collective-permute-start | bytes 786440 | tf_op jit(solution)/shard_map/ppermute | solution.py:645
  164.8 2.2 %collective-permute-start.17 = (f32[64,1024]{1,0:T(8,128)S(1)}, f32[64,1024]{1,0:T(8,128)S(1)}, u32[]{:S(2)}, u32[]{:S(2)}) collective-permute-start(f32[64,1024]{1,0:T(8,128)S(1)} %collective-permute-done.13.refs_1_), channel_id=1, source_target_pairs={{0,1},{1,0},{2,3},{3,2},{4,5},{5,4},{6,7},{7,6},{8,9},{9,8},{10,11... | collective-permute-start | bytes 786440 | tf_op jit(solution)/shard_map/ppermute | solution.py:622
  165.9 1.5 collective-permute-start.18
